TPU v7x, 256 devices: a whole 4x4x8 slice. The times are simulated.
256 devices in a mesh: tile: 2 (over core), ta: 16 (over y, x), gx: 8 (over z).
Axes of the slice: x: 4, y: 4, z: 8, core: 2. Of those that a mesh axis runs over, the one named last changes fastest.
Arguments:
- field: float32 [8192, 4096], P(('tile', 'ta'), 'gx'), parts along dimension 0, may hold values from -7.5 to 7.5
- time_period: float32 [2], P('tile'), parts along dimension 0, may hold values from 8192 to 16384
- space_period: float32 [2], P('tile'), parts along dimension 0, may hold values from 10240 to 16384
Outputs:
- updated_field: float32 [8192, 4096], P(('tile', 'ta'), 'gx'), parts along dimension 0
- residual: float32 [8192, 4096], P(('tile', 'ta'), 'gx'), parts along dimension 0
There are 2 independent parts, one for each index of `tile`. A program takes and returns all parts, laid end to end along the dimension named above; each array names one. Nothing has to cross between parts.
All inputs are finite; a program needn't handle non-finite values.
Results may differ from a plain program's by a relative error of at most 0.000092.
Values sent between devices are 32-bit elements; how exact they have to be, the bound alone decides.
No kernel may reach another device: no remote copies, remote signals or barrier semaphores. Data moves between devices by JAX's collectives and lax.ppermute only.
A program may use at most 64 MiB of HBM per device.

v0:
```python
import math

import jax
import jax.numpy as jnp
from jax import lax
from jax.sharding import PartitionSpec as P

TWO_PI = 2.0 * math.pi
GRAD_EPS = 1e-06


def contract(form, left_op, right_op):
    return jnp.einsum(form, left_op, right_op, precision=lax.Precision.HIGHEST)


def factor_pair(length):
    low_factor = 1
    for candidate in range(1, math.isqrt(length) + 1):
        if length % candidate == 0:
            low_factor = candidate
    return (low_factor, length // low_factor)


def phase_table(first_count, second_count, modulus, direction):
    first_index = jnp.arange(first_count, dtype=jnp.int32)[:, None]
    second_index = jnp.arange(second_count, dtype=jnp.int32)[None, :]
    angle = (
        direction * TWO_PI / modulus * (first_index * second_index % modulus).astype(jnp.float32)
    )
    return (jnp.cos(angle), jnp.sin(angle))


def all_tables(length, direction):
    low_factor, high_factor = factor_pair(length)
    cos_low, sin_low = phase_table(low_factor, low_factor, low_factor, direction)
    cos_high, sin_high = phase_table(high_factor, high_factor, high_factor, direction)
    cos_mid, sin_mid = phase_table(low_factor, high_factor, length, direction)
    return (low_factor, high_factor, cos_low, sin_low, cos_high, sin_high, cos_mid, sin_mid)


def complex_apply(form, real_part, imag_part, cos_table, sin_table):
    out_real = contract(form, real_part, cos_table) - contract(form, imag_part, sin_table)
    out_imag = contract(form, real_part, sin_table) + contract(form, imag_part, cos_table)
    return (out_real, out_imag)


def rotate(real_part, imag_part, cos_table, sin_table):
    return (
        real_part * cos_table - imag_part * sin_table,
        real_part * sin_table + imag_part * cos_table,
    )


def forward_rows(values):
    row_count, length = values.shape
    low_factor, high_factor, cos_low, sin_low, cos_high, sin_high, cos_mid, sin_mid = all_tables(
        length, -1.0
    )
    shaped = values.reshape(row_count, low_factor, high_factor)
    part_real = contract("mnq,nk->mkq", shaped, cos_low)
    part_imag = contract("mnq,nk->mkq", shaped, sin_low)
    part_real, part_imag = rotate(part_real, part_imag, cos_mid, sin_mid)
    part_real, part_imag = complex_apply("mkq,ql->mkl", part_real, part_imag, cos_high, sin_high)
    return (part_real.reshape(row_count, length), part_imag.reshape(row_count, length))


def inverse_rows(real_part, imag_part):
    row_count, length = real_part.shape
    low_factor, high_factor, cos_low, sin_low, cos_high, sin_high, cos_mid, sin_mid = all_tables(
        length, 1.0
    )
    part_real = real_part.reshape(row_count, low_factor, high_factor)
    part_imag = imag_part.reshape(row_count, low_factor, high_factor)
    part_real, part_imag = complex_apply("mkl,lq->mkq", part_real, part_imag, cos_high, sin_high)
    part_real, part_imag = rotate(part_real, part_imag, cos_mid, sin_mid)
    part_real, part_imag = complex_apply("mkq,kn->mnq", part_real, part_imag, cos_low, sin_low)
    return (part_real.reshape(row_count, length), part_imag.reshape(row_count, length))


def stacked_apply(form, stacked, cos_table, sin_table, half_width):
    with_cos = contract(form, stacked, cos_table)
    with_sin = contract(form, stacked, sin_table)
    out_real = with_cos[..., :half_width] - with_sin[..., half_width:]
    out_imag = with_sin[..., :half_width] + with_cos[..., half_width:]
    return (out_real, out_imag)


def forward_cols(stacked):
    length, col_width = stacked.shape
    half_width = col_width // 2
    low_factor, high_factor, cos_low, sin_low, cos_high, sin_high, cos_mid, sin_mid = all_tables(
        length, -1.0
    )
    shaped = stacked.reshape(low_factor, high_factor, col_width)
    part_real, part_imag = stacked_apply("nqc,nk->kqc", shaped, cos_low, sin_low, half_width)
    part_real, part_imag = rotate(part_real, part_imag, cos_mid[:, :, None], sin_mid[:, :, None])
    joined = jnp.concatenate([part_real, part_imag], axis=2)
    part_real, part_imag = stacked_apply("kqc,ql->klc", joined, cos_high, sin_high, half_width)
    return jnp.concatenate([part_real, part_imag], axis=2).reshape(length, col_width)


def inverse_cols(stacked):
    length, col_width = stacked.shape
    half_width = col_width // 2
    low_factor, high_factor, cos_low, sin_low, cos_high, sin_high, cos_mid, sin_mid = all_tables(
        length, 1.0
    )
    shaped = stacked.reshape(low_factor, high_factor, col_width)
    part_real, part_imag = stacked_apply("klc,lq->kqc", shaped, cos_high, sin_high, half_width)
    part_real, part_imag = rotate(part_real, part_imag, cos_mid[:, :, None], sin_mid[:, :, None])
    joined = jnp.concatenate([part_real, part_imag], axis=2)
    part_real, part_imag = stacked_apply("kqc,kn->nqc", joined, cos_low, sin_low, half_width)
    return jnp.concatenate([part_real, part_imag], axis=2).reshape(length, col_width)


def pack_blocks(real_part, imag_part, blocks):
    row_count, length = real_part.shape
    col_count = length // blocks
    paired = jnp.stack(
        [
            real_part.reshape(row_count, blocks, col_count),
            imag_part.reshape(row_count, blocks, col_count),
        ],
        axis=2,
    )
    return paired.reshape(row_count, 2 * length)


def unpack_blocks(stacked, blocks):
    row_count, total_width = stacked.shape
    length = total_width // 2
    shaped = stacked.reshape(row_count, blocks, 2, length // blocks)
    return (
        shaped[:, :, 0, :].reshape(row_count, length),
        shaped[:, :, 1, :].reshape(row_count, length),
    )


def mode_numbers(position, count):
    low_factor, high_factor = factor_pair(count)
    modes = position // high_factor + low_factor * (position % high_factor)
    signed = jnp.where(modes < count // 2, modes, modes - count)
    odd = jnp.where(modes == count // 2, 0, signed)
    return (signed.astype(jnp.float32), odd.astype(jnp.float32))


def local(field, time_period, space_period):
    time_blocks = lax.axis_size("ta")
    space_blocks = lax.axis_size("gx")
    blocks = time_blocks * space_blocks
    rows_field = lax.all_to_all(field, "gx", split_axis=0, concat_axis=1, tiled=True)
    row_count, space_len = rows_field.shape
    time_len = row_count * blocks
    col_count = space_len // blocks
    owned = lax.axis_index("ta") * space_blocks + lax.axis_index("gx")

    def to_spectral(stacked):
        return lax.all_to_all(stacked, ("ta", "gx"), split_axis=1, concat_axis=0, tiled=True)

    def to_physical(stacked):
        return lax.all_to_all(stacked, ("ta", "gx"), split_axis=0, concat_axis=1, tiled=True)

    inv_count = 1.0 / (time_len * space_len)
    time_signed, time_odd = mode_numbers(jnp.arange(time_len, dtype=jnp.int32), time_len)
    omega_col = (inv_count * TWO_PI * time_odd / time_period[0])[:, None]
    columns = owned * col_count + jnp.arange(col_count, dtype=jnp.int32)
    space_signed, space_odd = mode_numbers(columns, space_len)
    wave = TWO_PI * space_signed / space_period[0]
    wave_odd = TWO_PI * space_odd / space_period[0]
    real_row = (inv_count * (wave**4 - wave**2 - wave_odd))[None, :]

    def spectral_pass(values, time_sign):
        spec_real, spec_imag = forward_rows(values)
        stacked = forward_cols(to_spectral(pack_blocks(spec_real, spec_imag, blocks)))
        z_real = stacked[:, :col_count]
        z_imag = stacked[:, col_count:]
        imag_symbol = time_sign * omega_col
        mixed = jnp.concatenate(
            [real_row * z_real - imag_symbol * z_imag, real_row * z_imag + imag_symbol * z_real],
            axis=1,
        )
        back_real, back_imag = unpack_blocks(to_physical(inverse_cols(mixed)), blocks)
        return inverse_rows(back_real, back_imag)

    linear, slope = spectral_pass(rows_field, 1.0)
    residual = linear + rows_field * slope
    cost_local = 0.5 * jnp.sum(residual * residual)
    cost_total = lax.psum(cost_local, ("ta", "gx"))
    adjoint, residual_slope = spectral_pass(residual, -1.0)
    gradient = adjoint - rows_field * residual_slope
    grad_local = jnp.sum(gradient * gradient)
    grad_total = lax.psum(grad_local, ("ta", "gx"))
    step_size = cost_total / (grad_total + GRAD_EPS)
    updated = rows_field - step_size * gradient
    return (
        lax.all_to_all(updated, "gx", split_axis=1, concat_axis=0, tiled=True),
        lax.all_to_all(residual, "gx", split_axis=1, concat_axis=0, tiled=True),
    )


def solution(mesh):
    placed = (P(("tile", "ta"), "gx"), P("tile"), P("tile"))
    return jax.shard_map(
        local,
        mesh=mesh,
        in_specs=placed,
        out_specs=(P(("tile", "ta"), "gx"), P(("tile", "ta"), "gx")),
        check_vma=False,
    )
```

profile of v0, /device:TPU:32, one launch (start us, length us, event | category | flops | bytes accessed | tf_op | source)
XLA Modules:
  0.0 788.6 jit_solution(16757349861266021426)
XLA Ops:
  0.6 8.6 %all-to-all-start = ((f32[8,32,512]{2,1,0:T(8,128)}), f32[8,32,512]{2,1,0:T(8,128)S(1)}, u32[]{:S(2)}, u32[]{:S(2)}) async-start(f32[8,32,512]{2,1,0:T(8,128)} %bitcast.299), calls=%async_computation | async-start | bytes 1048576 | tf_op jit(solution)/shard_map/all_to_all | solution.py:151
  9.5 15.7 %all-to-all-done = f32[8,32,512]{2,1,0:T(8,128)S(1)} async-done(((f32[8,32,512]{2,1,0:T(8,128)}), f32[8,32,512]{2,1,0:T(8,128)S(1)}, u32[]{:S(2)}, u32[]{:S(2)}) %all-to-all-start) | async-done | bytes 524320 | tf_op jit(solution)/shard_map/all_to_all | solution.py:151
  34.3 2.7 stack_reshape_reshape.13
  37.0 3.0 copy.133
  40.0 3.3 convolution_subtract_fusion.5
  46.3 2.3 pad_maximum_fusion.8
  48.5 3.1 copy.134
  51.6 2.3 reshape.346
  53.9 10.2 %all-to-all-start.1 = ((f32[128,1,2048]{2,1,0:T(1,128)}), f32[128,1,2048]{2,1,0:T(1,128)S(1)}, u32[]{:S(2)}, u32[]{:S(2)}) async-start(f32[128,1,2048]{2,1,0:T(1,128)} %reshape.346), calls=%async_computation.1 | async-start | bytes 2097152 | tf_op jit(solution)/shard_map/all_to_all | solution.py:158
  65.9 29.7 %all-to-all-done.1 = f32[128,1,2048]{2,1,0:T(1,128)S(1)} async-done(((f32[128,1,2048]{2,1,0:T(1,128)}), f32[128,1,2048]{2,1,0:T(1,128)S(1)}, u32[]{:S(2)}, u32[]{:S(2)}) %all-to-all-start.1) | async-done | bytes 1048608 | tf_op jit(solution)/shard_map/all_to_all | solution.py:158
  96.2 3.1 reduce.2
  101.5 2.4 copy.136
  110.1 3.5 copy.140
  133.3 3.3 copy.151
  141.3 3.2 copy.154
  144.5 2.7 reshape.348
  147.2 36.1 %all_to_all.112 = f32[128,1,2048]{2,1,0:T(1,128)S(1)} all-to-all(f32[128,1,2048]{2,1,0:T(1,128)S(1)} %reshape.348), channel_id=1, replica_groups=mesh['tile'=2,'ta'=16,'gx'=8] {'ta','gx'}, dimensions={0} | all-to-all | bytes 2097152 | tf_op jit(solution)/shard_map/all_to_all | solution.py:161
  183.3 4.3 reduce.3
  200.9 3.0 copy.158
  205.9 2.3 convolution_add_fusion.4
  212.9 3.0 multiply_reduce_fusion.1
  221.5 2.3 convolution_add_fusion.2
  223.8 2.7 stack_reshape_reshape.15
  226.5 3.0 copy.169
  229.5 3.3 convolution_subtract_fusion.2
  235.7 2.3 pad_maximum_fusion.10
  238.0 3.1 copy.170
  241.1 2.3 reshape.350
  243.4 35.7 %all_to_all.113 = f32[128,1,2048]{2,1,0:T(1,128)S(1)} all-to-all(f32[128,1,2048]{2,1,0:T(1,128)} %reshape.350), channel_id=1, replica_groups=mesh['tile'=2,'ta'=16,'gx'=8] {'ta','gx'}, dimensions={0} | all-to-all | bytes 2097152 | tf_op jit(solution)/shard_map/all_to_all | solution.py:158
  279.1 3.1 reduce.4
  284.4 2.4 copy.172
  292.9 3.5 copy.176
  316.1 3.3 copy.185
  324.1 3.1 copy.188
  327.3 3.5 reshape.352
  330.8 6.6 all-to-all-start.4
  338.5 2.3 reshape.292
  341.4 22.8 %all-to-all-done.4 = f32[128,1,2048]{2,1,0:T(1,128)S(1)} async-done(((f32[128,1,2048]{2,1,0:T(1,128)}), f32[128,1,2048]{2,1,0:T(1,128)S(1)}, u32[]{:S(2)}, u32[]{:S(2)}) %all-to-all-start.4) | async-done | bytes 1048608 | tf_op jit(solution)/shard_map/all_to_all | solution.py:161
  364.2 4.3 reduce.5
  386.9 2.4 convolution_add_fusion.1
  389.3 2.3 convolution_subtract_fusion.1
  397.1 2.3 reshape.291
  399.4 4.5 multiply_reduce_fusion
  405.4 344.5 %all-reduce = (f32[]{:T(128)}, f32[]{:T(128)}) all-reduce(f32[]{:T(128)S(6)} %mul_shard_map.3, f32[]{:T(128)} %get-tuple-element.33), channel_id=1, replica_groups=mesh['tile'=2,'ta'=16,'gx'=8] {'ta','gx'}, use_global_device_ids=true, to_apply=%region_1.2 | all-reduce | flops 2 | bytes 16 | tf_op jit(solution)/shard_map/psum | solution.py:188
  751.2 3.5 copy_add_fusion
  754.7 15.4 %all_to_all.114 = f32[32,8,512]{2,0,1:T(8,128)S(1)} all-to-all(f32[32,8,512]{2,0,1:T(8,128)S(1)} %get-tuple-element.30), channel_id=1, replica_groups=mesh['tile'=2,'ta'=16,'gx'=8] {'gx'}, dimensions={1} | all-to-all | bytes 1048576 | tf_op jit(solution)/shard_map/all_to_all | solution.py:197
  770.1 4.8 all-to-all-start.5
  775.0 11.9 %all-to-all-done.5 = f32[32,8,512]{2,0,1:T(8,128)S(1)} async-done(((f32[32,8,512]{2,0,1:T(8,128)}), f32[32,8,512]{2,0,1:T(8,128)S(1)}, u32[]{:S(2)}, u32[]{:S(2)}) %all-to-all-start.5) | async-done | bytes 524320 | tf_op jit(solution)/shard_map/all_to_all | solution.py:196
  (109 shorter events, 135.0 us)
Async XLA Ops:
  0.6 24.6 %all-to-all-start = ((f32[8,32,512]{2,1,0:T(8,128)}), f32[8,32,512]{2,1,0:T(8,128)S(1)}, u32[]{:S(2)}, u32[]{:S(2)}) async-start(f32[8,32,512]{2,1,0:T(8,128)} %bitcast.299), calls=%async_computation | async-start | bytes 1048576 | tf_op jit(solution)/shard_map/all_to_all | solution.py:151
  25.2 0.8 copy-start.3
  53.9 41.7 %all-to-all-start.1 = ((f32[128,1,2048]{2,1,0:T(1,128)}), f32[128,1,2048]{2,1,0:T(1,128)S(1)}, u32[]{:S(2)}, u32[]{:S(2)}) async-start(f32[128,1,2048]{2,1,0:T(1,128)} %reshape.346), calls=%async_computation.1 | async-start | bytes 2097152 | tf_op jit(solution)/shard_map/all_to_all | solution.py:158
  212.9 3.0 copy-start.1
  327.3 10.2 %copy-start.2 = (f32[32,64,64]{2,1,0:T(8,128)S(1)}, f32[32,64,64]{2,1,0:T(8,128)}, u32[]{:S(2)}) copy-start(f32[32,64,64]{2,1,0:T(8,128)} %copy-done.1) | copy-start | bytes 1572868
  330.8 33.4 %all-to-all-start.4 = ((f32[128,1,2048]{2,1,0:T(1,128)}), f32[128,1,2048]{2,1,0:T(1,128)S(1)}, u32[]{:S(2)}, u32[]{:S(2)}) async-start(f32[128,1,2048]{2,1,0:T(1,128)} %reshape.352), calls=%async_computation.4 | async-start | bytes 2097152 | tf_op jit(solution)/shard_map/all_to_all | solution.py:161
  385.9 1.0 copy-start
  386.9 2.4 copy-start.4
  770.1 16.7 %all-to-all-start.5 = ((f32[32,8,512]{2,0,1:T(8,128)}), f32[32,8,512]{2,0,1:T(8,128)S(1)}, u32[]{:S(2)}, u32[]{:S(2)}) async-start(f32[32,8,512]{2,0,1:T(8,128)} %get-tuple-element.31), calls=%async_computation.5 | async-start | bytes 1048576 | tf_op jit(solution)/shard_map/all_to_all | solution.py:196
where the time goes:
time: 799 us; the launch traced here: 789 us
  blocking collectives  432 us (54%)
  local copies, waits for them, and re-layouts  116 us (15%)
  matrix products  86.7 us (11%)
  waiting for transfers between devices  80.1 us (10%)
  other arithmetic  39.4 us (5%)
  starting transfers between devices  30.3 us (4%)
    psum x1, blocking collectives, local(): cost_total = lax.psum(cost_local, ('ta', 'gx'))  345 us
    dot_general x28, matrix products, contract(): return jnp.einsum(form, left_op, right_op, precision=lax.Precision.HIGHEST)  54.3 us
    all_to_all x1, blocking collectives, to_physical(): lax.all_to_all(stacked, ('ta', 'gx'), split_axis=0, concat_axis=1, tiled=...  36.1 us
    all_to_all x1, blocking collectives, to_spectral(): lax.all_to_all(stacked, ('ta', 'gx'), split_axis=1, concat_axis=0, tiled=...  35.7 us
    unnamed x16, matrix products  32.4 us
    all_to_all x1, waiting for transfers between devices, to_spectral(): lax.all_to_all(stacked, ('ta', 'gx'), split_axis=1, concat_axis=0, tiled=...  29.7 us
    all_to_all x1, waiting for transfers between devices, to_physical(): lax.all_to_all(stacked, ('ta', 'gx'), split_axis=0, concat_axis=1, tiled=...  22.8 us
    unnamed x20, local copies, waits for them, and re-layouts  22.5 us
  transfers between devices with their start and end apart: 4, of which 4 were waited for; matrix products, arithmetic and copies ran while one was open for 1% of the time, Pallas kernels for 0%

commit v1 on v0

v1 whole, which is shorter than its diff:
```python
import math

import jax
import jax.numpy as jnp
import ml_dtypes
import numpy as np
from jax import lax
from jax.experimental import pallas as pl
from jax.experimental.pallas import tpu as pltpu
from jax.sharding import PartitionSpec as P

TWO_PI = 2.0 * math.pi
GRAD_EPS = 1e-06
LEN = 4096
RADIX = 16
SUB = 256
PARTS = 3
GROUP = 4
VMEM_LIMIT = 24 * 1024 * 1024


def np_parts(values):
    rest = np.asarray(values, np.float64)
    parts = []
    for _ in range(PARTS):
        part = rest.astype(np.float32).astype(ml_dtypes.bfloat16)
        parts.append(part)
        rest = rest - part.astype(np.float64)
    return parts


def np_tables():
    j = np.arange(SUB)
    angle = TWO_PI * (np.outer(j, j) % SUB) / SUB
    dft = np.stack(np_parts(np.cos(angle)) + np_parts(np.sin(angle)))
    k1 = np.arange(RADIX)
    twist = TWO_PI * np.outer(k1, j) / LEN
    mode = k1[:, None] + RADIX * j[None, :]
    signed = np.where(mode < LEN // 2, mode, mode - LEN)
    odd = np.where(mode == LEN // 2, 0, signed)
    small = np.stack([np.cos(twist), np.sin(twist), signed, odd]).astype(np.float32)
    return dft, small


def cadd(a, b):
    return (a[0] + b[0], a[1] + b[1])


def csub(a, b):
    return (a[0] - b[0], a[1] - b[1])


def dft4(x, sign):
    s = cadd(x[0], x[2])
    d = csub(x[0], x[2])
    t = cadd(x[1], x[3])
    e = csub(x[1], x[3])
    if sign < 0:
        ie = (e[1], -e[0])
    else:
        ie = (-e[1], e[0])
    return [cadd(s, t), cadd(d, ie), csub(s, t), csub(d, ie)]


def crot(x, turns, sign):
    if turns == 0:
        return x
    if turns == 4:
        return (x[1], -x[0]) if sign < 0 else (-x[1], x[0])
    c = math.cos(TWO_PI * turns / 16)
    s = sign * math.sin(TWO_PI * turns / 16)
    if turns == 2:
        return ((x[0] - sign * x[1]) * c, (x[1] + sign * x[0]) * c)
    if turns == 6:
        return ((x[0] + sign * x[1]) * c, (x[1] - sign * x[0]) * c)
    return (x[0] * c - x[1] * s, x[0] * s + x[1] * c)


def dft16(x, sign):
    out = [None] * 16
    rows = []
    for n2 in range(4):
        y = dft4([x[4 * n1 + n2] for n1 in range(4)], sign)
        rows.append([crot(y[k1], n2 * k1, sign) for k1 in range(4)])
    for k1 in range(4):
        z = dft4([rows[n2][k1] for n2 in range(4)], sign)
        for k2 in range(4):
            out[k1 + 4 * k2] = z[k2]
    return out


def split(values):
    parts = []
    rest = values
    for step in range(PARTS):
        part = rest.astype(jnp.bfloat16)
        parts.append(part)
        if step < PARTS - 1:
            rest = rest - part.astype(jnp.float32)
    return parts


def product(parts, table, first):
    total = None
    for order in reversed(range(PARTS)):
        for i in range(order + 1):
            term = jnp.dot(
                parts[i], table[first + order - i], preferred_element_type=jnp.float32
            )
            total = term if total is None else total + term
    return total


def transform(get, put, outputs, symbol, dft_ref, small_ref, a_ref, b_ref):
    for lane in range(2):
        lanes = slice(lane * 128, lane * 128 + 128)
        planes = dft16([get(m, lanes) for m in range(RADIX)], -1)
        for k1 in range(RADIX):
            re, im = planes[k1]
            if k1:
                c = small_ref[0, k1 : k1 + 1, lanes]
                s = small_ref[1, k1 : k1 + 1, lanes]
                re, im = re * c + im * s, im * c - re * s
            a_ref[k1, 0:16, lanes] = re
            a_ref[k1, 16:32, lanes] = im
    rows = GROUP * 16
    for group in range(RADIX // GROUP):
        ks = slice(group * GROUP, (group + 1) * GROUP)
        left = split(a_ref[ks].reshape(GROUP * 32, SUB))
        with_cos = product(left, dft_ref, 0).reshape(GROUP, 2, 16, SUB)
        with_sin = product(left, dft_ref, PARTS).reshape(GROUP, 2, 16, SUB)
        re = with_cos[:, 0] + with_sin[:, 1]
        im = with_cos[:, 1] - with_sin[:, 0]
        for o in range(outputs):
            sre, sim = symbol(o, ks, re, im)
            left = split(jnp.concatenate([sre, sim], axis=1).reshape(GROUP * 32, SUB))
            with_cos = product(left, dft_ref, 0).reshape(GROUP, 2, 16, SUB)
            with_sin = product(left, dft_ref, PARTS).reshape(GROUP, 2, 16, SUB)
            re2 = with_cos[:, 0] - with_sin[:, 1]
            im2 = with_cos[:, 1] + with_sin[:, 0]
            c = small_ref[0, ks][:, None, :]
            s = small_ref[1, ks][:, None, :]
            b_ref[o, ks, 0:16] = re2 * c - im2 * s
            b_ref[o, ks, 16:32] = im2 * c + re2 * s
    for lane in range(2):
        lanes = slice(lane * 128, lane * 128 + 128)
        outs = []
        for o in range(outputs):
            planes = [(b_ref[o, k, 0:16, lanes], b_ref[o, k, 16:32, lanes]) for k in range(RADIX)]
            outs.append(dft16(planes, 1))
        for m in range(RADIX):
            put(m, lanes, [outs[o][m] for o in range(outputs)])


def space_symbol(scale, small_ref):
    def symbol(o, ks, re, im):
        if o == 0:
            wave = small_ref[2, ks] * scale
            square = wave * wave
            even = ((square * square - square) * (1.0 / LEN))[:, None, :]
            return re * even, im * even
        odd = (small_ref[3, ks] * (scale * (1.0 / LEN)))[:, None, :]
        return -im * odd, re * odd

    return symbol


def time_symbol(scale, small_ref):
    def symbol(o, ks, re, im):
        odd = (small_ref[3, ks] * (scale * (1.0 / LEN)))[:, None, :]
        return -im * odd, re * odd

    return symbol


def space_at(m, lanes):
    start = (m % 2) * 256 + lanes.start
    return m // 2, slice(start, start + 128)


def blocks4(tiles):
    lane = lax.broadcasted_iota(jnp.int32, tiles[0].shape, len(tiles[0].shape) - 1)
    axis = len(tiles[0].shape) - 1
    low_half = lane < 64
    even = (lane // 32) % 2 == 0

    def swap(x, y, shift, mask):
        first = jnp.where(mask, x, pltpu.roll(y, shift, axis))
        second = jnp.where(mask, pltpu.roll(x, 128 - shift, axis), y)
        return first, second

    t0, t2 = swap(tiles[0], tiles[2], 64, low_half)
    t1, t3 = swap(tiles[1], tiles[3], 64, low_half)
    t0, t1 = swap(t0, t1, 32, even)
    t2, t3 = swap(t2, t3, 32, even)
    return [t0, t1, t2, t3]


def turn_kernel(u_ref, out_ref):
    for h in range(2):
        for a in range(4):
            tile = u_ref[h * 128 : h * 128 + 128, a * 128 : a * 128 + 128].T
            out_ref[:, a * 8 : a * 8 + 8, h * 128 : h * 128 + 128] = tile.reshape(16, 8, 128)


def space_first_kernel(scale_ref, u_ref, dft_ref, small_ref, out_ref, p_ref, a_ref, b_ref):
    def get(m, lanes):
        g, cols = space_at(m, lanes)
        return (u_ref[g, 0:16, cols], u_ref[g, 16:32, cols])

    def put(m, lanes, values):
        g, cols = space_at(m, lanes)
        for half in range(2):
            rows = slice(16 * half, 16 * half + 16)
            p_ref[g, rows, cols] = values[0][half] + u_ref[g, rows, cols] * values[1][half]

    transform(get, put, 2, space_symbol(scale_ref[0], small_ref), dft_ref, small_ref, a_ref, b_ref)
    for g in range(8):
        stack = jnp.concatenate([p_ref[g, :, a * 128 : a * 128 + 128] for a in range(4)], axis=0)
        turned = stack.T.reshape(16, 8, 128)
        for owner in range(16):
            out_ref[owner * 8 + g] = turned[owner]


def time_first_kernel(scale_ref, u_ref, dft_ref, small_ref, out_ref, q_ref, a_ref, b_ref):
    def get(m, lanes):
        return (u_ref[m, 0:16, lanes], u_ref[m, 16:32, lanes])

    def put(m, lanes, values):
        q_ref[m, 0:16, lanes] = values[0][0]
        q_ref[m, 16:32, lanes] = values[0][1]

    transform(get, put, 1, time_symbol(scale_ref[0], small_ref), dft_ref, small_ref, a_ref, b_ref)
    for m in range(16):
        for h in range(2):
            tiles = blocks4(
                [q_ref[m, 8 * a : 8 * a + 8, h * 128 : h * 128 + 128] for a in range(4)]
            )
            for k in range(4):
                out_ref[m * 8 + 4 * h + k] = tiles[k]


def time_second_kernel(
    scale_ref, q_ref, recv_ref, dft_ref, small_ref, out_ref, cost_ref, a_ref, b_ref
):
    total = jnp.zeros((8, 128), jnp.float32)
    for m in range(16):
        for h in range(2):
            tiles = blocks4([recv_ref[m * 8 + 4 * h + k, 0] for k in range(4)])
            for a in range(4):
                rows = slice(8 * a, 8 * a + 8)
                cols = slice(h * 128, h * 128 + 128)
                value = q_ref[m, rows, cols] + tiles[a]
                out_ref[m, 0, rows, cols] = value
                total = total + value * value
    cost_ref[...] = total * 0.5

    def get(m, lanes):
        return (out_ref[m, 0, 0:16, lanes], out_ref[m, 0, 16:32, lanes])

    def put(m, lanes, values):
        out_ref[m, 1, 0:16, lanes] = -values[0][0]
        out_ref[m, 1, 16:32, lanes] = -values[0][1]

    transform(get, put, 1, time_symbol(scale_ref[0], small_ref), dft_ref, small_ref, a_ref, b_ref)


def space_second_kernel(
    scale_ref, u_ref, p_ref, recv_ref, dft_ref, small_ref, out_ref, r_ref, a_ref, b_ref
):
    for g in range(8):
        stack = jnp.concatenate([recv_ref[owner * 8 + g, 1] for owner in range(16)], axis=0).T
        for a in range(4):
            cols = slice(a * 128, a * 128 + 128)
            r_ref[g, :, cols] = p_ref[g, :, cols] + stack[a * 32 : a * 32 + 32]

    def get(m, lanes):
        g, cols = space_at(m, lanes)
        return (r_ref[g, 0:16, cols], r_ref[g, 16:32, cols])

    def put(m, lanes, values):
        g, cols = space_at(m, lanes)
        for half in range(2):
            rows = slice(16 * half, 16 * half + 16)
            out_ref[g, rows, cols] = values[0][half] - u_ref[g, rows, cols] * values[1][half]

    transform(get, put, 2, space_symbol(scale_ref[0], small_ref), dft_ref, small_ref, a_ref, b_ref)


def unturn_kernel(recv_ref, r_ref, gt_ref):
    for o, ref in enumerate((r_ref, gt_ref)):
        for h in range(2):
            for a in range(4):
                tile = recv_ref[:, o, 8 * a : 8 * a + 8, h * 128 : h * 128 + 128]
                ref[h * 128 : h * 128 + 128, a * 128 : a * 128 + 128] = tile.reshape(128, 128).T


def norm_kernel(gx_ref, gt_ref, cost_ref, out_ref):
    g = gx_ref[...] + gt_ref[...]
    norm = jnp.sum(g * g)
    cost = jnp.sum(cost_ref[...])
    lane = lax.broadcasted_iota(jnp.int32, (128, 128), 1)
    out_ref[...] = jnp.where(lane == 0, norm, cost)


def update_kernel(u_ref, gx_ref, gt_ref, sums_ref, out_ref):
    sums = jnp.sum(sums_ref[...], axis=0, keepdims=True)
    step = sums[:, 1:2] / (sums[:, 0:1] + GRAD_EPS)
    out_ref[...] = u_ref[...] - step * (gx_ref[...] + gt_ref[...])


VM = pl.BlockSpec(memory_space=pltpu.VMEM)
SM = pl.BlockSpec(memory_space=pltpu.SMEM)


def f32(*shape):
    return jax.ShapeDtypeStruct(shape, jnp.float32)


def call(kernel, outs, scalars, arrays, work=0, flops=0):
    scratch = []
    if work:
        scratch = [
            pltpu.VMEM((RADIX, 32, SUB), jnp.float32),
            pltpu.VMEM((work, RADIX, 32, SUB), jnp.float32),
        ]
    return pl.pallas_call(
        kernel,
        out_shape=outs,
        in_specs=[SM] * len(scalars) + [VM] * len(arrays),
        out_specs=jax.tree.map(lambda _: VM, outs),
        scratch_shapes=scratch,
        cost_estimate=pl.CostEstimate(flops=flops, bytes_accessed=2**21, transcendentals=0),
        compiler_params=pltpu.CompilerParams(vmem_limit_bytes=VMEM_LIMIT),
    )(*scalars, *arrays)


def local(field, time_period, space_period):
    dft_np, small_np = np_tables()
    dft = jnp.asarray(dft_np)
    small = jnp.asarray(small_np)
    time_scale = TWO_PI / time_period
    space_scale = TWO_PI / space_period
    every = ("ta", "gx")

    rows_u = lax.all_to_all(field.reshape(8, 32, 512), "gx", 0, 0)
    turned = call(turn_kernel, f32(16, 32, 256), [], [field])
    cols_u = lax.all_to_all(turned, "ta", 0, 0)

    p_pieces, rows_p = call(
        space_first_kernel,
        (f32(128, 8, 128), f32(8, 32, 512)),
        [space_scale],
        [rows_u, dft, small],
        work=2,
        flops=3 * 10**9,
    )
    q_pieces, cols_q = call(
        time_first_kernel,
        (f32(128, 8, 128), f32(16, 32, 256)),
        [time_scale],
        [cols_u, dft, small],
        work=1,
        flops=2 * 10**9,
    )
    pieces = jnp.stack([p_pieces, q_pieces], axis=1)
    received = lax.all_to_all(pieces, every, 0, 0)

    turned_back, cost = call(
        time_second_kernel,
        (f32(16, 2, 32, 256), f32(8, 128)),
        [time_scale],
        [cols_q, received, dft, small],
        work=1,
        flops=2 * 10**9,
    )
    back = lax.all_to_all(turned_back, "ta", 0, 0)
    rows_g, _ = call(
        space_second_kernel,
        (f32(8, 32, 512), f32(8, 32, 512)),
        [space_scale],
        [rows_u, rows_p, received, dft, small],
        work=2,
        flops=3 * 10**9,
    )
    gx = lax.all_to_all(rows_g, "gx", 0, 0).reshape(256, 512)
    residual, gt = call(unturn_kernel, (f32(256, 512), f32(256, 512)), [], [back])

    sums = call(norm_kernel, f32(128, 128), [], [gx, gt, cost])
    sums = lax.all_to_all(sums, every, 0, 0, tiled=True)
    updated = call(update_kernel, f32(256, 512), [], [field, gx, gt, sums])
    return updated, residual


def solution(mesh):
    placed = (P(("tile", "ta"), "gx"), P("tile"), P("tile"))
    return jax.shard_map(
        local,
        mesh=mesh,
        in_specs=placed,
        out_specs=(P(("tile", "ta"), "gx"), P(("tile", "ta"), "gx")),
        check_vma=False,
    )
```

time: 799 us -> 147 us (0.18); the launches traced: 789 us -> 146 us
  blocking collectives: 432 us -> 72.7 us
  local copies, waits for them, and re-layouts: 116 us -> 1.75 us
  matrix products: 86.7 us -> 0 us
  waiting for transfers between devices: 80.1 us -> 31.1 us
  other arithmetic: 39.4 us -> 0.07 us
  Pallas kernels: 0 us -> 21.1 us
  starting transfers between devices: 30.3 us -> 16.9 us
    psum x1 -> x0, blocking collectives: 345 us -> none  [local(): cost_total = lax.psum(cost_local, ('ta', 'gx'))]
    dot_general x28 -> x0, matrix products: 54.3 us -> none  [contract(): return jnp.einsum(form, left_op, right_op, precision=lax.Precision.HIGHEST)]
    all_to_all x4 -> x3, waiting for transfers between devices: 80.1 us -> 31.1 us  [the longest x1 12 us: local(): gx = lax.all_to_all(rows_g, 'gx', 0, 0).reshape(256, 512)]
    unnamed x16 -> x0, matrix products: 32.4 us -> none
    another operation x12 -> x0, local copies, waits for them, and re-layouts: 24.8 us -> none  [the longest x8 17.2 us: pack_blocks(): jnp.stack([real_part.reshape(row_count, blocks, col_count), imag_part.res...]
    concatenate x8 -> x0, local copies, waits for them, and re-layouts: 22.4 us -> none  [the longest x2 6.99 us: forward_cols(): joined = jnp.concatenate([part_real, part_imag], axis=2)]
    reshape x13 -> x0, local copies, waits for them, and re-layouts: 22.2 us -> none  [the longest x4 6.86 us: inverse_cols(): shaped = stacked.reshape(low_factor, high_factor, col_width)]
    pallas_call x0 -> x8, Pallas kernels: none -> 21.1 us  [call(): pl.pallas_call(kernel, out_shape=outs, in_specs=[SM] * len(scalars) + [VM...]
  transfers between devices with their start and end apart: 4 -> 3, of which waited for: 4 -> 3; matrix products, arithmetic and copies ran while one was open for 1% -> 0% of each run, Pallas kernels for 0% -> 6%
where the time goes in v1:
time: 147 us; the launch traced here: 146 us
  blocking collectives  72.7 us (49%)
  waiting for transfers between devices  31.1 us (21%)
  Pallas kernels  21.1 us (14%)
  starting transfers between devices  16.9 us (11%)
  between operations  2.09 us (1%)
  local copies, waits for them, and re-layouts  1.75 us (1%)
    all_to_all x1, blocking collectives, local(): received = lax.all_to_all(pieces, every, 0, 0)  36.4 us
    pallas_call x8, Pallas kernels, call(): pl.pallas_call(kernel, out_shape=outs, in_specs=[SM] * len(scalars) + [VM...  21.1 us
    all_to_all x1, blocking collectives, local(): cols_u = lax.all_to_all(turned, 'ta', 0, 0)  18.4 us
    all_to_all x1, blocking collectives, local(): sums = lax.all_to_all(sums, every, 0, 0, tiled=True)  18 us
    all_to_all x1, waiting for transfers between devices, local(): gx = lax.all_to_all(rows_g, 'gx', 0, 0).reshape(256, 512)  12 us
    all_to_all x1, waiting for transfers between devices, local(): rows_u = lax.all_to_all(field.reshape(8, 32, 512), 'gx', 0, 0)  10.5 us
    all_to_all x1, starting transfers between devices, local(): rows_u = lax.all_to_all(field.reshape(8, 32, 512), 'gx', 0, 0)  8.7 us
    all_to_all x1, waiting for transfers between devices, local(): back = lax.all_to_all(turned_back, 'ta', 0, 0)  8.62 us
  transfers between devices with their start and end apart: 3, of which 3 were waited for; matrix products, arithmetic and copies ran while one was open for 0% of the time, Pallas kernels for 6%

profile of v1, /device:TPU:32, one launch (start us, length us, event | category | flops | bytes accessed | tf_op | source)
XLA Modules:
  0.0 145.7 jit_solution(5203290199649929072)
XLA Ops:
  0.6 1.2 shard_map.69
  1.9 18.4 %all_to_all.36.u_ref = f32[16,32,256]{2,1,0:T(8,128)S(1)} all-to-all(f32[16,32,256]{2,1,0:T(8,128)S(1)} %shard_map.69), channel_id=1, replica_groups=mesh['tile'=2,'ta'=16,'gx'=8] {'ta'}, dimensions={0} | all-to-all | bytes 1048576 | tf_op jit(solution)/shard_map/all_to_all | solution.py:348
  20.2 0.0 copy-start
  20.2 0.0 copy-start.1
  20.2 8.7 %all-to-all-start = ((f32[8,32,512]{2,1,0:T(8,128)}), f32[8,32,512]{2,1,0:T(8,128)S(1)}, u32[]{:S(2)}, u32[]{:S(2)}) async-start(f32[8,32,512]{2,1,0:T(8,128)} %bitcast), calls=%async_computation | async-start | bytes 1048576 | tf_op jit(solution)/shard_map/all_to_all | solution.py:346
  30.3 0.0 copy-done
  30.3 0.0 copy-done.1
  30.3 2.8 %shard_map.70 = (f32[128,8,128]{2,1,0:T(8,128)S(1)}, f32[16,32,256]{2,1,0:T(8,128)S(1)}) custom-call(f32[1]{0:T(128)S(6)} %div.7.scale_ref, f32[16,32,256]{2,1,0:T(8,128)S(1)} %all_to_all.36.u_ref, bf16[6,256,256]{2,1,0:T(8,128)(2,1)S(1)} %copy-done, f32[4,16,256]{2,1,0:T(8,128)S(1)} %copy-done.1), custom_call_target="tpu_custom_call" | custom-call | flops 2000000000 | bytes 2097152 | tf_op jit(solution)/shard_map/pallas_call | solution.py:327
  33.2 10.5 %all-to-all-done.u_ref = f32[8,32,512]{2,1,0:T(8,128)S(1)} async-done(((f32[8,32,512]{2,1,0:T(8,128)}), f32[8,32,512]{2,1,0:T(8,128)S(1)}, u32[]{:S(2)}, u32[]{:S(2)}) %all-to-all-start) | async-done | bytes 524320 | tf_op jit(solution)/shard_map/all_to_all | solution.py:346
  43.7 4.5 %shard_map.68 = (f32[128,8,128]{2,1,0:T(8,128)S(1)}, f32[8,32,512]{2,1,0:T(8,128)S(1)}) custom-call(f32[1]{0:T(128)S(6)} %div.6.scale_ref, f32[8,32,512]{2,1,0:T(8,128)S(1)} %all-to-all-done.u_ref, bf16[6,256,256]{2,1,0:T(8,128)(2,1)S(1)} %copy-done, f32[4,16,256]{2,1,0:T(8,128)S(1)} %copy-done.1), custom_call_target="tpu_custom_call" | custom-call | flops 3000000000 | bytes 2097152 | tf_op jit(solution)/shard_map/pallas_call | solution.py:327
  48.2 0.0 copy-start.2
  48.2 0.1 pad_maximum_fusion
  48.2 0.7 copy-done.2
  49.0 36.4 %all_to_all.37.recv_ref = f32[128,2,8,128]{3,2,1,0:T(8,128)S(1)} all-to-all(f32[128,2,8,128]{3,2,1,0:T(8,128)S(1)} %pad_maximum_fusion), channel_id=1, replica_groups=mesh['tile'=2,'ta'=16,'gx'=8] {'ta','gx'}, dimensions={0} | all-to-all | bytes 2097152 | tf_op jit(solution)/shard_map/all_to_all | solution.py:367
  85.3 3.9 %shard_map.72 = (f32[16,2,32,256]{3,2,1,0:T(8,128)}, f32[8,128]{1,0:T(8,128)S(1)}) custom-call(f32[1]{0:T(128)S(6)} %div.7.scale_ref, f32[16,32,256]{2,1,0:T(8,128)S(1)} %get-tuple-element.15.q_ref, f32[128,2,8,128]{3,2,1,0:T(8,128)S(1)} %all_to_all.37.recv_ref, bf16[6,256,256]{2,1,0:T(8,128)(2,1)S(1)} %copy-done, f32[4,16,256]{2,1,0:T(8,128)S(1)} %copy-done.1), custom_call_target="tpu_custom_call" | custom-call | flops 2000000000 | bytes 2097152 | tf_op jit(solution)/shard_map/pallas_call | solution.py:327
  89.2 3.8 %all-to-all-start.4 = ((f32[16,2,32,256]{3,2,1,0:T(8,128)}), f32[16,2,32,256]{3,2,1,0:T(8,128)S(1)}, u32[]{:S(2)}, u32[]{:S(2)}) async-start(f32[16,2,32,256]{3,2,1,0:T(8,128)} %get-tuple-element.16), calls=%async_computation.4 | async-start | bytes 2097152 | tf_op jit(solution)/shard_map/all_to_all | solution.py:377
  93.0 0.0 copy-start.3
  93.0 1.0 copy-done.3
  94.1 5.3 %shard_map.71 = (f32[8,32,512]{2,1,0:T(8,128)}, f32[8,32,512]{2,1,0:T(8,128)}) custom-call(f32[1]{0:T(128)S(6)} %div.6.scale_ref, f32[8,32,512]{2,1,0:T(8,128)S(1)} %all-to-all-done.u_ref, f32[8,32,512]{2,1,0:T(8,128)S(1)} %copy-done.3, f32[128,2,8,128]{3,2,1,0:T(8,128)S(1)} %all_to_all.37.recv_ref, bf16[6,256,256]{2,1,0:T(8,128)(2,1)S(1)} %copy-done, ...), custom_call_target="tpu_custom_call" | custom-call | flops 3000000000 | bytes 2097152 | tf_op jit(solution)/shard_map/pallas_call | solution.py:327
  99.3 8.6 %all-to-all-done.4.recv_ref = f32[16,2,32,256]{3,2,1,0:T(8,128)S(1)} async-done(((f32[16,2,32,256]{3,2,1,0:T(8,128)}), f32[16,2,32,256]{3,2,1,0:T(8,128)S(1)}, u32[]{:S(2)}, u32[]{:S(2)}) %all-to-all-start.4) | async-done | bytes 1048608 | tf_op jit(solution)/shard_map/all_to_all | solution.py:377
  107.9 4.4 %all-to-all-start.3 = ((f32[8,32,512]{2,1,0:T(8,128)}), f32[8,32,512]{2,1,0:T(8,128)S(1)}, u32[]{:S(2)}, u32[]{:S(2)}) async-start(f32[8,32,512]{2,1,0:T(8,128)} %get-tuple-element.14), calls=%async_computation.3 | async-start | bytes 1048576 | tf_op jit(solution)/shard_map/all_to_all | solution.py:386
  112.3 1.0 shard_map.73
  113.3 12.0 %all-to-all-done.3 = f32[8,32,512]{2,1,0:T(8,128)S(1)} async-done(((f32[8,32,512]{2,1,0:T(8,128)}), f32[8,32,512]{2,1,0:T(8,128)S(1)}, u32[]{:S(2)}, u32[]{:S(2)}) %all-to-all-start.3) | async-done | bytes 524320 | tf_op jit(solution)/shard_map/all_to_all | solution.py:386
  125.3 0.3 shard_map.74
  125.6 18.0 %all_to_all.38 = f32[128,1,128]{2,1,0:T(1,128)S(1)} all-to-all(f32[128,1,128]{2,1,0:T(1,128)S(1)} %bitcast.13), channel_id=1, replica_groups=mesh['tile'=2,'ta'=16,'gx'=8] {'ta','gx'}, dimensions={0} | all-to-all | bytes 131072 | tf_op jit(solution)/shard_map/all_to_all | solution.py:390
  143.6 2.1 %shard_map.75 = f32[256,512]{1,0:T(8,128)} custom-call(f32[256,512]{1,0:T(8,128)} %u_ref.3, f32[256,512]{1,0:T(8,128)S(1)} %bitcast.9, f32[256,512]{1,0:T(8,128)S(1)} %get-tuple-element.17.gt_ref, f32[128,128]{1,0:T(8,128)S(1)} %bitcast.12), custom_call_target="tpu_custom_call" | custom-call | bytes 2097152 | tf_op jit(solution)/shard_map/pallas_call | solution.py:327
Async XLA Ops:
  20.2 10.1 %copy-start = (bf16[6,256,256]{2,1,0:T(8,128)(2,1)S(1)}, bf16[6,256,256]{2,1,0:T(8,128)(2,1)}, u32[]{:S(2)}) copy-start(bf16[6,256,256]{2,1,0:T(8,128)(2,1)} %constant.6.clone.dft_ref) | copy-start | bytes 2359300
  20.2 10.1 %copy-start.1 = (f32[4,16,256]{2,1,0:T(8,128)S(1)}, f32[4,16,256]{2,1,0:T(8,128)}, u32[]{:S(2)}) copy-start(f32[4,16,256]{2,1,0:T(8,128)} %constant.7.clone.small_ref) | copy-start | bytes 196612
  20.2 23.4 %all-to-all-start = ((f32[8,32,512]{2,1,0:T(8,128)}), f32[8,32,512]{2,1,0:T(8,128)S(1)}, u32[]{:S(2)}, u32[]{:S(2)}) async-start(f32[8,32,512]{2,1,0:T(8,128)} %bitcast), calls=%async_computation | async-start | bytes 1048576 | tf_op jit(solution)/shard_map/all_to_all | solution.py:346
  48.2 0.8 copy-start.2
  89.2 18.8 %all-to-all-start.4 = ((f32[16,2,32,256]{3,2,1,0:T(8,128)}), f32[16,2,32,256]{3,2,1,0:T(8,128)S(1)}, u32[]{:S(2)}, u32[]{:S(2)}) async-start(f32[16,2,32,256]{3,2,1,0:T(8,128)} %get-tuple-element.16), calls=%async_computation.4 | async-start | bytes 2097152 | tf_op jit(solution)/shard_map/all_to_all | solution.py:377
  93.0 1.0 copy-start.3
  107.9 17.4 %all-to-all-start.3 = ((f32[8,32,512]{2,1,0:T(8,128)}), f32[8,32,512]{2,1,0:T(8,128)S(1)}, u32[]{:S(2)}, u32[]{:S(2)}) async-start(f32[8,32,512]{2,1,0:T(8,128)} %get-tuple-element.14), calls=%async_computation.3 | async-start | bytes 1048576 | tf_op jit(solution)/shard_map/all_to_all | solution.py:386

commit v2 on v1

--- a/solution.py
+++ b/solution.py
@@ -203,26 +203,44 @@
             out_ref[:, a * 8 : a * 8 + 8, h * 128 : h * 128 + 128] = tile.reshape(16, 8, 128)
 
 
-def space_first_kernel(scale_ref, u_ref, dft_ref, small_ref, out_ref, p_ref, a_ref, b_ref):
-    def get(m, lanes):
+def space_kernel(scale_ref, u_ref, dft_ref, small_ref, out_ref, p_ref, v_ref, a_ref, b_ref):
+    def send(slot, ref):
+        for g in range(8):
+            stack = jnp.concatenate([ref[g, :, a * 128 : a * 128 + 128] for a in range(4)], axis=0)
+            turned = stack.T.reshape(16, 8, 128)
+            for owner in range(16):
+                out_ref[owner * 8 + g, 8 * slot : 8 * slot + 8] = turned[owner]
+
+    def get_u(m, lanes):
         g, cols = space_at(m, lanes)
         return (u_ref[g, 0:16, cols], u_ref[g, 16:32, cols])
 
-    def put(m, lanes, values):
+    def put_u(m, lanes, values):
         g, cols = space_at(m, lanes)
         for half in range(2):
             rows = slice(16 * half, 16 * half + 16)
             p_ref[g, rows, cols] = values[0][half] + u_ref[g, rows, cols] * values[1][half]
-
-    transform(get, put, 2, space_symbol(scale_ref[0], small_ref), dft_ref, small_ref, a_ref, b_ref)
-    for g in range(8):
-        stack = jnp.concatenate([p_ref[g, :, a * 128 : a * 128 + 128] for a in range(4)], axis=0)
-        turned = stack.T.reshape(16, 8, 128)
-        for owner in range(16):
-            out_ref[owner * 8 + g] = turned[owner]
-
-
-def time_first_kernel(scale_ref, u_ref, dft_ref, small_ref, out_ref, q_ref, a_ref, b_ref):
+            v_ref[g, rows, cols] = values[1][half]
+
+    def get_p(m, lanes):
+        g, cols = space_at(m, lanes)
+        return (p_ref[g, 0:16, cols], p_ref[g, 16:32, cols])
+
+    def put_p(m, lanes, values):
+        g, cols = space_at(m, lanes)
+        for half in range(2):
+            rows = slice(16 * half, 16 * half + 16)
+            v_ref[g, rows, cols] = values[0][half] - u_ref[g, rows, cols] * values[1][half]
+
+    symbol = space_symbol(scale_ref[0], small_ref)
+    transform(get_u, put_u, 2, symbol, dft_ref, small_ref, a_ref, b_ref)
+    send(0, v_ref)
+    send(1, p_ref)
+    transform(get_p, put_p, 2, symbol, dft_ref, small_ref, a_ref, b_ref)
+    send(2, v_ref)
+
+
+def time_first_kernel(scale_ref, u_ref, dft_ref, small_ref, q_ref, a_ref, b_ref):
     def get(m, lanes):
         return (u_ref[m, 0:16, lanes], u_ref[m, 16:32, lanes])
 
@@ -231,82 +249,81 @@
         q_ref[m, 16:32, lanes] = values[0][1]
 
     transform(get, put, 1, time_symbol(scale_ref[0], small_ref), dft_ref, small_ref, a_ref, b_ref)
+
+
+def time_second_kernel(
+    scale_ref, u_ref, q_ref, recv_ref, dft_ref, small_ref, out_ref, v_ref, s_ref, g_ref, a_ref, b_ref
+):
+    cost = jnp.zeros((8, 128), jnp.float32)
     for m in range(16):
         for h in range(2):
-            tiles = blocks4(
-                [q_ref[m, 8 * a : 8 * a + 8, h * 128 : h * 128 + 128] for a in range(4)]
-            )
-            for k in range(4):
-                out_ref[m * 8 + 4 * h + k] = tiles[k]
-
-
-def time_second_kernel(
-    scale_ref, q_ref, recv_ref, dft_ref, small_ref, out_ref, cost_ref, a_ref, b_ref
-):
-    total = jnp.zeros((8, 128), jnp.float32)
-    for m in range(16):
-        for h in range(2):
-            tiles = blocks4([recv_ref[m * 8 + 4 * h + k, 0] for k in range(4)])
+            cols = slice(h * 128, h * 128 + 128)
+            tiles = [
+                blocks4([recv_ref[m * 8 + 4 * h + k, 8 * o : 8 * o + 8] for k in range(4)])
+                for o in range(3)
+            ]
             for a in range(4):
                 rows = slice(8 * a, 8 * a + 8)
-                cols = slice(h * 128, h * 128 + 128)
-                value = q_ref[m, rows, cols] + tiles[a]
-                out_ref[m, 0, rows, cols] = value
-                total = total + value * value
-    cost_ref[...] = total * 0.5
-
-    def get(m, lanes):
-        return (out_ref[m, 0, 0:16, lanes], out_ref[m, 0, 16:32, lanes])
-
-    def put(m, lanes, values):
-        out_ref[m, 1, 0:16, lanes] = -values[0][0]
-        out_ref[m, 1, 16:32, lanes] = -values[0][1]
-
-    transform(get, put, 1, time_symbol(scale_ref[0], small_ref), dft_ref, small_ref, a_ref, b_ref)
-
-
-def space_second_kernel(
-    scale_ref, u_ref, p_ref, recv_ref, dft_ref, small_ref, out_ref, r_ref, a_ref, b_ref
-):
-    for g in range(8):
-        stack = jnp.concatenate([recv_ref[owner * 8 + g, 1] for owner in range(16)], axis=0).T
-        for a in range(4):
-            cols = slice(a * 128, a * 128 + 128)
-            r_ref[g, :, cols] = p_ref[g, :, cols] + stack[a * 32 : a * 32 + 32]
-
-    def get(m, lanes):
-        g, cols = space_at(m, lanes)
-        return (r_ref[g, 0:16, cols], r_ref[g, 16:32, cols])
-
-    def put(m, lanes, values):
-        g, cols = space_at(m, lanes)
-        for half in range(2):
-            rows = slice(16 * half, 16 * half + 16)
-            out_ref[g, rows, cols] = values[0][half] - u_ref[g, rows, cols] * values[1][half]
-
-    transform(get, put, 2, space_symbol(scale_ref[0], small_ref), dft_ref, small_ref, a_ref, b_ref)
-
-
-def unturn_kernel(recv_ref, r_ref, gt_ref):
-    for o, ref in enumerate((r_ref, gt_ref)):
+                q = q_ref[m, rows, cols]
+                v_ref[m, rows, cols] = tiles[0][a]
+                s_ref[m, rows, cols] = q + u_ref[m, rows, cols] * tiles[0][a]
+                r = q + tiles[1][a]
+                out_ref[m, rows, cols] = r
+                cost = cost + r * r
+                g_ref[m, rows, cols] = tiles[2][a]
+
+    halves = (slice(0, 16), slice(16, 32))
+    norm = [jnp.zeros((16, 128), jnp.float32)]
+
+    def get_v(m, lanes):
+        return tuple(v_ref[m, rows, lanes] for rows in halves)
+
+    def put_v(m, lanes, values):
+        for half, rows in enumerate(halves):
+            g_ref[m, rows, lanes] = (
+                g_ref[m, rows, lanes] - u_ref[m, rows, lanes] * values[0][half]
+            )
+
+    def get_s(m, lanes):
+        return tuple(s_ref[m, rows, lanes] for rows in halves)
+
+    def put_s(m, lanes, values):
+        for half, rows in enumerate(halves):
+            g = g_ref[m, rows, lanes] - values[0][half]
+            out_ref[m, 32 + rows.start : 32 + rows.stop, lanes] = g
+            norm[0] = norm[0] + g * g
+
+    symbol = time_symbol(scale_ref[0], small_ref)
+    transform(get_v, put_v, 1, symbol, dft_ref, small_ref, a_ref, b_ref)
+    transform(get_s, put_s, 1, symbol, dft_ref, small_ref, a_ref, b_ref)
+    norm = norm[0][0:8] + norm[0][8:16]
+    for m in range(16):
+        out_ref[m, 64:72, 0:128] = 0.5 * cost
+        out_ref[m, 64:72, 128:256] = norm
+
+
+def sums_kernel(recv_ref, out_ref):
+    total = jnp.sum(recv_ref[:, 64:72, :], axis=0)
+    cost = jnp.sum(total[:, 0:128], axis=0, keepdims=True)
+    norm = jnp.sum(total[:, 128:256], axis=0, keepdims=True)
+    row = lax.broadcasted_iota(jnp.int32, (8, 128), 0)
+    out_ref[...] = jnp.broadcast_to(jnp.where(row == 0, cost, norm)[None], (8, 8, 128))
+
+
+def unturn_kernel(recv_ref, r_ref, g_ref):
+    for o, ref in enumerate((r_ref, g_ref)):
         for h in range(2):
             for a in range(4):
-                tile = recv_ref[:, o, 8 * a : 8 * a + 8, h * 128 : h * 128 + 128]
+                first = 32 * o + 8 * a
+                tile = recv_ref[:, first : first + 8, h * 128 : h * 128 + 128]
                 ref[h * 128 : h * 128 + 128, a * 128 : a * 128 + 128] = tile.reshape(128, 128).T
 
 
-def norm_kernel(gx_ref, gt_ref, cost_ref, out_ref):
-    g = gx_ref[...] + gt_ref[...]
-    norm = jnp.sum(g * g)
-    cost = jnp.sum(cost_ref[...])
-    lane = lax.broadcasted_iota(jnp.int32, (128, 128), 1)
-    out_ref[...] = jnp.where(lane == 0, norm, cost)
-
-
-def update_kernel(u_ref, gx_ref, gt_ref, sums_ref, out_ref):
-    sums = jnp.sum(sums_ref[...], axis=0, keepdims=True)
-    step = sums[:, 1:2] / (sums[:, 0:1] + GRAD_EPS)
-    out_ref[...] = u_ref[...] - step * (gx_ref[...] + gt_ref[...])
+def update_kernel(u_ref, g_ref, sums_ref, out_ref):
+    sums = jnp.sum(sums_ref[...], axis=0)
+    cost = jnp.sum(sums[0:1, :], axis=1, keepdims=True)
+    norm = jnp.sum(sums[1:2, :], axis=1, keepdims=True)
+    out_ref[...] = u_ref[...] - (cost / (norm + GRAD_EPS)) * g_ref[...]
 
 
 VM = pl.BlockSpec(memory_space=pltpu.VMEM)
@@ -317,19 +334,13 @@
     return jax.ShapeDtypeStruct(shape, jnp.float32)
 
 
-def call(kernel, outs, scalars, arrays, work=0, flops=0):
-    scratch = []
-    if work:
-        scratch = [
-            pltpu.VMEM((RADIX, 32, SUB), jnp.float32),
-            pltpu.VMEM((work, RADIX, 32, SUB), jnp.float32),
-        ]
+def call(kernel, outs, scalars, arrays, scratch=(), flops=0):
     return pl.pallas_call(
         kernel,
         out_shape=outs,
         in_specs=[SM] * len(scalars) + [VM] * len(arrays),
         out_specs=jax.tree.map(lambda _: VM, outs),
-        scratch_shapes=scratch,
+        scratch_shapes=[pltpu.VMEM(shape, jnp.float32) for shape in scratch],
         cost_estimate=pl.CostEstimate(flops=flops, bytes_accessed=2**21, transcendentals=0),
         compiler_params=pltpu.CompilerParams(vmem_limit_bytes=VMEM_LIMIT),
     )(*scalars, *arrays)
@@ -342,53 +353,44 @@
     time_scale = TWO_PI / time_period
     space_scale = TWO_PI / space_period
     every = ("ta", "gx")
-
-    rows_u = lax.all_to_all(field.reshape(8, 32, 512), "gx", 0, 0)
-    turned = call(turn_kernel, f32(16, 32, 256), [], [field])
+    rows, cols = (8, 32, 512), (16, 32, 256)
+    planes = (RADIX, 32, SUB)
+
+    rows_u = lax.all_to_all(field.reshape(rows), "gx", 0, 0)
+    turned = call(turn_kernel, f32(*cols), [], [field])
+    rows_u, turned = lax.optimization_barrier((rows_u, turned))
     cols_u = lax.all_to_all(turned, "ta", 0, 0)
 
-    p_pieces, rows_p = call(
-        space_first_kernel,
-        (f32(128, 8, 128), f32(8, 32, 512)),
+    pieces = call(
+        space_kernel,
+        f32(128, 24, 128),
         [space_scale],
         [rows_u, dft, small],
-        work=2,
-        flops=3 * 10**9,
+        [rows, rows, planes, (2, *planes)],
+        flops=8 * 10**9,
     )
-    q_pieces, cols_q = call(
+    received = lax.all_to_all(pieces, every, 0, 0)
+    cols_q = call(
         time_first_kernel,
-        (f32(128, 8, 128), f32(16, 32, 256)),
+        f32(*cols),
         [time_scale],
         [cols_u, dft, small],
-        work=1,
+        [planes, (1, *planes)],
         flops=2 * 10**9,
     )
-    pieces = jnp.stack([p_pieces, q_pieces], axis=1)
-    received = lax.all_to_all(pieces, every, 0, 0)
-
-    turned_back, cost = call(
+    cols_out = call(
         time_second_kernel,
-        (f32(16, 2, 32, 256), f32(8, 128)),
+        f32(16, 72, 256),
         [time_scale],
-        [cols_q, received, dft, small],
-        work=1,
-        flops=2 * 10**9,
+        [cols_u, cols_q, received, dft, small],
+        [cols, cols, cols, planes, (1, *planes)],
+        flops=4 * 10**9,
     )
-    back = lax.all_to_all(turned_back, "ta", 0, 0)
-    rows_g, _ = call(
-        space_second_kernel,
-        (f32(8, 32, 512), f32(8, 32, 512)),
-        [space_scale],
-        [rows_u, rows_p, received, dft, small],
-        work=2,
-        flops=3 * 10**9,
-    )
-    gx = lax.all_to_all(rows_g, "gx", 0, 0).reshape(256, 512)
-    residual, gt = call(unturn_kernel, (f32(256, 512), f32(256, 512)), [], [back])
-
-    sums = call(norm_kernel, f32(128, 128), [], [gx, gt, cost])
-    sums = lax.all_to_all(sums, every, 0, 0, tiled=True)
-    updated = call(update_kernel, f32(256, 512), [], [field, gx, gt, sums])
+    back = lax.all_to_all(cols_out, "ta", 0, 0)
+    sums = call(sums_kernel, f32(8, 8, 128), [], [back])
+    sums = lax.all_to_all(sums, "gx", 0, 0)
+    residual, gradient = call(unturn_kernel, (f32(256, 512), f32(256, 512)), [], [back])
+    updated = call(update_kernel, f32(256, 512), [], [field, gradient, sums])
     return updated, residual
 
 

time: 147 us -> 132 us (0.90)
  blocking collectives: 72.7 us -> 19.5 us
  waiting for transfers between devices: 31.1 us -> 58.2 us
  starting transfers between devices: 16.9 us -> 29.9 us
    all_to_all x3 -> x1, blocking collectives: 72.7 us -> 19.5 us  [local(): back = lax.all_to_all(cols_out, 'ta', 0, 0)]
    all_to_all x3 -> x4, waiting for transfers between devices: 31.1 us -> 58.2 us  [the longest x1 39.1 us: local(): received = lax.all_to_all(pieces, every, 0, 0)]
    all_to_all x3 -> x4, starting transfers between devices: 16.9 us -> 29.9 us  [the longest x1 9.62 us: local(): received = lax.all_to_all(pieces, every, 0, 0)]
    pallas_call x8 -> x7, Pallas kernels: 21.1 us -> 20.6 us  [call(): pl.pallas_call(kernel, out_shape=outs, in_specs=[SM] * len(scalars) + [VM...]
  transfers between devices with their start and end apart: 3 -> 4, of which waited for: 3 -> 4; matrix products, arithmetic and copies ran while one was open for 0% -> 0% of each run, Pallas kernels for 6% -> 11%
where the time goes in v2:
time: 132 us; the launch traced here: 131 us
  waiting for transfers between devices  58.2 us (44%)
  starting transfers between devices  29.9 us (23%)
  Pallas kernels  20.6 us (16%)
  blocking collectives  19.5 us (15%)
  between operations  2.08 us (2%)
    all_to_all x1, waiting for transfers between devices, local(): received = lax.all_to_all(pieces, every, 0, 0)  39.1 us
    pallas_call x7, Pallas kernels, call(): pl.pallas_call(kernel, out_shape=outs, in_specs=[SM] * len(scalars) + [VM...  20.6 us
    all_to_all x1, blocking collectives, local(): back = lax.all_to_all(cols_out, 'ta', 0, 0)  19.5 us
    all_to_all x1, waiting for transfers between devices, local(): rows_u = lax.all_to_all(field.reshape(rows), 'gx', 0, 0)  13.3 us
    all_to_all x1, starting transfers between devices, local(): received = lax.all_to_all(pieces, every, 0, 0)  9.62 us
    all_to_all x1, starting transfers between devices, local(): rows_u = lax.all_to_all(field.reshape(rows), 'gx', 0, 0)  8.71 us
    all_to_all x1, starting transfers between devices, local(): cols_u = lax.all_to_all(turned, 'ta', 0, 0)  7.04 us
    all_to_all x1, waiting for transfers between devices, local(): sums = lax.all_to_all(sums, 'gx', 0, 0)  5.6 us
  transfers between devices with their start and end apart: 4, of which 4 were waited for; matrix products, arithmetic and copies ran while one was open for 0% of the time, Pallas kernels for 11%

profile of v2, /device:TPU:32, one launch (start us, length us, event | category | flops | bytes accessed | tf_op | source)
XLA Modules:
  0.0 131.4 jit_solution(9825255901861953643)
XLA Ops:
  0.6 0.0 copy-start.2
  0.6 0.0 copy-start.3
  0.7 8.7 %all-to-all-start = ((f32[8,32,512]{2,1,0:T(8,128)}), f32[8,32,512]{2,1,0:T(8,128)S(1)}, u32[]{:S(2)}, u32[]{:S(2)}) async-start(f32[8,32,512]{2,1,0:T(8,128)} %bitcast.1), calls=%async_computation | async-start | bytes 1048576 | tf_op jit(solution)/shard_map/all_to_all | solution.py:359
  9.4 0.0 copy-start
  9.4 1.1 copy-done
  10.4 1.0 shard_map.68
  12.1 13.3 %all-to-all-done.u_ref = f32[8,32,512]{2,1,0:T(8,128)S(1)} async-done(((f32[8,32,512]{2,1,0:T(8,128)}), f32[8,32,512]{2,1,0:T(8,128)S(1)}, u32[]{:S(2)}, u32[]{:S(2)}) %all-to-all-start) | async-done | bytes 524320 | tf_op jit(solution)/shard_map/all_to_all | solution.py:359
  25.4 7.0 %all-to-all-start.1 = ((f32[16,32,256]{2,1,0:T(8,128)}), f32[16,32,256]{2,1,0:T(8,128)S(1)}, u32[]{:S(2)}, u32[]{:S(2)}) async-start(f32[16,32,256]{2,1,0:T(8,128)} %shard_map.68), calls=%async_computation.1 | async-start | bytes 1048576 | tf_op jit(solution)/shard_map/all_to_all | solution.py:362
  32.4 0.0 copy-done.2
  32.5 0.0 copy-done.3
  32.5 9.8 %shard_map.70 = f32[128,24,128]{2,1,0:T(8,128)} custom-call(f32[1]{0:T(128)S(6)} %div.7.scale_ref, f32[8,32,512]{2,1,0:T(8,128)S(1)} %all-to-all-done.u_ref, bf16[6,256,256]{2,1,0:T(8,128)(2,1)S(1)} %copy-done.2, f32[4,16,256]{2,1,0:T(8,128)S(1)} %copy-done.3), custom_call_target="tpu_custom_call" | custom-call | flops 8000000000 | bytes 2097152 | tf_op jit(solution)/shard_map/pallas_call | solution.py:338
  42.3 0.3 all-to-all-done.1.u_ref
  42.6 9.6 %all-to-all-start.2 = ((f32[128,24,128]{2,1,0:T(8,128)}), f32[128,24,128]{2,1,0:T(8,128)S(1)}, u32[]{:S(2)}, u32[]{:S(2)}) async-start(f32[128,24,128]{2,1,0:T(8,128)} %shard_map.70), calls=%async_computation.2 | async-start | bytes 3145728 | tf_op jit(solution)/shard_map/all_to_all | solution.py:372
  52.9 2.5 %shard_map.69.q_ref = f32[16,32,256]{2,1,0:T(8,128)S(1)} custom-call(f32[1]{0:T(128)S(6)} %div.6.scale_ref, f32[16,32,256]{2,1,0:T(8,128)S(1)} %all-to-all-done.1.u_ref, bf16[6,256,256]{2,1,0:T(8,128)(2,1)S(1)} %copy-done.2, f32[4,16,256]{2,1,0:T(8,128)S(1)} %copy-done.3), custom_call_target="tpu_custom_call" | custom-call | flops 2000000000 | bytes 2097152 | tf_op jit(solution)/shard_map/pallas_call | solution.py:338
  55.4 39.1 %all-to-all-done.2.recv_ref = f32[128,24,128]{2,1,0:T(8,128)S(1)} async-done(((f32[128,24,128]{2,1,0:T(8,128)}), f32[128,24,128]{2,1,0:T(8,128)S(1)}, u32[]{:S(2)}, u32[]{:S(2)}) %all-to-all-start.2) | async-done | bytes 1572896 | tf_op jit(solution)/shard_map/all_to_all | solution.py:372
  94.4 4.7 %shard_map.71 = f32[16,72,256]{2,1,0:T(8,128)S(1)} custom-call(f32[1]{0:T(128)S(6)} %div.6.scale_ref, f32[16,32,256]{2,1,0:T(8,128)S(1)} %all-to-all-done.1.u_ref, f32[16,32,256]{2,1,0:T(8,128)S(1)} %shard_map.69.q_ref, f32[128,24,128]{2,1,0:T(8,128)S(1)} %all-to-all-done.2.recv_ref, bf16[6,256,256]{2,1,0:T(8,128)(2,1)S(1)} %copy-done.2, ...), custom_call_target="tpu_custom_call" | custom-call | flops 4000000000 | bytes 2097152 | tf_op jit(solution)/shard_map/pallas_call | solution.py:338
  99.1 19.5 %all_to_all.25.recv_ref = f32[16,72,256]{2,1,0:T(8,128)S(1)} all-to-all(f32[16,72,256]{2,1,0:T(8,128)S(1)} %shard_map.71), channel_id=1, replica_groups=mesh['tile'=2,'ta'=16,'gx'=8] {'ta'}, dimensions={0} | all-to-all | bytes 2359296 | tf_op jit(solution)/shard_map/all_to_all | solution.py:389
  118.6 0.0 copy-start.1
  118.6 0.6 shard_map.73
  119.3 4.5 %all-to-all-start.4 = ((f32[8,8,128]{2,1,0:T(8,128)}), f32[8,8,128]{2,1,0:T(8,128)S(1)}, u32[]{:S(2)}, u32[]{:S(2)}) async-start(f32[8,8,128]{2,1,0:T(8,128)} %shard_map.73), calls=%async_computation.4 | async-start | bytes 65536 | tf_op jit(solution)/shard_map/all_to_all | solution.py:391
  123.8 1.0 shard_map.72
  124.8 5.6 %all-to-all-done.4.sums_ref = f32[8,8,128]{2,1,0:T(8,128)S(1)} async-done(((f32[8,8,128]{2,1,0:T(8,128)}), f32[8,8,128]{2,1,0:T(8,128)S(1)}, u32[]{:S(2)}, u32[]{:S(2)}) %all-to-all-start.4) | async-done | bytes 32800 | tf_op jit(solution)/shard_map/all_to_all | solution.py:391
  130.4 0.0 copy-done.1
  130.4 1.0 shard_map.74
Async XLA Ops:
  0.6 31.8 %copy-start.2 = (bf16[6,256,256]{2,1,0:T(8,128)(2,1)S(1)}, bf16[6,256,256]{2,1,0:T(8,128)(2,1)}, u32[]{:S(2)}) copy-start(bf16[6,256,256]{2,1,0:T(8,128)(2,1)} %constant.6.clone.dft_ref) | copy-start | bytes 2359300
  0.6 31.8 %copy-start.3 = (f32[4,16,256]{2,1,0:T(8,128)S(1)}, f32[4,16,256]{2,1,0:T(8,128)}, u32[]{:S(2)}) copy-start(f32[4,16,256]{2,1,0:T(8,128)} %constant.7.clone.small_ref) | copy-start | bytes 196612
  0.7 24.8 %all-to-all-start = ((f32[8,32,512]{2,1,0:T(8,128)}), f32[8,32,512]{2,1,0:T(8,128)S(1)}, u32[]{:S(2)}, u32[]{:S(2)}) async-start(f32[8,32,512]{2,1,0:T(8,128)} %bitcast.1), calls=%async_computation | async-start | bytes 1048576 | tf_op jit(solution)/shard_map/all_to_all | solution.py:359
  9.4 1.1 copy-start
  25.4 17.2 %all-to-all-start.1 = ((f32[16,32,256]{2,1,0:T(8,128)}), f32[16,32,256]{2,1,0:T(8,128)S(1)}, u32[]{:S(2)}, u32[]{:S(2)}) async-start(f32[16,32,256]{2,1,0:T(8,128)} %shard_map.68), calls=%async_computation.1 | async-start | bytes 1048576 | tf_op jit(solution)/shard_map/all_to_all | solution.py:362
  42.6 51.8 %all-to-all-start.2 = ((f32[128,24,128]{2,1,0:T(8,128)}), f32[128,24,128]{2,1,0:T(8,128)S(1)}, u32[]{:S(2)}, u32[]{:S(2)}) async-start(f32[128,24,128]{2,1,0:T(8,128)} %shard_map.70), calls=%async_computation.2 | async-start | bytes 3145728 | tf_op jit(solution)/shard_map/all_to_all | solution.py:372
  118.6 11.7 %copy-start.1 = (f32[256,512]{1,0:T(8,128)S(1)}, f32[256,512]{1,0:T(8,128)}, u32[]{:S(2)}) copy-start(f32[256,512]{1,0:T(8,128)} %u_ref.3) | copy-start | bytes 1572868
  119.3 11.1 %all-to-all-start.4 = ((f32[8,8,128]{2,1,0:T(8,128)}), f32[8,8,128]{2,1,0:T(8,128)S(1)}, u32[]{:S(2)}, u32[]{:S(2)}) async-start(f32[8,8,128]{2,1,0:T(8,128)} %shard_map.73), calls=%async_computation.4 | async-start | bytes 65536 | tf_op jit(solution)/shard_map/all_to_all | solution.py:391

commit v3 on v2

--- a/solution.py
+++ b/solution.py
@@ -12,10 +12,10 @@
 TWO_PI = 2.0 * math.pi
 GRAD_EPS = 1e-06
 LEN = 4096
-RADIX = 16
-SUB = 256
+RADIX = 32
+SUB = 128
 PARTS = 3
-GROUP = 4
+GROUP = 8
 VMEM_LIMIT = 24 * 1024 * 1024
 
 
@@ -32,7 +32,8 @@
 def np_tables():
     j = np.arange(SUB)
     angle = TWO_PI * (np.outer(j, j) % SUB) / SUB
-    dft = np.stack(np_parts(np.cos(angle)) + np_parts(np.sin(angle)))
+    cos, sin = np.cos(angle), np.sin(angle)
+    dft = np.stack(np_parts(np.block([[cos, -sin], [sin, cos]])))
     k1 = np.arange(RADIX)
     twist = TWO_PI * np.outer(k1, j) / LEN
     mode = k1[:, None] + RADIX * j[None, :]
@@ -63,33 +64,40 @@
 
 
 def crot(x, turns, sign):
+    turns = turns % 32
     if turns == 0:
         return x
+    if turns == 8:
+        return (x[1], -x[0]) if sign < 0 else (-x[1], x[0])
+    c = math.cos(TWO_PI * turns / 32)
+    s = sign * math.sin(TWO_PI * turns / 32)
     if turns == 4:
-        return (x[1], -x[0]) if sign < 0 else (-x[1], x[0])
-    c = math.cos(TWO_PI * turns / 16)
-    s = sign * math.sin(TWO_PI * turns / 16)
-    if turns == 2:
         return ((x[0] - sign * x[1]) * c, (x[1] + sign * x[0]) * c)
-    if turns == 6:
+    if turns == 12:
         return ((x[0] + sign * x[1]) * c, (x[1] - sign * x[0]) * c)
     return (x[0] * c - x[1] * s, x[0] * s + x[1] * c)
 
 
-def dft16(x, sign):
-    out = [None] * 16
+def dft8(x, sign):
+    even = dft4(x[0::2], sign)
+    odd = [crot(value, 4 * k, sign) for k, value in enumerate(dft4(x[1::2], sign))]
+    return [cadd(even[k], odd[k]) for k in range(4)] + [csub(even[k], odd[k]) for k in range(4)]
+
+
+def dft32(x, sign):
+    out = [None] * 32
     rows = []
-    for n2 in range(4):
-        y = dft4([x[4 * n1 + n2] for n1 in range(4)], sign)
+    for n2 in range(8):
+        y = dft4([x(8 * n1 + n2) for n1 in range(4)], sign)
         rows.append([crot(y[k1], n2 * k1, sign) for k1 in range(4)])
     for k1 in range(4):
-        z = dft4([rows[n2][k1] for n2 in range(4)], sign)
-        for k2 in range(4):
+        z = dft8([rows[n2][k1] for n2 in range(8)], sign)
+        for k2 in range(8):
             out[k1 + 4 * k2] = z[k2]
     return out
 
 
-def split(values):
+def product(values, table_ref):
     parts = []
     rest = values
     for step in range(PARTS):
@@ -97,59 +105,47 @@
         parts.append(part)
         if step < PARTS - 1:
             rest = rest - part.astype(jnp.float32)
-    return parts
-
-
-def product(parts, table, first):
-    total = None
-    for order in reversed(range(PARTS)):
-        for i in range(order + 1):
-            term = jnp.dot(
-                parts[i], table[first + order - i], preferred_element_type=jnp.float32
-            )
-            total = term if total is None else total + term
-    return total
+    order = [(i, k - i) for k in reversed(range(PARTS)) for i in range(k + 1)]
+    left = jnp.concatenate([parts[i] for i, _ in order], axis=1)
+    right = jnp.concatenate([table_ref[j] for _, j in order], axis=0)
+    return jnp.dot(left, right, preferred_element_type=jnp.float32)
 
 
 def transform(get, put, outputs, symbol, dft_ref, small_ref, a_ref, b_ref):
-    for lane in range(2):
-        lanes = slice(lane * 128, lane * 128 + 128)
-        planes = dft16([get(m, lanes) for m in range(RADIX)], -1)
+    re_lanes, im_lanes = slice(0, SUB), slice(SUB, 2 * SUB)
+    for half in range(2):
+        rows = slice(8 * half, 8 * half + 8)
+        planes = dft32(lambda m: get(m, half), -1)
         for k1 in range(RADIX):
             re, im = planes[k1]
             if k1:
-                c = small_ref[0, k1 : k1 + 1, lanes]
-                s = small_ref[1, k1 : k1 + 1, lanes]
+                c = small_ref[0, k1 : k1 + 1, :]
+                s = small_ref[1, k1 : k1 + 1, :]
                 re, im = re * c + im * s, im * c - re * s
-            a_ref[k1, 0:16, lanes] = re
-            a_ref[k1, 16:32, lanes] = im
-    rows = GROUP * 16
+            a_ref[k1, rows, re_lanes] = re
+            a_ref[k1, rows, im_lanes] = im
     for group in range(RADIX // GROUP):
         ks = slice(group * GROUP, (group + 1) * GROUP)
-        left = split(a_ref[ks].reshape(GROUP * 32, SUB))
-        with_cos = product(left, dft_ref, 0).reshape(GROUP, 2, 16, SUB)
-        with_sin = product(left, dft_ref, PARTS).reshape(GROUP, 2, 16, SUB)
-        re = with_cos[:, 0] + with_sin[:, 1]
-        im = with_cos[:, 1] - with_sin[:, 0]
+        got = product(a_ref[ks].reshape(GROUP * 16, 2 * SUB), dft_ref)
+        got = got.reshape(GROUP, 16, 2 * SUB)
+        re, im = got[:, :, re_lanes], got[:, :, im_lanes]
         for o in range(outputs):
-            sre, sim = symbol(o, ks, re, im)
-            left = split(jnp.concatenate([sre, sim], axis=1).reshape(GROUP * 32, SUB))
-            with_cos = product(left, dft_ref, 0).reshape(GROUP, 2, 16, SUB)
-            with_sin = product(left, dft_ref, PARTS).reshape(GROUP, 2, 16, SUB)
-            re2 = with_cos[:, 0] - with_sin[:, 1]
-            im2 = with_cos[:, 1] + with_sin[:, 0]
+            swapped = jnp.concatenate(symbol(o, ks, re, im)[::-1], axis=2)
+            got = product(swapped.reshape(GROUP * 16, 2 * SUB), dft_ref)
+            got = got.reshape(GROUP, 16, 2 * SUB)
+            im2, re2 = got[:, :, re_lanes], got[:, :, im_lanes]
             c = small_ref[0, ks][:, None, :]
             s = small_ref[1, ks][:, None, :]
-            b_ref[o, ks, 0:16] = re2 * c - im2 * s
-            b_ref[o, ks, 16:32] = im2 * c + re2 * s
-    for lane in range(2):
-        lanes = slice(lane * 128, lane * 128 + 128)
-        outs = []
-        for o in range(outputs):
-            planes = [(b_ref[o, k, 0:16, lanes], b_ref[o, k, 16:32, lanes]) for k in range(RADIX)]
-            outs.append(dft16(planes, 1))
+            b_ref[o, ks, :, re_lanes] = re2 * c - im2 * s
+            b_ref[o, ks, :, im_lanes] = im2 * c + re2 * s
+    for half in range(2):
+        rows = slice(8 * half, 8 * half + 8)
+        outs = [
+            dft32(lambda k: (b_ref[o, k, rows, re_lanes], b_ref[o, k, rows, im_lanes]), 1)
+            for o in range(outputs)
+        ]
         for m in range(RADIX):
-            put(m, lanes, [outs[o][m] for o in range(outputs)])
+            put(m, half, [outs[o][m] for o in range(outputs)])
 
 
 def space_symbol(scale, small_ref):
@@ -173,9 +169,16 @@
     return symbol
 
 
-def space_at(m, lanes):
-    start = (m % 2) * 256 + lanes.start
-    return m // 2, slice(start, start + 128)
+def row_parts(half):
+    return slice(8 * half, 8 * half + 8), slice(16 + 8 * half, 24 + 8 * half)
+
+
+def space_at(m):
+    return m // 4, slice((m % 4) * 128, (m % 4) * 128 + 128)
+
+
+def time_at(m):
+    return m // 2, slice((m % 2) * 128, (m % 2) * 128 + 128)
 
 
 def blocks4(tiles):
@@ -211,26 +214,24 @@
             for owner in range(16):
                 out_ref[owner * 8 + g, 8 * slot : 8 * slot + 8] = turned[owner]
 
-    def get_u(m, lanes):
-        g, cols = space_at(m, lanes)
-        return (u_ref[g, 0:16, cols], u_ref[g, 16:32, cols])
-
-    def put_u(m, lanes, values):
-        g, cols = space_at(m, lanes)
-        for half in range(2):
-            rows = slice(16 * half, 16 * half + 16)
-            p_ref[g, rows, cols] = values[0][half] + u_ref[g, rows, cols] * values[1][half]
-            v_ref[g, rows, cols] = values[1][half]
-
-    def get_p(m, lanes):
-        g, cols = space_at(m, lanes)
-        return (p_ref[g, 0:16, cols], p_ref[g, 16:32, cols])
-
-    def put_p(m, lanes, values):
-        g, cols = space_at(m, lanes)
-        for half in range(2):
-            rows = slice(16 * half, 16 * half + 16)
-            v_ref[g, rows, cols] = values[0][half] - u_ref[g, rows, cols] * values[1][half]
+    def get_u(m, half):
+        g, cols = space_at(m)
+        return tuple(u_ref[g, rows, cols] for rows in row_parts(half))
+
+    def put_u(m, half, values):
+        g, cols = space_at(m)
+        for part, rows in enumerate(row_parts(half)):
+            p_ref[g, rows, cols] = values[0][part] + u_ref[g, rows, cols] * values[1][part]
+            v_ref[g, rows, cols] = values[1][part]
+
+    def get_p(m, half):
+        g, cols = space_at(m)
+        return tuple(p_ref[g, rows, cols] for rows in row_parts(half))
+
+    def put_p(m, half, values):
+        g, cols = space_at(m)
+        for part, rows in enumerate(row_parts(half)):
+            v_ref[g, rows, cols] = values[0][part] - u_ref[g, rows, cols] * values[1][part]
 
     symbol = space_symbol(scale_ref[0], small_ref)
     transform(get_u, put_u, 2, symbol, dft_ref, small_ref, a_ref, b_ref)
@@ -240,13 +241,20 @@
     send(2, v_ref)
 
 
-def time_first_kernel(scale_ref, u_ref, dft_ref, small_ref, q_ref, a_ref, b_ref):
-    def get(m, lanes):
-        return (u_ref[m, 0:16, lanes], u_ref[m, 16:32, lanes])
-
-    def put(m, lanes, values):
-        q_ref[m, 0:16, lanes] = values[0][0]
-        q_ref[m, 16:32, lanes] = values[0][1]
+def time_first_kernel(
+    scale_ref, place_ref, moved_ref, dft_ref, small_ref, u_ref, q_ref, a_ref, b_ref
+):
+    for m in range(16):
+        u_ref[m] = moved_ref[(place_ref[0] + 4 - m // 4) % 4, (place_ref[1] + 4 - m % 4) % 4]
+
+    def get(m, half):
+        t, cols = time_at(m)
+        return tuple(u_ref[t, rows, cols] for rows in row_parts(half))
+
+    def put(m, half, values):
+        t, cols = time_at(m)
+        for part, rows in enumerate(row_parts(half)):
+            q_ref[t, rows, cols] = values[0][part]
 
     transform(get, put, 1, time_symbol(scale_ref[0], small_ref), dft_ref, small_ref, a_ref, b_ref)
 
@@ -272,34 +280,34 @@
                 cost = cost + r * r
                 g_ref[m, rows, cols] = tiles[2][a]
 
-    halves = (slice(0, 16), slice(16, 32))
-    norm = [jnp.zeros((16, 128), jnp.float32)]
-
-    def get_v(m, lanes):
-        return tuple(v_ref[m, rows, lanes] for rows in halves)
-
-    def put_v(m, lanes, values):
-        for half, rows in enumerate(halves):
-            g_ref[m, rows, lanes] = (
-                g_ref[m, rows, lanes] - u_ref[m, rows, lanes] * values[0][half]
-            )
-
-    def get_s(m, lanes):
-        return tuple(s_ref[m, rows, lanes] for rows in halves)
-
-    def put_s(m, lanes, values):
-        for half, rows in enumerate(halves):
-            g = g_ref[m, rows, lanes] - values[0][half]
-            out_ref[m, 32 + rows.start : 32 + rows.stop, lanes] = g
+    norm = [jnp.zeros((8, 128), jnp.float32)]
+
+    def get_v(m, half):
+        t, cols = time_at(m)
+        return tuple(v_ref[t, rows, cols] for rows in row_parts(half))
+
+    def put_v(m, half, values):
+        t, cols = time_at(m)
+        for part, rows in enumerate(row_parts(half)):
+            g_ref[t, rows, cols] = g_ref[t, rows, cols] - u_ref[t, rows, cols] * values[0][part]
+
+    def get_s(m, half):
+        t, cols = time_at(m)
+        return tuple(s_ref[t, rows, cols] for rows in row_parts(half))
+
+    def put_s(m, half, values):
+        t, cols = time_at(m)
+        for part, rows in enumerate(row_parts(half)):
+            g = g_ref[t, rows, cols] - values[0][part]
+            out_ref[t, 32 + rows.start : 32 + rows.stop, cols] = g
             norm[0] = norm[0] + g * g
 
     symbol = time_symbol(scale_ref[0], small_ref)
     transform(get_v, put_v, 1, symbol, dft_ref, small_ref, a_ref, b_ref)
     transform(get_s, put_s, 1, symbol, dft_ref, small_ref, a_ref, b_ref)
-    norm = norm[0][0:8] + norm[0][8:16]
     for m in range(16):
         out_ref[m, 64:72, 0:128] = 0.5 * cost
-        out_ref[m, 64:72, 128:256] = norm
+        out_ref[m, 64:72, 128:256] = norm[0]
 
 
 def sums_kernel(recv_ref, out_ref):
@@ -346,6 +354,32 @@
     )(*scalars, *arrays)
 
 
+def shift_pairs(axis, shift):
+    pairs = []
+    for y in range(4):
+        for x in range(4):
+            to = (y, (x + shift) % 4) if axis else ((y + shift) % 4, x)
+            pairs.append((4 * y + x, 4 * to[0] + to[1]))
+    return pairs
+
+
+def to_columns(turned):
+    here = lax.axis_index("ta")
+    y, x = here // 4, here % 4
+    pieces = turned.reshape(4, 4, 32, 256)
+    along_x = []
+    for d in range(4):
+        piece = lax.dynamic_index_in_dim(pieces, (x + d) % 4, 1, keepdims=False)
+        along_x.append(lax.ppermute(piece, "ta", shift_pairs(1, d)) if d else piece)
+    along_y = []
+    for e in range(4):
+        piece = jnp.stack(
+            [lax.dynamic_index_in_dim(part, (y + e) % 4, 0, keepdims=False) for part in along_x]
+        )
+        along_y.append(lax.ppermute(piece, "ta", shift_pairs(0, e)) if e else piece)
+    return jnp.stack(along_y), jnp.stack([y, x])
+
+
 def local(field, time_period, space_period):
     dft_np, small_np = np_tables()
     dft = jnp.asarray(dft_np)
@@ -354,13 +388,10 @@
     space_scale = TWO_PI / space_period
     every = ("ta", "gx")
     rows, cols = (8, 32, 512), (16, 32, 256)
-    planes = (RADIX, 32, SUB)
+    planes = (RADIX, 16, 2 * SUB)
 
     rows_u = lax.all_to_all(field.reshape(rows), "gx", 0, 0)
     turned = call(turn_kernel, f32(*cols), [], [field])
-    rows_u, turned = lax.optimization_barrier((rows_u, turned))
-    cols_u = lax.all_to_all(turned, "ta", 0, 0)
-
     pieces = call(
         space_kernel,
         f32(128, 24, 128),
@@ -369,12 +400,14 @@
         [rows, rows, planes, (2, *planes)],
         flops=8 * 10**9,
     )
+    pieces, turned = lax.optimization_barrier((pieces, turned))
     received = lax.all_to_all(pieces, every, 0, 0)
-    cols_q = call(
+    moved, place = to_columns(turned)
+    cols_u, cols_q = call(
         time_first_kernel,
-        f32(*cols),
-        [time_scale],
-        [cols_u, dft, small],
+        (f32(*cols), f32(*cols)),
+        [time_scale, place],
+        [moved, dft, small],
         [planes, (1, *planes)],
         flops=2 * 10**9,
     )

time: 132 us -> 124 us (0.939)
  waiting for transfers between devices: 58.2 us -> 47 us
  Pallas kernels: 20.6 us -> 14.6 us
  starting transfers between devices: 29.9 us -> 34.7 us
  local copies, waits for them, and re-layouts: 1.09 us -> 4.17 us
    all_to_all x1, waiting for transfers between devices: 39.1 us -> 10.4 us  [local(): received = lax.all_to_all(pieces, every, 0, 0)]
    ppermute x0 -> x6, waiting for transfers between devices: none -> 16.9 us  [the longest x3 10.8 us: to_columns(): along_x.append(lax.ppermute(piece, 'ta', shift_pairs(1, d)) if d else piece)]
    ppermute x0 -> x6, starting transfers between devices: none -> 11.5 us  [the longest x3 6.44 us: to_columns(): along_y.append(lax.ppermute(piece, 'ta', shift_pairs(0, e)) if e else piece)]
    all_to_all x1 -> x0, starting transfers between devices: 7.04 us -> none  [local(): cols_u = lax.all_to_all(turned, 'ta', 0, 0)]
    pallas_call x7, Pallas kernels: 20.6 us -> 14.6 us  [call(): pl.pallas_call(kernel, out_shape=outs, in_specs=[SM] * len(scalars) + [VM...]
    unnamed x8 -> x14, local copies, waits for them, and re-layouts: 1.09 us -> 4.08 us
  transfers between devices with their start and end apart: 4 -> 9, of which waited for: 4 -> 7; matrix products, arithmetic and copies ran while one was open for 0% -> 0% of each run, Pallas kernels for 11% -> 3%
where the time goes in v3:
time: 124 us; the launch traced here: 123 us
  waiting for transfers between devices  47 us (38%)
  starting transfers between devices  34.7 us (28%)
  blocking collectives  20.3 us (16%)
  Pallas kernels  14.6 us (12%)
  local copies, waits for them, and re-layouts  4.17 us (3%)
  between operations  2.23 us (2%)
    all_to_all x1, blocking collectives, local(): back = lax.all_to_all(cols_out, 'ta', 0, 0)  20.3 us
    pallas_call x7, Pallas kernels, call(): pl.pallas_call(kernel, out_shape=outs, in_specs=[SM] * len(scalars) + [VM...  14.6 us
    all_to_all x1, waiting for transfers between devices, local(): rows_u = lax.all_to_all(field.reshape(rows), 'gx', 0, 0)  14.1 us
    ppermute x3, waiting for transfers between devices, to_columns(): along_x.append(lax.ppermute(piece, 'ta', shift_pairs(1, d)) if d else piece)  10.8 us
    all_to_all x1, waiting for transfers between devices, local(): received = lax.all_to_all(pieces, every, 0, 0)  10.4 us
    all_to_all x1, starting transfers between devices, local(): received = lax.all_to_all(pieces, every, 0, 0)  9.73 us
    all_to_all x1, starting transfers between devices, local(): rows_u = lax.all_to_all(field.reshape(rows), 'gx', 0, 0)  8.71 us
    ppermute x3, starting transfers between devices, to_columns(): along_y.append(lax.ppermute(piece, 'ta', shift_pairs(0, e)) if e else piece)  6.44 us
  transfers between devices with their start and end apart: 9, of which 7 were waited for; matrix products, arithmetic and copies ran while one was open for 0% of the time, Pallas kernels for 3%

profile of v3, /device:TPU:32, one launch (start us, length us, event | category | flops | bytes accessed | tf_op | source)
XLA Modules:
  0.0 123.1 jit_solution(13815703077083126249)
XLA Ops:
  0.6 0.0 copy-start.4
  0.6 0.0 copy-start.3
  0.7 8.7 %all-to-all-start = ((f32[8,32,512]{2,1,0:T(8,128)}), f32[8,32,512]{2,1,0:T(8,128)S(1)}, u32[]{:S(2)}, u32[]{:S(2)}) async-start(f32[8,32,512]{2,1,0:T(8,128)} %bitcast.23), calls=%async_computation | async-start | bytes 1048576 | tf_op jit(solution)/shard_map/all_to_all | solution.py:393
  9.4 0.0 copy-start
  9.4 1.1 copy-done
  10.4 0.2 shard_map.69
  11.3 14.1 %all-to-all-done.u_ref = f32[8,32,512]{2,1,0:T(8,128)S(1)} async-done(((f32[8,32,512]{2,1,0:T(8,128)}), f32[8,32,512]{2,1,0:T(8,128)S(1)}, u32[]{:S(2)}, u32[]{:S(2)}) %all-to-all-start) | async-done | bytes 524320 | tf_op jit(solution)/shard_map/all_to_all | solution.py:393
  25.4 0.0 copy-done.4
  25.4 0.0 copy-done.3
  25.4 5.3 %shard_map.68 = f32[128,24,128]{2,1,0:T(8,128)S(1)} custom-call(f32[1]{0:T(128)S(6)} %div.18.scale_ref, f32[8,32,512]{2,1,0:T(8,128)S(1)} %all-to-all-done.u_ref, bf16[3,256,256]{2,1,0:T(8,128)(2,1)S(1)} %copy-done.3, f32[4,32,128]{2,1,0:T(8,128)S(1)} %copy-done.4), custom_call_target="tpu_custom_call" | custom-call | flops 8000000000 | bytes 2097152 | tf_op jit(solution)/shard_map/pallas_call | solution.py:346
  30.7 0.0 copy-start.2
  30.8 1.2 copy-done.2
  31.9 9.7 %all-to-all-start.1 = ((f32[128,24,128]{2,1,0:T(8,128)}), f32[128,24,128]{2,1,0:T(8,128)S(1)}, u32[]{:S(2)}, u32[]{:S(2)}) async-start(f32[128,24,128]{2,1,0:T(8,128)} %copy-done.2), calls=%async_computation.1 | async-start | bytes 3145728 | tf_op jit(solution)/shard_map/all_to_all | solution.py:404
  41.8 1.5 %collective-permute-start = (f32[4,32,256]{2,1,0:T(8,128)S(1)}, f32[4,32,256]{2,1,0:T(8,128)S(1)}, u32[]{:S(2)}, u32[]{:S(2)}) collective-permute-start(f32[4,32,256]{2,1,0:T(8,128)S(1)} %get-tuple-element.18), channel_id=1, source_target_pairs={{0,8},{8,16},{16,24},{24,0},{32,40},{40,48},{48,56},{56,32},{64,72... | collective-permute-start | bytes 393224 | tf_op jit(solution)/shard_map/ppermute | solution.py:373
  43.3 1.8 %collective-permute-start.2 = (f32[4,32,256]{2,1,0:T(8,128)S(1)}, f32[4,32,256]{2,1,0:T(8,128)S(1)}, u32[]{:S(2)}, u32[]{:S(2)}) collective-permute-start(f32[4,32,256]{2,1,0:T(8,128)S(1)} %get-tuple-element.19), channel_id=1, source_target_pairs={{0,24},{8,0},{16,8},{24,16},{32,56},{40,32},{48,40},{56,48},{64,88... | collective-permute-start | bytes 393224 | tf_op jit(solution)/shard_map/ppermute | solution.py:373
  45.1 1.8 %collective-permute-start.1 = (f32[4,32,256]{2,1,0:T(8,128)S(1)}, f32[4,32,256]{2,1,0:T(8,128)S(1)}, u32[]{:S(2)}, u32[]{:S(2)}) collective-permute-start(f32[4,32,256]{2,1,0:T(8,128)S(1)} %get-tuple-element.20), channel_id=1, source_target_pairs={{0,16},{8,24},{16,0},{24,8},{32,48},{40,56},{48,32},{56,40},{64,80... | collective-permute-start | bytes 393224 | tf_op jit(solution)/shard_map/ppermute | solution.py:373
  46.9 7.3 %collective-permute-done = f32[4,32,256]{2,1,0:T(8,128)S(1)} collective-permute-done((f32[4,32,256]{2,1,0:T(8,128)S(1)}, f32[4,32,256]{2,1,0:T(8,128)S(1)}, u32[]{:S(2)}, u32[]{:S(2)}) %collective-permute-start) | collective-permute-done | bytes 131104 | tf_op jit(solution)/shard_map/ppermute | solution.py:373
  54.1 0.0 collective-permute-done.2
  54.2 3.5 %collective-permute-done.1 = f32[4,32,256]{2,1,0:T(8,128)S(1)} collective-permute-done((f32[4,32,256]{2,1,0:T(8,128)S(1)}, f32[4,32,256]{2,1,0:T(8,128)S(1)}, u32[]{:S(2)}, u32[]{:S(2)}) %collective-permute-start.1) | collective-permute-done | bytes 131104 | tf_op jit(solution)/shard_map/ppermute | solution.py:373
  57.7 1.7 %collective-permute-start.3 = (f32[4,32,256]{2,1,0:T(8,128)S(1)}, f32[4,32,256]{2,1,0:T(8,128)S(1)}, u32[]{:S(2)}, u32[]{:S(2)}) collective-permute-start(f32[4,32,256]{2,1,0:T(8,128)S(1)} %pad_maximum_fusion.1), channel_id=1, source_target_pairs={{0,32},{8,40},{16,48},{24,56},{32,64},{40,72},{48,80},{56,88},{64,... | collective-permute-start | bytes 393224 | tf_op jit(solution)/shard_map/ppermute | solution.py:379
  59.5 3.2 %collective-permute-start.4 = (f32[4,32,256]{2,1,0:T(8,128)S(1)}, f32[4,32,256]{2,1,0:T(8,128)S(1)}, u32[]{:S(2)}, u32[]{:S(2)}) collective-permute-start(f32[4,32,256]{2,1,0:T(8,128)S(1)} %pad_maximum_fusion.2), channel_id=1, source_target_pairs={{0,64},{8,72},{16,80},{24,88},{32,96},{40,104},{48,112},{56,120},{... | collective-permute-start | bytes 393224 | tf_op jit(solution)/shard_map/ppermute | solution.py:379
  62.7 1.5 %collective-permute-start.5 = (f32[4,32,256]{2,1,0:T(8,128)S(1)}, f32[4,32,256]{2,1,0:T(8,128)S(1)}, u32[]{:S(2)}, u32[]{:S(2)}) collective-permute-start(f32[4,32,256]{2,1,0:T(8,128)S(1)} %pad_maximum_fusion.3), channel_id=1, source_target_pairs={{0,96},{8,104},{16,112},{24,120},{32,0},{40,8},{48,16},{56,24},{64... | collective-permute-start | bytes 393224 | tf_op jit(solution)/shard_map/ppermute | solution.py:379
  64.2 0.1 pad_add_fusion.place_ref
  65.0 2.0 %collective-permute-done.3 = f32[4,32,256]{2,1,0:T(8,128)S(1)} collective-permute-done((f32[4,32,256]{2,1,0:T(8,128)S(1)}, f32[4,32,256]{2,1,0:T(8,128)S(1)}, u32[]{:S(2)}, u32[]{:S(2)}) %collective-permute-start.3) | collective-permute-done | bytes 131104 | tf_op jit(solution)/shard_map/ppermute | solution.py:379
  67.0 4.1 %collective-permute-done.4 = f32[4,32,256]{2,1,0:T(8,128)S(1)} collective-permute-done((f32[4,32,256]{2,1,0:T(8,128)S(1)}, f32[4,32,256]{2,1,0:T(8,128)S(1)}, u32[]{:S(2)}, u32[]{:S(2)}) %collective-permute-start.4) | collective-permute-done | bytes 131104 | tf_op jit(solution)/shard_map/ppermute | solution.py:379
  71.1 0.0 collective-permute-done.5
  71.2 2.1 %shard_map.70 = (f32[16,32,256]{2,1,0:T(8,128)S(1)}, f32[16,32,256]{2,1,0:T(8,128)S(1)}) custom-call(f32[1]{0:T(128)S(6)} %div.14.scale_ref, s32[2]{0:T(128)S(1)} %pad_add_fusion.place_ref, f32[4,4,32,256]{3,2,1,0:T(8,128)S(1)} %pad_maximum_fusion.moved_ref, bf16[3,256,256]{2,1,0:T(8,128)(2,1)S(1)} %copy-done.3, f32[4,32,128]{2,1,0:T(8,128)S(1)} %copy-done.4), custom_call_target="tpu_custom_call" | custom-call | flops 2000000000 | bytes 2097152 | tf_op jit(solution)/shard_map/pallas_call | solution.py:346
  73.2 0.0 copy-start.5
  73.2 0.8 copy-done.5
  74.0 10.4 %all-to-all-done.1.recv_ref = f32[128,24,128]{2,1,0:T(8,128)S(1)} async-done(((f32[128,24,128]{2,1,0:T(8,128)}), f32[128,24,128]{2,1,0:T(8,128)S(1)}, u32[]{:S(2)}, u32[]{:S(2)}) %all-to-all-start.1) | async-done | bytes 1572896 | tf_op jit(solution)/shard_map/all_to_all | solution.py:404
  84.4 0.0 copy-start.6
  84.4 1.0 copy-done.6
  85.5 4.4 %shard_map.71 = f32[16,72,256]{2,1,0:T(8,128)S(1)} custom-call(f32[1]{0:T(128)S(6)} %div.14.scale_ref, f32[16,32,256]{2,1,0:T(8,128)S(1)} %get-tuple-element.9.u_ref, f32[16,32,256]{2,1,0:T(8,128)S(1)} %copy-done.6, f32[128,24,128]{2,1,0:T(8,128)S(1)} %all-to-all-done.1.recv_ref, bf16[3,256,256]{2,1,0:T(8,128)(2,1)S(1)} %copy-done.3, f32[4,32,128]{2,1,0:T(8,128)S(1)} %copy-done.4), custom_call_target="tpu_custom_call" | custom-call | flops 4000000000 | bytes 2097152 | tf_op jit(solution)/shard_map/pallas_call | solution.py:346
  89.9 20.3 %all_to_all.20.recv_ref = f32[16,72,256]{2,1,0:T(8,128)S(1)} all-to-all(f32[16,72,256]{2,1,0:T(8,128)S(1)} %shard_map.71), channel_id=1, replica_groups=mesh['tile'=2,'ta'=16,'gx'=8] {'ta'}, dimensions={0} | all-to-all | bytes 2359296 | tf_op jit(solution)/shard_map/all_to_all | solution.py:422
  110.1 0.0 copy-start.1
  110.1 0.6 shard_map.73
  110.8 4.7 %all-to-all-start.3 = ((f32[8,8,128]{2,1,0:T(8,128)}), f32[8,8,128]{2,1,0:T(8,128)S(1)}, u32[]{:S(2)}, u32[]{:S(2)}) async-start(f32[8,8,128]{2,1,0:T(8,128)} %shard_map.73), calls=%async_computation.3 | async-start | bytes 65536 | tf_op jit(solution)/shard_map/all_to_all | solution.py:424
  115.5 1.0 shard_map.72
  116.5 5.6 %all-to-all-done.3.sums_ref = f32[8,8,128]{2,1,0:T(8,128)S(1)} async-done(((f32[8,8,128]{2,1,0:T(8,128)}), f32[8,8,128]{2,1,0:T(8,128)S(1)}, u32[]{:S(2)}, u32[]{:S(2)}) %all-to-all-start.3) | async-done | bytes 32800 | tf_op jit(solution)/shard_map/all_to_all | solution.py:424
  122.1 0.0 copy-done.1
  122.1 1.0 shard_map.74
  (10 shorter events, 0.2 us)
Async XLA Ops:
  0.6 24.8 %copy-start.4 = (f32[4,32,128]{2,1,0:T(8,128)S(1)}, f32[4,32,128]{2,1,0:T(8,128)}, u32[]{:S(2)}) copy-start(f32[4,32,128]{2,1,0:T(8,128)} %constant.222.clone.small_ref) | copy-start | bytes 196612
  0.6 24.8 %copy-start.3 = (bf16[3,256,256]{2,1,0:T(8,128)(2,1)S(1)}, bf16[3,256,256]{2,1,0:T(8,128)(2,1)}, u32[]{:S(2)}) copy-start(bf16[3,256,256]{2,1,0:T(8,128)(2,1)} %constant.221.clone.dft_ref) | copy-start | bytes 1179652
  0.7 24.8 %all-to-all-start = ((f32[8,32,512]{2,1,0:T(8,128)}), f32[8,32,512]{2,1,0:T(8,128)S(1)}, u32[]{:S(2)}, u32[]{:S(2)}) async-start(f32[8,32,512]{2,1,0:T(8,128)} %bitcast.23), calls=%async_computation | async-start | bytes 1048576 | tf_op jit(solution)/shard_map/all_to_all | solution.py:393
  9.4 1.1 copy-start
  30.7 1.2 copy-start.2
  31.9 52.5 %all-to-all-start.1 = ((f32[128,24,128]{2,1,0:T(8,128)}), f32[128,24,128]{2,1,0:T(8,128)S(1)}, u32[]{:S(2)}, u32[]{:S(2)}) async-start(f32[128,24,128]{2,1,0:T(8,128)} %copy-done.2), calls=%async_computation.1 | async-start | bytes 3145728 | tf_op jit(solution)/shard_map/all_to_all | solution.py:404
  41.8 12.4 %collective-permute-start = (f32[4,32,256]{2,1,0:T(8,128)S(1)}, f32[4,32,256]{2,1,0:T(8,128)S(1)}, u32[]{:S(2)}, u32[]{:S(2)}) collective-permute-start(f32[4,32,256]{2,1,0:T(8,128)S(1)} %get-tuple-element.18), channel_id=1, source_target_pairs={{0,8},{8,16},{16,24},{24,0},{32,40},{40,48},{48,56},{56,32},{64,72... | collective-permute-start | bytes 393224 | tf_op jit(solution)/shard_map/ppermute | solution.py:373
  43.3 10.8 %collective-permute-start.2 = (f32[4,32,256]{2,1,0:T(8,128)S(1)}, f32[4,32,256]{2,1,0:T(8,128)S(1)}, u32[]{:S(2)}, u32[]{:S(2)}) collective-permute-start(f32[4,32,256]{2,1,0:T(8,128)S(1)} %get-tuple-element.19), channel_id=1, source_target_pairs={{0,24},{8,0},{16,8},{24,16},{32,56},{40,32},{48,40},{56,48},{64,88... | collective-permute-start | bytes 393224 | tf_op jit(solution)/shard_map/ppermute | solution.py:373
  45.1 12.6 %collective-permute-start.1 = (f32[4,32,256]{2,1,0:T(8,128)S(1)}, f32[4,32,256]{2,1,0:T(8,128)S(1)}, u32[]{:S(2)}, u32[]{:S(2)}) collective-permute-start(f32[4,32,256]{2,1,0:T(8,128)S(1)} %get-tuple-element.20), channel_id=1, source_target_pairs={{0,16},{8,24},{16,0},{24,8},{32,48},{40,56},{48,32},{56,40},{64,80... | collective-permute-start | bytes 393224 | tf_op jit(solution)/shard_map/ppermute | solution.py:373
  57.7 9.3 %collective-permute-start.3 = (f32[4,32,256]{2,1,0:T(8,128)S(1)}, f32[4,32,256]{2,1,0:T(8,128)S(1)}, u32[]{:S(2)}, u32[]{:S(2)}) collective-permute-start(f32[4,32,256]{2,1,0:T(8,128)S(1)} %pad_maximum_fusion.1), channel_id=1, source_target_pairs={{0,32},{8,40},{16,48},{24,56},{32,64},{40,72},{48,80},{56,88},{64,... | collective-permute-start | bytes 393224 | tf_op jit(solution)/shard_map/ppermute | solution.py:379
  59.5 11.6 %collective-permute-start.4 = (f32[4,32,256]{2,1,0:T(8,128)S(1)}, f32[4,32,256]{2,1,0:T(8,128)S(1)}, u32[]{:S(2)}, u32[]{:S(2)}) collective-permute-start(f32[4,32,256]{2,1,0:T(8,128)S(1)} %pad_maximum_fusion.2), channel_id=1, source_target_pairs={{0,64},{8,72},{16,80},{24,88},{32,96},{40,104},{48,112},{56,120},{... | collective-permute-start | bytes 393224 | tf_op jit(solution)/shard_map/ppermute | solution.py:379
  62.7 8.4 %collective-permute-start.5 = (f32[4,32,256]{2,1,0:T(8,128)S(1)}, f32[4,32,256]{2,1,0:T(8,128)S(1)}, u32[]{:S(2)}, u32[]{:S(2)}) collective-permute-start(f32[4,32,256]{2,1,0:T(8,128)S(1)} %pad_maximum_fusion.3), channel_id=1, source_target_pairs={{0,96},{8,104},{16,112},{24,120},{32,0},{40,8},{48,16},{56,24},{64... | collective-permute-start | bytes 393224 | tf_op jit(solution)/shard_map/ppermute | solution.py:379
  73.2 0.8 copy-start.5
  84.4 1.0 copy-start.6
  110.1 11.9 %copy-start.1 = (f32[256,512]{1,0:T(8,128)S(1)}, f32[256,512]{1,0:T(8,128)}, u32[]{:S(2)}) copy-start(f32[256,512]{1,0:T(8,128)} %u_ref.3) | copy-start | bytes 1572868
  110.8 11.3 %all-to-all-start.3 = ((f32[8,8,128]{2,1,0:T(8,128)}), f32[8,8,128]{2,1,0:T(8,128)S(1)}, u32[]{:S(2)}, u32[]{:S(2)}) async-start(f32[8,8,128]{2,1,0:T(8,128)} %shard_map.73), calls=%async_computation.3 | async-start | bytes 65536 | tf_op jit(solution)/shard_map/all_to_all | solution.py:424

commit v4 on v3

--- a/solution.py
+++ b/solution.py
@@ -206,23 +206,38 @@
             out_ref[:, a * 8 : a * 8 + 8, h * 128 : h * 128 + 128] = tile.reshape(16, 8, 128)
 
 
-def space_kernel(scale_ref, u_ref, dft_ref, small_ref, out_ref, p_ref, v_ref, a_ref, b_ref):
-    def send(slot, ref):
+def space_kernel(
+    scale_ref,
+    place_ref,
+    u_ref,
+    dft_ref,
+    small_ref,
+    out_ref,
+    *rest,
+):
+    p_outs = rest[:8]
+    cost_ref, p_ref, v_ref, v_send, g_send, a_ref, b_ref, sems, p_sems = rest[8:]
+
+    def pack(ref, send_ref):
         for g in range(8):
             stack = jnp.concatenate([ref[g, :, a * 128 : a * 128 + 128] for a in range(4)], axis=0)
             turned = stack.T.reshape(16, 8, 128)
             for owner in range(16):
-                out_ref[owner * 8 + g, 8 * slot : 8 * slot + 8] = turned[owner]
+                send_ref[owner * 8 + g] = turned[owner]
 
     def get_u(m, half):
         g, cols = space_at(m)
         return tuple(u_ref[g, rows, cols] for rows in row_parts(half))
 
+    cost = [jnp.zeros((8, 128), jnp.float32)]
+
     def put_u(m, half, values):
         g, cols = space_at(m)
         for part, rows in enumerate(row_parts(half)):
-            p_ref[g, rows, cols] = values[0][part] + u_ref[g, rows, cols] * values[1][part]
+            p = values[0][part] + u_ref[g, rows, cols] * values[1][part]
+            p_ref[g, rows, cols] = p
             v_ref[g, rows, cols] = values[1][part]
+            cost[0] = cost[0] + p * p
 
     def get_p(m, half):
         g, cols = space_at(m)
@@ -235,14 +250,25 @@
 
     symbol = space_symbol(scale_ref[0], small_ref)
     transform(get_u, put_u, 2, symbol, dft_ref, small_ref, a_ref, b_ref)
-    send(0, v_ref)
-    send(1, p_ref)
+    cost_ref[...] = cost[0]
+    copies = []
+    for d in range(8):
+        plane = (place_ref[0] + d) % 8
+        copies.append(pltpu.make_async_copy(p_ref.at[plane], p_outs[d], p_sems.at[d]))
+        copies[-1].start()
+    pack(v_ref, v_send)
+    copies.append(pltpu.make_async_copy(v_send, out_ref.at[:, 0:8, :], sems.at[0]))
+    copies[-1].start()
     transform(get_p, put_p, 2, symbol, dft_ref, small_ref, a_ref, b_ref)
-    send(2, v_ref)
+    pack(v_ref, g_send)
+    copies.append(pltpu.make_async_copy(g_send, out_ref.at[:, 8:16, :], sems.at[1]))
+    copies[-1].start()
+    for copy in copies:
+        copy.wait()
 
 
 def time_first_kernel(
-    scale_ref, place_ref, moved_ref, dft_ref, small_ref, u_ref, q_ref, a_ref, b_ref
+    scale_ref, place_ref, moved_ref, dft_ref, small_ref, u_ref, q_out, q_ref, a_ref, b_ref, sems
 ):
     for m in range(16):
         u_ref[m] = moved_ref[(place_ref[0] + 4 - m // 4) % 4, (place_ref[1] + 4 - m % 4) % 4]
@@ -257,30 +283,38 @@
             q_ref[t, rows, cols] = values[0][part]
 
     transform(get, put, 1, time_symbol(scale_ref[0], small_ref), dft_ref, small_ref, a_ref, b_ref)
+    copy = pltpu.make_async_copy(q_ref, q_out, sems.at[0])
+    copy.start()
+    copy.wait()
 
 
 def time_second_kernel(
-    scale_ref, u_ref, q_ref, recv_ref, dft_ref, small_ref, out_ref, v_ref, s_ref, g_ref, a_ref, b_ref
+    scale_ref,
+    u_ref,
+    q_in,
+    recv_ref,
+    cost_ref,
+    dft_ref,
+    small_ref,
+    out_ref,
+    q_ref,
+    v_ref,
+    s_ref,
+    g_ref,
+    sums_ref,
+    a_ref,
+    b_ref,
+    sems,
 ):
-    cost = jnp.zeros((8, 128), jnp.float32)
+    q_copy = pltpu.make_async_copy(q_in, q_ref, sems.at[0])
+    q_copy.start()
     for m in range(16):
         for h in range(2):
             cols = slice(h * 128, h * 128 + 128)
-            tiles = [
-                blocks4([recv_ref[m * 8 + 4 * h + k, 8 * o : 8 * o + 8] for k in range(4)])
-                for o in range(3)
-            ]
-            for a in range(4):
-                rows = slice(8 * a, 8 * a + 8)
-                q = q_ref[m, rows, cols]
-                v_ref[m, rows, cols] = tiles[0][a]
-                s_ref[m, rows, cols] = q + u_ref[m, rows, cols] * tiles[0][a]
-                r = q + tiles[1][a]
-                out_ref[m, rows, cols] = r
-                cost = cost + r * r
-                g_ref[m, rows, cols] = tiles[2][a]
-
-    norm = [jnp.zeros((8, 128), jnp.float32)]
+            for o, ref in enumerate((v_ref, g_ref)):
+                tiles = blocks4([recv_ref[m * 8 + 4 * h + k, 8 * o : 8 * o + 8] for k in range(4)])
+                for a in range(4):
+                    ref[m, 8 * a : 8 * a + 8, cols] = tiles[a]
 
     def get_v(m, half):
         t, cols = time_at(m)
@@ -291,6 +325,24 @@
         for part, rows in enumerate(row_parts(half)):
             g_ref[t, rows, cols] = g_ref[t, rows, cols] - u_ref[t, rows, cols] * values[0][part]
 
+    symbol = time_symbol(scale_ref[0], small_ref)
+    transform(get_v, put_v, 1, symbol, dft_ref, small_ref, a_ref, b_ref)
+
+    q_copy.wait()
+    q_back = pltpu.make_async_copy(q_ref, out_ref.at[:, 0:32, :], sems.at[1])
+    q_back.start()
+    cost = 0.5 * cost_ref[...]
+    for m in range(16):
+        for h in range(2):
+            cols = slice(h * 128, h * 128 + 128)
+            for a in range(4):
+                rows = slice(8 * a, 8 * a + 8)
+                q = q_ref[m, rows, cols]
+                w = u_ref[m, rows, cols] * v_ref[m, rows, cols]
+                s_ref[m, rows, cols] = q + w
+                cost = cost + q * (0.5 * q + w)
+    norm = [jnp.zeros((8, 128), jnp.float32)]
+
     def get_s(m, half):
         t, cols = time_at(m)
         return tuple(s_ref[t, rows, cols] for rows in row_parts(half))
@@ -299,32 +351,48 @@
         t, cols = time_at(m)
         for part, rows in enumerate(row_parts(half)):
             g = g_ref[t, rows, cols] - values[0][part]
-            out_ref[t, 32 + rows.start : 32 + rows.stop, cols] = g
+            g_ref[t, rows, cols] = g
             norm[0] = norm[0] + g * g
 
-    symbol = time_symbol(scale_ref[0], small_ref)
-    transform(get_v, put_v, 1, symbol, dft_ref, small_ref, a_ref, b_ref)
     transform(get_s, put_s, 1, symbol, dft_ref, small_ref, a_ref, b_ref)
+    g_back = pltpu.make_async_copy(g_ref, out_ref.at[:, 32:64, :], sems.at[2])
+    g_back.start()
     for m in range(16):
-        out_ref[m, 64:72, 0:128] = 0.5 * cost
-        out_ref[m, 64:72, 128:256] = norm[0]
+        sums_ref[m, :, 0:128] = cost
+        sums_ref[m, :, 128:256] = norm[0]
+    sums_back = pltpu.make_async_copy(sums_ref, out_ref.at[:, 64:72, :], sems.at[3])
+    sums_back.start()
+    q_back.wait()
+    g_back.wait()
+    sums_back.wait()
 
 
 def sums_kernel(recv_ref, out_ref):
-    total = jnp.sum(recv_ref[:, 64:72, :], axis=0)
+    total = jnp.sum(recv_ref[...], axis=0)
     cost = jnp.sum(total[:, 0:128], axis=0, keepdims=True)
     norm = jnp.sum(total[:, 128:256], axis=0, keepdims=True)
     row = lax.broadcasted_iota(jnp.int32, (8, 128), 0)
     out_ref[...] = jnp.broadcast_to(jnp.where(row == 0, cost, norm)[None], (8, 8, 128))
 
 
-def unturn_kernel(recv_ref, r_ref, g_ref):
-    for o, ref in enumerate((r_ref, g_ref)):
-        for h in range(2):
-            for a in range(4):
-                first = 32 * o + 8 * a
-                tile = recv_ref[:, first : first + 8, h * 128 : h * 128 + 128]
-                ref[h * 128 : h * 128 + 128, a * 128 : a * 128 + 128] = tile.reshape(128, 128).T
+def unturn(recv_ref, first, ref):
+    for h in range(2):
+        for a in range(4):
+            rows = slice(first + 8 * a, first + 8 * a + 8)
+            tile = recv_ref[:, rows, h * 128 : h * 128 + 128]
+            ref[h * 128 : h * 128 + 128, a * 128 : a * 128 + 128] = tile.reshape(128, 128).T
+
+
+def unturn_kernel(recv_ref, q_ref, g_ref):
+    unturn(recv_ref, 0, q_ref)
+    unturn(recv_ref, 32, g_ref)
+
+
+def residual_kernel(place_ref, q_ref, *refs):
+    r_ref = refs[8]
+    for d in range(8):
+        rows = pl.ds(pl.multiple_of((place_ref[0] + 8 - d) % 8 * 32, 32), 32)
+        r_ref[rows, :] = q_ref[rows, :] + refs[d][...]
 
 
 def update_kernel(u_ref, g_ref, sums_ref, out_ref):
@@ -336,22 +404,24 @@
 
 VM = pl.BlockSpec(memory_space=pltpu.VMEM)
 SM = pl.BlockSpec(memory_space=pltpu.SMEM)
+HB = pl.BlockSpec(memory_space=pl.ANY)
 
 
 def f32(*shape):
     return jax.ShapeDtypeStruct(shape, jnp.float32)
 
 
-def call(kernel, outs, scalars, arrays, scratch=(), flops=0):
+def call(kernel, outs, ins, scratch=(), sems=(), flops=0):
     return pl.pallas_call(
         kernel,
-        out_shape=outs,
-        in_specs=[SM] * len(scalars) + [VM] * len(arrays),
-        out_specs=jax.tree.map(lambda _: VM, outs),
-        scratch_shapes=[pltpu.VMEM(shape, jnp.float32) for shape in scratch],
+        out_shape=[f32(*shape) for shape, _ in outs],
+        in_specs=[spec for _, spec in ins],
+        out_specs=[spec for _, spec in outs],
+        scratch_shapes=[pltpu.VMEM(shape, jnp.float32) for shape in scratch]
+        + [pltpu.SemaphoreType.DMA((count,)) for count in sems],
         cost_estimate=pl.CostEstimate(flops=flops, bytes_accessed=2**21, transcendentals=0),
         compiler_params=pltpu.CompilerParams(vmem_limit_bytes=VMEM_LIMIT),
-    )(*scalars, *arrays)
+    )(*[array for array, _ in ins])
 
 
 def shift_pairs(axis, shift):
@@ -363,67 +433,86 @@
     return pairs
 
 
-def to_columns(turned):
+def along_x(turned, x):
+    pieces = turned.reshape(4, 4, 32, 256)
+    moved = []
+    for d in range(4):
+        piece = lax.dynamic_index_in_dim(pieces, (x + d) % 4, 1, keepdims=False)
+        moved.append(lax.ppermute(piece, "ta", shift_pairs(1, d)) if d else piece)
+    return moved
+
+
+def along_y(pieces, y):
+    moved = []
+    for e in range(4):
+        piece = jnp.stack(
+            [lax.dynamic_index_in_dim(part, (y + e) % 4, 0, keepdims=False) for part in pieces]
+        )
+        moved.append(lax.ppermute(piece, "ta", shift_pairs(0, e)) if e else piece)
+    return jnp.stack(moved)
+
+
+def local(field, time_period, space_period):
+    dft_np, small_np = np_tables()
+    dft = (jnp.asarray(dft_np), VM)
+    small = (jnp.asarray(small_np), VM)
+    time_scale = (TWO_PI / time_period, SM)
+    space_scale = (TWO_PI / space_period, SM)
+    rows, cols = (8, 32, 512), (16, 32, 256)
+    planes = (RADIX, 16, 2 * SUB)
     here = lax.axis_index("ta")
     y, x = here // 4, here % 4
-    pieces = turned.reshape(4, 4, 32, 256)
-    along_x = []
-    for d in range(4):
-        piece = lax.dynamic_index_in_dim(pieces, (x + d) % 4, 1, keepdims=False)
-        along_x.append(lax.ppermute(piece, "ta", shift_pairs(1, d)) if d else piece)
-    along_y = []
-    for e in range(4):
-        piece = jnp.stack(
-            [lax.dynamic_index_in_dim(part, (y + e) % 4, 0, keepdims=False) for part in along_x]
-        )
-        along_y.append(lax.ppermute(piece, "ta", shift_pairs(0, e)) if e else piece)
-    return jnp.stack(along_y), jnp.stack([y, x])
-
-
-def local(field, time_period, space_period):
-    dft_np, small_np = np_tables()
-    dft = jnp.asarray(dft_np)
-    small = jnp.asarray(small_np)
-    time_scale = TWO_PI / time_period
-    space_scale = TWO_PI / space_period
-    every = ("ta", "gx")
-    rows, cols = (8, 32, 512), (16, 32, 256)
-    planes = (RADIX, 16, 2 * SUB)
+    z = lax.axis_index("gx")
+    z_place = (z.reshape(1), SM)
+    t_place = (jnp.stack([y, x]), SM)
 
     rows_u = lax.all_to_all(field.reshape(rows), "gx", 0, 0)
-    turned = call(turn_kernel, f32(*cols), [], [field])
-    pieces = call(
+    (turned,) = call(turn_kernel, [(cols, VM)], [(field, VM)])
+    first_move = along_x(turned, x)
+    pieces, *p_planes, p_cost = call(
         space_kernel,
-        f32(128, 24, 128),
-        [space_scale],
-        [rows_u, dft, small],
-        [rows, rows, planes, (2, *planes)],
+        [((128, 16, 128), HB)] + [((32, 512), HB)] * 8 + [((8, 128), VM)],
+        [space_scale, z_place, (rows_u, VM), dft, small],
+        [rows, rows, (128, 8, 128), (128, 8, 128), planes, (2, *planes)],
+        [2, 8],
         flops=8 * 10**9,
     )
-    pieces, turned = lax.optimization_barrier((pieces, turned))
-    received = lax.all_to_all(pieces, every, 0, 0)
-    moved, place = to_columns(turned)
+    pieces, first_move = lax.optimization_barrier((pieces, first_move))
+    received = lax.all_to_all(pieces, ("ta", "gx"), 0, 0)
+    moved = along_y(first_move, y)
     cols_u, cols_q = call(
         time_first_kernel,
-        (f32(*cols), f32(*cols)),
-        [time_scale, place],
-        [moved, dft, small],
-        [planes, (1, *planes)],
+        [(cols, VM), (cols, HB)],
+        [time_scale, t_place, (moved, VM), dft, small],
+        [cols, planes, (1, *planes)],
+        [1],
         flops=2 * 10**9,
     )
-    cols_out = call(
+    (cols_out,) = call(
         time_second_kernel,
-        f32(16, 72, 256),
-        [time_scale],
-        [cols_u, cols_q, received, dft, small],
-        [cols, cols, cols, planes, (1, *planes)],
+        [((16, 72, 256), HB)],
+        [time_scale, (cols_u, VM), (cols_q, HB), (received, VM), (p_cost, VM), dft, small],
+        [cols, cols, cols, cols, (16, 8, 256), planes, (1, *planes)],
+        [4],
         flops=4 * 10**9,
     )
+    cols_out, p_planes = lax.optimization_barrier((cols_out, p_planes))
     back = lax.all_to_all(cols_out, "ta", 0, 0)
-    sums = call(sums_kernel, f32(8, 8, 128), [], [back])
+    p_block = [
+        lax.ppermute(plane, "gx", [(i, (i + d) % 8) for i in range(8)]) if d else plane
+        for d, plane in enumerate(p_planes)
+    ]
+    (sums,) = call(sums_kernel, [((8, 8, 128), VM)], [(back[:, 64:72, :], VM)])
     sums = lax.all_to_all(sums, "gx", 0, 0)
-    residual, gradient = call(unturn_kernel, (f32(256, 512), f32(256, 512)), [], [back])
-    updated = call(update_kernel, f32(256, 512), [], [field, gradient, sums])
+    block_q, block_g = call(unturn_kernel, [((256, 512), VM), ((256, 512), VM)], [(back, VM)])
+    (residual,) = call(
+        residual_kernel,
+        [((256, 512), VM)],
+        [z_place, (block_q, VM)] + [(plane, VM) for plane in p_block],
+    )
+    (updated,) = call(
+        update_kernel, [((256, 512), VM)], [(field, VM), (block_g, VM), (sums, VM)]
+    )
     return updated, residual
 
 

time: 124 us -> 116 us (0.935)
  blocking collectives: 20.3 us -> 0 us
  starting transfers between devices: 34.7 us -> 50.4 us
  waiting for transfers between devices: 47 us -> 40.7 us
  Pallas kernels: 14.6 us -> 17.2 us
    all_to_all x1 -> x0, blocking collectives: 20.3 us -> none  [local(): back = lax.all_to_all(cols_out, 'ta', 0, 0)]
    ppermute x6 -> x13, starting transfers between devices: 11.5 us -> 23.7 us  [the longest x7 12.9 us: local(): lax.ppermute(plane, 'gx', [(i, (i + d) % 8) for i in range(8)])]
    ppermute x6 -> x13, waiting for transfers between devices: 16.9 us -> 8.32 us  [the longest x3 8.3 us: along_y(): moved.append(lax.ppermute(piece, 'ta', shift_pairs(0, e)) if e else piece)]
    all_to_all x1 -> x2, waiting for transfers between devices: 10.4 us -> 17 us  [the longest x1 12.1 us: local(): received = lax.all_to_all(pieces, ('ta', 'gx'), 0, 0)]
    all_to_all x1, waiting for transfers between devices: 14.1 us -> 9.96 us  [local(): rows_u = lax.all_to_all(field.reshape(rows), 'gx', 0, 0)]
    all_to_all x1 -> x2, starting transfers between devices: 9.73 us -> 13.5 us  [the longest x1 9.74 us: local(): received = lax.all_to_all(pieces, ('ta', 'gx'), 0, 0)]
    pallas_call x7 -> x8, Pallas kernels: 14.6 us -> 17.2 us  [call(): pl.pallas_call(kernel, out_shape=[f32(*shape) for shape, _ in outs], in_s...]
  transfers between devices with their start and end apart: 9 -> 17, of which waited for: 7 -> 6; matrix products, arithmetic and copies ran while one was open for 0% -> 1% of each run, Pallas kernels for 3% -> 10%
where the time goes in v4:
time: 116 us; the launch traced here: 115 us
  starting transfers between devices  50.4 us (43%)
  waiting for transfers between devices  40.7 us (35%)
  Pallas kernels  17.2 us (15%)
  local copies, waits for them, and re-layouts  4.45 us (4%)
  between operations  2.34 us (2%)
    pallas_call x8, Pallas kernels, call(): pl.pallas_call(kernel, out_shape=[f32(*shape) for shape, _ in outs], in_s...  17.2 us
    ppermute x7, starting transfers between devices, local(): lax.ppermute(plane, 'gx', [(i, (i + d) % 8) for i in range(8)])  12.9 us
    all_to_all x1, waiting for transfers between devices, local(): received = lax.all_to_all(pieces, ('ta', 'gx'), 0, 0)  12.1 us
    all_to_all x1, waiting for transfers between devices, local(): rows_u = lax.all_to_all(field.reshape(rows), 'gx', 0, 0)  9.96 us
    all_to_all x1, starting transfers between devices, local(): received = lax.all_to_all(pieces, ('ta', 'gx'), 0, 0)  9.74 us
    all_to_all x1, starting transfers between devices, local(): rows_u = lax.all_to_all(field.reshape(rows), 'gx', 0, 0)  8.71 us
    ppermute x3, waiting for transfers between devices, along_y(): moved.append(lax.ppermute(piece, 'ta', shift_pairs(0, e)) if e else piece)  8.3 us
    ppermute x3, starting transfers between devices, along_y(): moved.append(lax.ppermute(piece, 'ta', shift_pairs(0, e)) if e else piece)  6.34 us
  transfers between devices with their start and end apart: 17, of which 6 were waited for; matrix products, arithmetic and copies ran while one was open for 1% of the time, Pallas kernels for 10%

profile of v4, /device:TPU:32, one launch (start us, length us, event | category | flops | bytes accessed | tf_op | source)
XLA Modules:
  0.0 115.2 jit_solution(8384816439042494245)
XLA Ops:
  0.6 8.7 %all-to-all-start = ((f32[8,32,512]{2,1,0:T(8,128)}), f32[8,32,512]{2,1,0:T(8,128)S(1)}, u32[]{:S(2)}, u32[]{:S(2)}) async-start(f32[8,32,512]{2,1,0:T(8,128)} %bitcast.26), calls=%async_computation | async-start | bytes 1048576 | tf_op jit(solution)/shard_map/all_to_all | solution.py:469
  9.4 0.2 shard_map.69
  9.6 0.7 dynamic-slice_bitcast_fusion
  10.3 2.8 %collective-permute-start.2 = (f32[4,32,256]{2,1,0:T(8,128)}, f32[4,32,256]{2,1,0:T(8,128)S(1)}, u32[]{:S(2)}, u32[]{:S(2)}) collective-permute-start(f32[4,32,256]{2,1,0:T(8,128)} %get-tuple-element.58), channel_id=1, source_target_pairs={{0,24},{8,0},{16,8},{24,16},{32,56},{40,32},{48,40},{56,48},{64,88... | collective-permute-start | bytes 393224 | tf_op jit(solution)/shard_map/ppermute | solution.py:441
  13.0 0.8 collective-permute-start.1
  13.8 0.9 collective-permute-start
  15.4 10.0 %all-to-all-done.u_ref = f32[8,32,512]{2,1,0:T(8,128)S(1)} async-done(((f32[8,32,512]{2,1,0:T(8,128)}), f32[8,32,512]{2,1,0:T(8,128)S(1)}, u32[]{:S(2)}, u32[]{:S(2)}) %all-to-all-start) | async-done | bytes 524320 | tf_op jit(solution)/shard_map/all_to_all | solution.py:469
  25.4 7.1 %shard_map.68 = (f32[128,16,128]{2,1,0:T(8,128)}, f32[32,512]{1,0:T(8,128)S(1)}, f32[32,512]{1,0:T(8,128)S(1)}, f32[32,512]{1,0:T(8,128)S(1)}, f32[32,512]{1,0:T...) custom-call(f32[1]{0:T(128)S(6)} %div.18.scale_ref, ...), custom_call_target="tpu_custom_call" | custom-call | flops 8000000000 | bytes 2097152 | tf_op jit(solution)/shard_map/pallas_call | solution.py:415
  32.5 0.0 collective-permute-done.2
  32.5 0.0 collective-permute-done.1
  32.5 0.0 collective-permute-done
  32.5 9.7 %all-to-all-start.1 = ((f32[128,16,128]{2,1,0:T(8,128)}), f32[128,16,128]{2,1,0:T(8,128)S(1)}, u32[]{:S(2)}, u32[]{:S(2)}) async-start(f32[128,16,128]{2,1,0:T(8,128)} %get-tuple-element.37), calls=%async_computation.1 | async-start | bytes 2097152 | tf_op jit(solution)/shard_map/all_to_all | solution.py:481
  42.5 1.6 %collective-permute-start.3 = (f32[4,32,256]{2,1,0:T(8,128)S(1)}, f32[4,32,256]{2,1,0:T(8,128)S(1)}, u32[]{:S(2)}, u32[]{:S(2)}) collective-permute-start(f32[4,32,256]{2,1,0:T(8,128)S(1)} %pad_maximum_fusion.1), channel_id=1, source_target_pairs={{0,32},{8,40},{16,48},{24,56},{32,64},{40,72},{48,80},{56,88},{64,... | collective-permute-start | bytes 393224 | tf_op jit(solution)/shard_map/ppermute | solution.py:451
  44.1 3.2 %collective-permute-start.4 = (f32[4,32,256]{2,1,0:T(8,128)S(1)}, f32[4,32,256]{2,1,0:T(8,128)S(1)}, u32[]{:S(2)}, u32[]{:S(2)}) collective-permute-start(f32[4,32,256]{2,1,0:T(8,128)S(1)} %pad_maximum_fusion.2), channel_id=1, source_target_pairs={{0,64},{8,72},{16,80},{24,88},{32,96},{40,104},{48,112},{56,120},{... | collective-permute-start | bytes 393224 | tf_op jit(solution)/shard_map/ppermute | solution.py:451
  47.4 1.5 %collective-permute-start.5 = (f32[4,32,256]{2,1,0:T(8,128)S(1)}, f32[4,32,256]{2,1,0:T(8,128)S(1)}, u32[]{:S(2)}, u32[]{:S(2)}) collective-permute-start(f32[4,32,256]{2,1,0:T(8,128)S(1)} %pad_maximum_fusion.3), channel_id=1, source_target_pairs={{0,96},{8,104},{16,112},{24,120},{32,0},{40,8},{48,16},{56,24},{64... | collective-permute-start | bytes 393224 | tf_op jit(solution)/shard_map/ppermute | solution.py:451
  48.9 0.1 pad_add_fusion.place_ref
  49.6 2.5 %collective-permute-done.3 = f32[4,32,256]{2,1,0:T(8,128)S(1)} collective-permute-done((f32[4,32,256]{2,1,0:T(8,128)S(1)}, f32[4,32,256]{2,1,0:T(8,128)S(1)}, u32[]{:S(2)}, u32[]{:S(2)}) %collective-permute-start.3) | collective-permute-done | bytes 131104 | tf_op jit(solution)/shard_map/ppermute | solution.py:451
  52.1 5.8 %collective-permute-done.4 = f32[4,32,256]{2,1,0:T(8,128)S(1)} collective-permute-done((f32[4,32,256]{2,1,0:T(8,128)S(1)}, f32[4,32,256]{2,1,0:T(8,128)S(1)}, u32[]{:S(2)}, u32[]{:S(2)}) %collective-permute-start.4) | collective-permute-done | bytes 131104 | tf_op jit(solution)/shard_map/ppermute | solution.py:451
  57.9 0.0 collective-permute-done.5
  58.0 2.1 %shard_map.70 = (f32[16,32,256]{2,1,0:T(8,128)S(1)}, f32[16,32,256]{2,1,0:T(8,128)S(1)}) custom-call(f32[1]{0:T(128)S(6)} %div.14.scale_ref, s32[2]{0:T(128)S(1)} %pad_add_fusion.place_ref, f32[4,4,32,256]{3,2,1,0:T(8,128)S(1)} %pad_maximum_fusion.moved_ref, bf16[3,256,256]{2,1,0:T(8,128)(2,1)S(1)} %copy-done.1, f32[4,32,128]{2,1,0:T(8,128)S(1)} %copy-done.2), custom_call_target="tpu_custom_call" | custom-call | flops 2000000000 | bytes 2097152 | tf_op jit(solution)/shard_map/pallas_call | solution.py:415
  60.1 0.0 copy-start.3
  60.1 0.8 copy-done.3
  60.9 0.8 copy-done.5
  61.7 12.1 %all-to-all-done.1.recv_ref = f32[128,16,128]{2,1,0:T(8,128)S(1)} async-done(((f32[128,16,128]{2,1,0:T(8,128)}), f32[128,16,128]{2,1,0:T(8,128)S(1)}, u32[]{:S(2)}, u32[]{:S(2)}) %all-to-all-start.1) | async-done | bytes 1048608 | tf_op jit(solution)/shard_map/all_to_all | solution.py:481
  73.8 1.0 copy-done.4
  74.9 1.0 copy-done.6
  75.9 4.9 %shard_map.71 = f32[16,72,256]{2,1,0:T(8,128)} custom-call(f32[1]{0:T(128)S(6)} %div.14.scale_ref, f32[16,32,256]{2,1,0:T(8,128)S(1)} %copy-done.4, f32[16,32,256]{2,1,0:T(8,128)S(1)} %copy-done.6, f32[128,16,128]{2,1,0:T(8,128)S(1)} %all-to-all-done.1.recv_ref, f32[8,128]{1,0:T(8,128)S(1)} %get-tuple-element.38.cost_ref, ...), custom_call_target="tpu_custom_call" | custom-call | flops 4000000000 | bytes 2097152 | tf_op jit(solution)/shard_map/pallas_call | solution.py:415
  80.9 3.7 %all-to-all-start.2 = ((f32[16,72,256]{2,1,0:T(8,128)}), f32[16,72,256]{2,1,0:T(8,128)S(1)}, u32[]{:S(2)}, u32[]{:S(2)}) async-start(f32[16,72,256]{2,1,0:T(8,128)} %shard_map.71), calls=%async_computation.2 | async-start | bytes 2359296 | tf_op jit(solution)/shard_map/all_to_all | solution.py:500
  84.6 0.1 collective-permute-start.6
  84.7 1.1 collective-permute-start.7
  85.8 1.8 %collective-permute-start.8 = (f32[32,512]{1,0:T(8,128)S(1)}, f32[32,512]{1,0:T(8,128)S(1)}, u32[]{:S(2)}, u32[]{:S(2)}) collective-permute-start(f32[32,512]{1,0:T(8,128)S(1)} %get-tuple-element.53), channel_id=1, source_target_pairs={{0,3},{1,4},{2,5},{3,6},{4,7},{5,0},{6,1},{7,2},{8,11},{9,12},{10,... | collective-permute-start | bytes 196616 | tf_op jit(solution)/shard_map/ppermute | solution.py:502
  87.6 3.7 %collective-permute-start.9 = (f32[32,512]{1,0:T(8,128)S(1)}, f32[32,512]{1,0:T(8,128)S(1)}, u32[]{:S(2)}, u32[]{:S(2)}) collective-permute-start(f32[32,512]{1,0:T(8,128)S(1)} %get-tuple-element.54), channel_id=1, source_target_pairs={{0,4},{1,5},{2,6},{3,7},{4,0},{5,1},{6,2},{7,3},{8,12},{9,13},{10,... | collective-permute-start | bytes 196616 | tf_op jit(solution)/shard_map/ppermute | solution.py:502
  91.3 4.9 %collective-permute-start.10 = (f32[32,512]{1,0:T(8,128)S(1)}, f32[32,512]{1,0:T(8,128)S(1)}, u32[]{:S(2)}, u32[]{:S(2)}) collective-permute-start(f32[32,512]{1,0:T(8,128)S(1)} %get-tuple-element.55), channel_id=1, source_target_pairs={{0,5},{1,6},{2,7},{3,0},{4,1},{5,2},{6,3},{7,4},{8,13},{9,14},{10,... | collective-permute-start | bytes 196616 | tf_op jit(solution)/shard_map/ppermute | solution.py:502
  96.2 0.0 collective-permute-done.6.refs_1_
  96.2 0.0 collective-permute-start.11
  96.2 0.0 collective-permute-done.7.refs_2_
  96.2 1.3 %collective-permute-start.12 = (f32[32,512]{1,0:T(8,128)S(1)}, f32[32,512]{1,0:T(8,128)S(1)}, u32[]{:S(2)}, u32[]{:S(2)}) collective-permute-start(f32[32,512]{1,0:T(8,128)S(1)} %get-tuple-element.57), channel_id=1, source_target_pairs={{0,7},{1,0},{2,1},{3,2},{4,3},{5,4},{6,5},{7,6},{8,15},{9,8},{10,9... | collective-permute-start | bytes 196616 | tf_op jit(solution)/shard_map/ppermute | solution.py:502
  97.5 4.9 %all-to-all-done.2.recv_ref = f32[16,72,256]{2,1,0:T(8,128)S(1)} async-done(((f32[16,72,256]{2,1,0:T(8,128)}), f32[16,72,256]{2,1,0:T(8,128)S(1)}, u32[]{:S(2)}, u32[]{:S(2)}) %all-to-all-start.2) | async-done | bytes 1179680 | tf_op jit(solution)/shard_map/all_to_all | solution.py:500
  102.4 0.6 shard_map.73
  103.1 4.5 %all-to-all-start.3 = ((f32[8,8,128]{2,1,0:T(8,128)}), f32[8,8,128]{2,1,0:T(8,128)S(1)}, u32[]{:S(2)}, u32[]{:S(2)}) async-start(f32[8,8,128]{2,1,0:T(8,128)} %shard_map.73), calls=%async_computation.3 | async-start | bytes 65536 | tf_op jit(solution)/shard_map/all_to_all | solution.py:506
  107.6 0.3 shard_map.72
  107.9 0.0 collective-permute-done.8.refs_3_
  107.9 0.0 collective-permute-done.9.refs_4_
  107.9 0.0 collective-permute-done.10.refs_5_
  108.0 0.0 collective-permute-done.11.refs_6_
  108.0 0.9 shard_map.75
  108.8 5.4 %all-to-all-done.3.sums_ref = f32[8,8,128]{2,1,0:T(8,128)S(1)} async-done(((f32[8,8,128]{2,1,0:T(8,128)}), f32[8,8,128]{2,1,0:T(8,128)S(1)}, u32[]{:S(2)}, u32[]{:S(2)}) %all-to-all-start.3) | async-done | bytes 32800 | tf_op jit(solution)/shard_map/all_to_all | solution.py:506
  114.2 1.0 shard_map.74
  (18 shorter events, 0.2 us)
Async XLA Ops:
  0.6 8.7 %copy-start = (f32[256,512]{1,0:T(8,128)S(1)}, f32[256,512]{1,0:T(8,128)}, u32[]{:S(2)}) copy-start(f32[256,512]{1,0:T(8,128)} %u_ref.3) | copy-start | bytes 1572868
  0.6 24.8 %all-to-all-start = ((f32[8,32,512]{2,1,0:T(8,128)}), f32[8,32,512]{2,1,0:T(8,128)S(1)}, u32[]{:S(2)}, u32[]{:S(2)}) async-start(f32[8,32,512]{2,1,0:T(8,128)} %bitcast.26), calls=%async_computation | async-start | bytes 1048576 | tf_op jit(solution)/shard_map/all_to_all | solution.py:469
  9.4 16.0 %copy-start.1 = (bf16[3,256,256]{2,1,0:T(8,128)(2,1)S(1)}, bf16[3,256,256]{2,1,0:T(8,128)(2,1)}, u32[]{:S(2)}) copy-start(bf16[3,256,256]{2,1,0:T(8,128)(2,1)} %constant.144.clone.dft_ref) | copy-start | bytes 1179652
  9.4 16.0 %copy-start.2 = (f32[4,32,128]{2,1,0:T(8,128)S(1)}, f32[4,32,128]{2,1,0:T(8,128)}, u32[]{:S(2)}) copy-start(f32[4,32,128]{2,1,0:T(8,128)} %constant.145.clone.small_ref) | copy-start | bytes 196612
  10.3 22.2 %collective-permute-start.2 = (f32[4,32,256]{2,1,0:T(8,128)}, f32[4,32,256]{2,1,0:T(8,128)S(1)}, u32[]{:S(2)}, u32[]{:S(2)}) collective-permute-start(f32[4,32,256]{2,1,0:T(8,128)} %get-tuple-element.58), channel_id=1, source_target_pairs={{0,24},{8,0},{16,8},{24,16},{32,56},{40,32},{48,40},{56,48},{64,88... | collective-permute-start | bytes 393224 | tf_op jit(solution)/shard_map/ppermute | solution.py:441
  13.0 19.5 %collective-permute-start.1 = (f32[4,32,256]{2,1,0:T(8,128)S(1)}, f32[4,32,256]{2,1,0:T(8,128)S(1)}, u32[]{:S(2)}, u32[]{:S(2)}) collective-permute-start(f32[4,32,256]{2,1,0:T(8,128)S(1)} %get-tuple-element.59), channel_id=1, source_target_pairs={{0,16},{8,24},{16,0},{24,8},{32,48},{40,56},{48,32},{56,40},{64,80... | collective-permute-start | bytes 393224 | tf_op jit(solution)/shard_map/ppermute | solution.py:441
  13.8 18.7 %collective-permute-start = (f32[4,32,256]{2,1,0:T(8,128)S(1)}, f32[4,32,256]{2,1,0:T(8,128)S(1)}, u32[]{:S(2)}, u32[]{:S(2)}) collective-permute-start(f32[4,32,256]{2,1,0:T(8,128)S(1)} %get-tuple-element.60), channel_id=1, source_target_pairs={{0,8},{8,16},{16,24},{24,0},{32,40},{40,48},{48,56},{56,32},{64,72... | collective-permute-start | bytes 393224 | tf_op jit(solution)/shard_map/ppermute | solution.py:441
  32.5 41.3 %all-to-all-start.1 = ((f32[128,16,128]{2,1,0:T(8,128)}), f32[128,16,128]{2,1,0:T(8,128)S(1)}, u32[]{:S(2)}, u32[]{:S(2)}) async-start(f32[128,16,128]{2,1,0:T(8,128)} %get-tuple-element.37), calls=%async_computation.1 | async-start | bytes 2097152 | tf_op jit(solution)/shard_map/all_to_all | solution.py:481
  42.5 9.6 %collective-permute-start.3 = (f32[4,32,256]{2,1,0:T(8,128)S(1)}, f32[4,32,256]{2,1,0:T(8,128)S(1)}, u32[]{:S(2)}, u32[]{:S(2)}) collective-permute-start(f32[4,32,256]{2,1,0:T(8,128)S(1)} %pad_maximum_fusion.1), channel_id=1, source_target_pairs={{0,32},{8,40},{16,48},{24,56},{32,64},{40,72},{48,80},{56,88},{64,... | collective-permute-start | bytes 393224 | tf_op jit(solution)/shard_map/ppermute | solution.py:451
  44.1 13.8 %collective-permute-start.4 = (f32[4,32,256]{2,1,0:T(8,128)S(1)}, f32[4,32,256]{2,1,0:T(8,128)S(1)}, u32[]{:S(2)}, u32[]{:S(2)}) collective-permute-start(f32[4,32,256]{2,1,0:T(8,128)S(1)} %pad_maximum_fusion.2), channel_id=1, source_target_pairs={{0,64},{8,72},{16,80},{24,88},{32,96},{40,104},{48,112},{56,120},{... | collective-permute-start | bytes 393224 | tf_op jit(solution)/shard_map/ppermute | solution.py:451
  47.4 10.6 %collective-permute-start.5 = (f32[4,32,256]{2,1,0:T(8,128)S(1)}, f32[4,32,256]{2,1,0:T(8,128)S(1)}, u32[]{:S(2)}, u32[]{:S(2)}) collective-permute-start(f32[4,32,256]{2,1,0:T(8,128)S(1)} %pad_maximum_fusion.3), channel_id=1, source_target_pairs={{0,96},{8,104},{16,112},{24,120},{32,0},{40,8},{48,16},{56,24},{64... | collective-permute-start | bytes 393224 | tf_op jit(solution)/shard_map/ppermute | solution.py:451
  60.1 0.8 copy-start.3
  60.9 0.8 copy-start.5
  73.8 1.0 copy-start.4
  74.9 1.0 copy-start.6
  80.9 21.5 %all-to-all-start.2 = ((f32[16,72,256]{2,1,0:T(8,128)}), f32[16,72,256]{2,1,0:T(8,128)S(1)}, u32[]{:S(2)}, u32[]{:S(2)}) async-start(f32[16,72,256]{2,1,0:T(8,128)} %shard_map.71), calls=%async_computation.2 | async-start | bytes 2359296 | tf_op jit(solution)/shard_map/all_to_all | solution.py:500
  84.6 11.6 %collective-permute-start.6 = (f32[32,512]{1,0:T(8,128)S(1)}, f32[32,512]{1,0:T(8,128)S(1)}, u32[]{:S(2)}, u32[]{:S(2)}) collective-permute-start(f32[32,512]{1,0:T(8,128)S(1)} %get-tuple-element.51), channel_id=1, source_target_pairs={{0,1},{1,2},{2,3},{3,4},{4,5},{5,6},{6,7},{7,0},{8,9},{9,10},{10,1... | collective-permute-start | bytes 196616 | tf_op jit(solution)/shard_map/ppermute | solution.py:502
  84.7 11.5 %collective-permute-start.7 = (f32[32,512]{1,0:T(8,128)S(1)}, f32[32,512]{1,0:T(8,128)S(1)}, u32[]{:S(2)}, u32[]{:S(2)}) collective-permute-start(f32[32,512]{1,0:T(8,128)S(1)} %get-tuple-element.52), channel_id=1, source_target_pairs={{0,2},{1,3},{2,4},{3,5},{4,6},{5,7},{6,0},{7,1},{8,10},{9,11},{10,... | collective-permute-start | bytes 196616 | tf_op jit(solution)/shard_map/ppermute | solution.py:502
  85.8 22.2 %collective-permute-start.8 = (f32[32,512]{1,0:T(8,128)S(1)}, f32[32,512]{1,0:T(8,128)S(1)}, u32[]{:S(2)}, u32[]{:S(2)}) collective-permute-start(f32[32,512]{1,0:T(8,128)S(1)} %get-tuple-element.53), channel_id=1, source_target_pairs={{0,3},{1,4},{2,5},{3,6},{4,7},{5,0},{6,1},{7,2},{8,11},{9,12},{10,... | collective-permute-start | bytes 196616 | tf_op jit(solution)/shard_map/ppermute | solution.py:502
  87.6 20.4 %collective-permute-start.9 = (f32[32,512]{1,0:T(8,128)S(1)}, f32[32,512]{1,0:T(8,128)S(1)}, u32[]{:S(2)}, u32[]{:S(2)}) collective-permute-start(f32[32,512]{1,0:T(8,128)S(1)} %get-tuple-element.54), channel_id=1, source_target_pairs={{0,4},{1,5},{2,6},{3,7},{4,0},{5,1},{6,2},{7,3},{8,12},{9,13},{10,... | collective-permute-start | bytes 196616 | tf_op jit(solution)/shard_map/ppermute | solution.py:502
  91.3 16.7 %collective-permute-start.10 = (f32[32,512]{1,0:T(8,128)S(1)}, f32[32,512]{1,0:T(8,128)S(1)}, u32[]{:S(2)}, u32[]{:S(2)}) collective-permute-start(f32[32,512]{1,0:T(8,128)S(1)} %get-tuple-element.55), channel_id=1, source_target_pairs={{0,5},{1,6},{2,7},{3,0},{4,1},{5,2},{6,3},{7,4},{8,13},{9,14},{10,... | collective-permute-start | bytes 196616 | tf_op jit(solution)/shard_map/ppermute | solution.py:502
  96.2 11.8 %collective-permute-start.11 = (f32[32,512]{1,0:T(8,128)S(1)}, f32[32,512]{1,0:T(8,128)S(1)}, u32[]{:S(2)}, u32[]{:S(2)}) collective-permute-start(f32[32,512]{1,0:T(8,128)S(1)} %get-tuple-element.56), channel_id=1, source_target_pairs={{0,6},{1,7},{2,0},{3,1},{4,2},{5,3},{6,4},{7,5},{8,14},{9,15},{10,... | collective-permute-start | bytes 196616 | tf_op jit(solution)/shard_map/ppermute | solution.py:502
  96.2 11.8 %collective-permute-start.12 = (f32[32,512]{1,0:T(8,128)S(1)}, f32[32,512]{1,0:T(8,128)S(1)}, u32[]{:S(2)}, u32[]{:S(2)}) collective-permute-start(f32[32,512]{1,0:T(8,128)S(1)} %get-tuple-element.57), channel_id=1, source_target_pairs={{0,7},{1,0},{2,1},{3,2},{4,3},{5,4},{6,5},{7,6},{8,15},{9,8},{10,9... | collective-permute-start | bytes 196616 | tf_op jit(solution)/shard_map/ppermute | solution.py:502
  103.1 11.1 %all-to-all-start.3 = ((f32[8,8,128]{2,1,0:T(8,128)}), f32[8,8,128]{2,1,0:T(8,128)S(1)}, u32[]{:S(2)}, u32[]{:S(2)}) async-start(f32[8,8,128]{2,1,0:T(8,128)} %shard_map.73), calls=%async_computation.3 | async-start | bytes 65536 | tf_op jit(solution)/shard_map/all_to_all | solution.py:506

commit v5 on v4

--- a/solution.py
+++ b/solution.py
@@ -206,6 +206,11 @@
             out_ref[:, a * 8 : a * 8 + 8, h * 128 : h * 128 + 128] = tile.reshape(16, 8, 128)
 
 
+def fold(values):
+    lanes = sum(values[:, a * 128 : a * 128 + 128] for a in range(4))
+    return sum(lanes[8 * a : 8 * a + 8] for a in range(4))
+
+
 def space_kernel(
     scale_ref,
     place_ref,
@@ -229,15 +234,12 @@
         g, cols = space_at(m)
         return tuple(u_ref[g, rows, cols] for rows in row_parts(half))
 
-    cost = [jnp.zeros((8, 128), jnp.float32)]
-
     def put_u(m, half, values):
         g, cols = space_at(m)
         for part, rows in enumerate(row_parts(half)):
             p = values[0][part] + u_ref[g, rows, cols] * values[1][part]
             p_ref[g, rows, cols] = p
             v_ref[g, rows, cols] = values[1][part]
-            cost[0] = cost[0] + p * p
 
     def get_p(m, half):
         g, cols = space_at(m)
@@ -250,12 +252,12 @@
 
     symbol = space_symbol(scale_ref[0], small_ref)
     transform(get_u, put_u, 2, symbol, dft_ref, small_ref, a_ref, b_ref)
-    cost_ref[...] = cost[0]
     copies = []
     for d in range(8):
         plane = (place_ref[0] + d) % 8
         copies.append(pltpu.make_async_copy(p_ref.at[plane], p_outs[d], p_sems.at[d]))
         copies[-1].start()
+    cost_ref[...] = fold(jnp.sum(p_ref[...] * p_ref[...], axis=0))
     pack(v_ref, v_send)
     copies.append(pltpu.make_async_copy(v_send, out_ref.at[:, 0:8, :], sems.at[0]))
     copies[-1].start()
@@ -267,37 +269,30 @@
         copy.wait()
 
 
-def time_first_kernel(
-    scale_ref, place_ref, moved_ref, dft_ref, small_ref, u_ref, q_out, q_ref, a_ref, b_ref, sems
-):
+def time_first_kernel(scale_ref, place_ref, moved_ref, dft_ref, small_ref, uq_ref, a_ref, b_ref):
     for m in range(16):
-        u_ref[m] = moved_ref[(place_ref[0] + 4 - m // 4) % 4, (place_ref[1] + 4 - m % 4) % 4]
+        uq_ref[0, m] = moved_ref[(place_ref[0] + 4 - m // 4) % 4, (place_ref[1] + 4 - m % 4) % 4]
 
     def get(m, half):
         t, cols = time_at(m)
-        return tuple(u_ref[t, rows, cols] for rows in row_parts(half))
+        return tuple(uq_ref[0, t, rows, cols] for rows in row_parts(half))
 
     def put(m, half, values):
         t, cols = time_at(m)
         for part, rows in enumerate(row_parts(half)):
-            q_ref[t, rows, cols] = values[0][part]
+            uq_ref[1, t, rows, cols] = values[0][part]
 
     transform(get, put, 1, time_symbol(scale_ref[0], small_ref), dft_ref, small_ref, a_ref, b_ref)
-    copy = pltpu.make_async_copy(q_ref, q_out, sems.at[0])
-    copy.start()
-    copy.wait()
 
 
 def time_second_kernel(
     scale_ref,
-    u_ref,
-    q_in,
+    uq_ref,
     recv_ref,
-    cost_ref,
+    p_cost_ref,
     dft_ref,
     small_ref,
     out_ref,
-    q_ref,
     v_ref,
     s_ref,
     g_ref,
@@ -306,15 +301,22 @@
     b_ref,
     sems,
 ):
-    q_copy = pltpu.make_async_copy(q_in, q_ref, sems.at[0])
-    q_copy.start()
+    copies = [pltpu.make_async_copy(uq_ref.at[1], out_ref.at[:, 0:32, :], sems.at[0])]
+    copies[-1].start()
+    costs = [jnp.zeros((8, 128), jnp.float32)] * 8
     for m in range(16):
         for h in range(2):
             cols = slice(h * 128, h * 128 + 128)
             for o, ref in enumerate((v_ref, g_ref)):
                 tiles = blocks4([recv_ref[m * 8 + 4 * h + k, 8 * o : 8 * o + 8] for k in range(4)])
                 for a in range(4):
-                    ref[m, 8 * a : 8 * a + 8, cols] = tiles[a]
+                    rows = slice(8 * a, 8 * a + 8)
+                    ref[m, rows, cols] = tiles[a]
+                    if o == 0:
+                        q = uq_ref[1, m, rows, cols]
+                        w = uq_ref[0, m, rows, cols] * tiles[a]
+                        s_ref[m, rows, cols] = q + w
+                        costs[4 * h + a] = costs[4 * h + a] + q * (0.5 * q + w)
 
     def get_v(m, half):
         t, cols = time_at(m)
@@ -323,25 +325,11 @@
     def put_v(m, half, values):
         t, cols = time_at(m)
         for part, rows in enumerate(row_parts(half)):
-            g_ref[t, rows, cols] = g_ref[t, rows, cols] - u_ref[t, rows, cols] * values[0][part]
-
-    symbol = time_symbol(scale_ref[0], small_ref)
-    transform(get_v, put_v, 1, symbol, dft_ref, small_ref, a_ref, b_ref)
-
-    q_copy.wait()
-    q_back = pltpu.make_async_copy(q_ref, out_ref.at[:, 0:32, :], sems.at[1])
-    q_back.start()
-    cost = 0.5 * cost_ref[...]
-    for m in range(16):
-        for h in range(2):
-            cols = slice(h * 128, h * 128 + 128)
-            for a in range(4):
-                rows = slice(8 * a, 8 * a + 8)
-                q = q_ref[m, rows, cols]
-                w = u_ref[m, rows, cols] * v_ref[m, rows, cols]
-                s_ref[m, rows, cols] = q + w
-                cost = cost + q * (0.5 * q + w)
-    norm = [jnp.zeros((8, 128), jnp.float32)]
+            v_ref[t, rows, cols] = (
+                g_ref[t, rows, cols] - uq_ref[0, t, rows, cols] * values[0][part]
+            )
+
+    norms = [jnp.zeros((8, 128), jnp.float32)] * 8
 
     def get_s(m, half):
         t, cols = time_at(m)
@@ -350,21 +338,25 @@
     def put_s(m, half, values):
         t, cols = time_at(m)
         for part, rows in enumerate(row_parts(half)):
-            g = g_ref[t, rows, cols] - values[0][part]
+            g = v_ref[t, rows, cols] - values[0][part]
             g_ref[t, rows, cols] = g
-            norm[0] = norm[0] + g * g
-
+            slot = 2 * (m % 4) + part
+            norms[slot] = norms[slot] + g * g
+
+    symbol = time_symbol(scale_ref[0], small_ref)
+    transform(get_v, put_v, 1, symbol, dft_ref, small_ref, a_ref, b_ref)
     transform(get_s, put_s, 1, symbol, dft_ref, small_ref, a_ref, b_ref)
-    g_back = pltpu.make_async_copy(g_ref, out_ref.at[:, 32:64, :], sems.at[2])
-    g_back.start()
+    copies.append(pltpu.make_async_copy(g_ref, out_ref.at[:, 32:64, :], sems.at[1]))
+    copies[-1].start()
+    cost = sum(costs) + 0.5 * p_cost_ref[...]
+    norm = sum(norms)
     for m in range(16):
         sums_ref[m, :, 0:128] = cost
-        sums_ref[m, :, 128:256] = norm[0]
-    sums_back = pltpu.make_async_copy(sums_ref, out_ref.at[:, 64:72, :], sems.at[3])
-    sums_back.start()
-    q_back.wait()
-    g_back.wait()
-    sums_back.wait()
+        sums_ref[m, :, 128:256] = norm
+    copies.append(pltpu.make_async_copy(sums_ref, out_ref.at[:, 64:72, :], sems.at[2]))
+    copies[-1].start()
+    for copy in copies:
+        copy.wait()
 
 
 def sums_kernel(recv_ref, out_ref):
@@ -480,20 +472,19 @@
     pieces, first_move = lax.optimization_barrier((pieces, first_move))
     received = lax.all_to_all(pieces, ("ta", "gx"), 0, 0)
     moved = along_y(first_move, y)
-    cols_u, cols_q = call(
+    (cols_uq,) = call(
         time_first_kernel,
-        [(cols, VM), (cols, HB)],
+        [((2, *cols), VM)],
         [time_scale, t_place, (moved, VM), dft, small],
-        [cols, planes, (1, *planes)],
-        [1],
+        [planes, (1, *planes)],
         flops=2 * 10**9,
     )
     (cols_out,) = call(
         time_second_kernel,
         [((16, 72, 256), HB)],
-        [time_scale, (cols_u, VM), (cols_q, HB), (received, VM), (p_cost, VM), dft, small],
-        [cols, cols, cols, cols, (16, 8, 256), planes, (1, *planes)],
-        [4],
+        [time_scale, (cols_uq, VM), (received, VM), (p_cost, VM), dft, small],
+        [cols, cols, cols, (16, 8, 256), planes, (1, *planes)],
+        [3],
         flops=4 * 10**9,
     )
     cols_out, p_planes = lax.optimization_barrier((cols_out, p_planes))

time: 116 us -> 114 us (0.983)
  local copies, waits for them, and re-layouts: 4.45 us -> 3 us
    unnamed x14 -> x10, local copies, waits for them, and re-layouts: 3.67 us -> 2.22 us
where the time goes in v5:
time: 114 us; the launch traced here: 113 us
  starting transfers between devices  50.4 us (44%)
  waiting for transfers between devices  41.3 us (36%)
  Pallas kernels  16.1 us (14%)
  local copies, waits for them, and re-layouts  3 us (3%)
  between operations  2.34 us (2%)
    pallas_call x8, Pallas kernels, call(): pl.pallas_call(kernel, out_shape=[f32(*shape) for shape, _ in outs], in_s...  16.1 us
    ppermute x7, starting transfers between devices, local(): lax.ppermute(plane, 'gx', [(i, (i + d) % 8) for i in range(8)])  12.9 us
    all_to_all x1, waiting for transfers between devices, local(): received = lax.all_to_all(pieces, ('ta', 'gx'), 0, 0)  12.8 us
    all_to_all x1, waiting for transfers between devices, local(): rows_u = lax.all_to_all(field.reshape(rows), 'gx', 0, 0)  9.96 us
    all_to_all x1, starting transfers between devices, local(): received = lax.all_to_all(pieces, ('ta', 'gx'), 0, 0)  9.74 us
    all_to_all x1, starting transfers between devices, local(): rows_u = lax.all_to_all(field.reshape(rows), 'gx', 0, 0)  8.71 us
    ppermute x3, waiting for transfers between devices, along_y(): moved.append(lax.ppermute(piece, 'ta', shift_pairs(0, e)) if e else piece)  8.29 us
    ppermute x3, starting transfers between devices, along_y(): moved.append(lax.ppermute(piece, 'ta', shift_pairs(0, e)) if e else piece)  6.34 us
  transfers between devices with their start and end apart: 17, of which 6 were waited for; matrix products, arithmetic and copies ran while one was open for 1% of the time, Pallas kernels for 10%

profile of v5, /device:TPU:32, one launch (start us, length us, event | category | flops | bytes accessed | tf_op | source)
XLA Modules:
  0.0 113.3 jit_solution(7510910647185049357)
XLA Ops:
  0.6 0.0 copy-start
  0.6 8.7 %all-to-all-start = ((f32[8,32,512]{2,1,0:T(8,128)}), f32[8,32,512]{2,1,0:T(8,128)S(1)}, u32[]{:S(2)}, u32[]{:S(2)}) async-start(f32[8,32,512]{2,1,0:T(8,128)} %bitcast.26), calls=%async_computation | async-start | bytes 1048576 | tf_op jit(solution)/shard_map/all_to_all | solution.py:461
  9.4 0.0 copy-done
  9.4 0.2 shard_map.69
  9.6 0.7 dynamic-slice_bitcast_fusion
  10.3 2.8 %collective-permute-start.2 = (f32[4,32,256]{2,1,0:T(8,128)}, f32[4,32,256]{2,1,0:T(8,128)S(1)}, u32[]{:S(2)}, u32[]{:S(2)}) collective-permute-start(f32[4,32,256]{2,1,0:T(8,128)} %get-tuple-element.54), channel_id=1, source_target_pairs={{0,24},{8,0},{16,8},{24,16},{32,56},{40,32},{48,40},{56,48},{64,88... | collective-permute-start | bytes 393224 | tf_op jit(solution)/shard_map/ppermute | solution.py:433
  13.0 0.8 collective-permute-start.1
  13.8 0.9 collective-permute-start
  15.4 10.0 %all-to-all-done.u_ref = f32[8,32,512]{2,1,0:T(8,128)S(1)} async-done(((f32[8,32,512]{2,1,0:T(8,128)}), f32[8,32,512]{2,1,0:T(8,128)S(1)}, u32[]{:S(2)}, u32[]{:S(2)}) %all-to-all-start) | async-done | bytes 524320 | tf_op jit(solution)/shard_map/all_to_all | solution.py:461
  25.4 7.1 %shard_map.68 = (f32[128,16,128]{2,1,0:T(8,128)}, f32[32,512]{1,0:T(8,128)S(1)}, f32[32,512]{1,0:T(8,128)S(1)}, f32[32,512]{1,0:T(8,128)S(1)}, f32[32,512]{1,0:T...) custom-call(f32[1]{0:T(128)S(6)} %div.18.scale_ref, ...), custom_call_target="tpu_custom_call" | custom-call | flops 8000000000 | bytes 2097152 | tf_op jit(solution)/shard_map/pallas_call | solution.py:407
  32.5 0.0 collective-permute-done.2
  32.5 0.0 collective-permute-done.1
  32.5 0.0 collective-permute-done
  32.5 9.7 %all-to-all-start.1 = ((f32[128,16,128]{2,1,0:T(8,128)}), f32[128,16,128]{2,1,0:T(8,128)S(1)}, u32[]{:S(2)}, u32[]{:S(2)}) async-start(f32[128,16,128]{2,1,0:T(8,128)} %get-tuple-element.33), calls=%async_computation.1 | async-start | bytes 2097152 | tf_op jit(solution)/shard_map/all_to_all | solution.py:473
  42.5 1.6 %collective-permute-start.3 = (f32[4,32,256]{2,1,0:T(8,128)S(1)}, f32[4,32,256]{2,1,0:T(8,128)S(1)}, u32[]{:S(2)}, u32[]{:S(2)}) collective-permute-start(f32[4,32,256]{2,1,0:T(8,128)S(1)} %pad_maximum_fusion.1), channel_id=1, source_target_pairs={{0,32},{8,40},{16,48},{24,56},{32,64},{40,72},{48,80},{56,88},{64,... | collective-permute-start | bytes 393224 | tf_op jit(solution)/shard_map/ppermute | solution.py:443
  44.1 3.2 %collective-permute-start.4 = (f32[4,32,256]{2,1,0:T(8,128)S(1)}, f32[4,32,256]{2,1,0:T(8,128)S(1)}, u32[]{:S(2)}, u32[]{:S(2)}) collective-permute-start(f32[4,32,256]{2,1,0:T(8,128)S(1)} %pad_maximum_fusion.2), channel_id=1, source_target_pairs={{0,64},{8,72},{16,80},{24,88},{32,96},{40,104},{48,112},{56,120},{... | collective-permute-start | bytes 393224 | tf_op jit(solution)/shard_map/ppermute | solution.py:443
  47.3 1.5 %collective-permute-start.5 = (f32[4,32,256]{2,1,0:T(8,128)S(1)}, f32[4,32,256]{2,1,0:T(8,128)S(1)}, u32[]{:S(2)}, u32[]{:S(2)}) collective-permute-start(f32[4,32,256]{2,1,0:T(8,128)S(1)} %pad_maximum_fusion.3), channel_id=1, source_target_pairs={{0,96},{8,104},{16,112},{24,120},{32,0},{40,8},{48,16},{56,24},{64... | collective-permute-start | bytes 393224 | tf_op jit(solution)/shard_map/ppermute | solution.py:443
  48.8 0.1 pad_add_fusion.place_ref
  49.6 2.5 %collective-permute-done.3 = f32[4,32,256]{2,1,0:T(8,128)S(1)} collective-permute-done((f32[4,32,256]{2,1,0:T(8,128)S(1)}, f32[4,32,256]{2,1,0:T(8,128)S(1)}, u32[]{:S(2)}, u32[]{:S(2)}) %collective-permute-start.3) | collective-permute-done | bytes 131104 | tf_op jit(solution)/shard_map/ppermute | solution.py:443
  52.1 5.8 %collective-permute-done.4 = f32[4,32,256]{2,1,0:T(8,128)S(1)} collective-permute-done((f32[4,32,256]{2,1,0:T(8,128)S(1)}, f32[4,32,256]{2,1,0:T(8,128)S(1)}, u32[]{:S(2)}, u32[]{:S(2)}) %collective-permute-start.4) | collective-permute-done | bytes 131104 | tf_op jit(solution)/shard_map/ppermute | solution.py:443
  57.9 0.0 collective-permute-done.5
  57.9 2.1 %shard_map.70.uq_ref = f32[2,16,32,256]{3,2,1,0:T(8,128)S(1)} custom-call(f32[1]{0:T(128)S(6)} %div.14.scale_ref, s32[2]{0:T(128)S(1)} %pad_add_fusion.place_ref, f32[4,4,32,256]{3,2,1,0:T(8,128)S(1)} %pad_maximum_fusion.moved_ref, bf16[3,256,256]{2,1,0:T(8,128)(2,1)S(1)} %copy-done.1, f32[4,32,128]{2,1,0:T(8,128)S(1)} %copy-done.2), custom_call_target="tpu_custom_call" | custom-call | flops 2000000000 | bytes 2097152 | tf_op jit(solution)/shard_map/pallas_call | solution.py:407
  60.0 1.0 copy-done.3
  61.0 12.8 %all-to-all-done.1.recv_ref = f32[128,16,128]{2,1,0:T(8,128)S(1)} async-done(((f32[128,16,128]{2,1,0:T(8,128)}), f32[128,16,128]{2,1,0:T(8,128)S(1)}, u32[]{:S(2)}, u32[]{:S(2)}) %all-to-all-start.1) | async-done | bytes 1048608 | tf_op jit(solution)/shard_map/all_to_all | solution.py:473
  73.8 1.2 %copy-done.4 = f32[2,16,32,256]{3,2,1,0:T(8,128)S(1)} copy-done((f32[2,16,32,256]{3,2,1,0:T(8,128)S(1)}, f32[2,16,32,256]{3,2,1,0:T(8,128)}, u32[]{:S(2)}) %copy-start.4) | copy-done | bytes 1048600
  75.0 4.0 %shard_map.71 = f32[16,72,256]{2,1,0:T(8,128)} custom-call(f32[1]{0:T(128)S(6)} %div.14.scale_ref, f32[2,16,32,256]{3,2,1,0:T(8,128)S(1)} %copy-done.4, f32[128,16,128]{2,1,0:T(8,128)S(1)} %all-to-all-done.1.recv_ref, f32[8,128]{1,0:T(8,128)S(1)} %get-tuple-element.34.p_cost_ref, bf16[3,256,256]{2,1,0:T(8,128)(2,1)S(1)} %copy-done.1, f32[4,32,128]{2,1,0:T(8,128)S(1)} %copy-done.2), custom_call_target="tpu_custom_call" | custom-call | flops 4000000000 | bytes 2097152 | tf_op jit(solution)/shard_map/pallas_call | solution.py:407
  79.0 3.7 %all-to-all-start.2 = ((f32[16,72,256]{2,1,0:T(8,128)}), f32[16,72,256]{2,1,0:T(8,128)S(1)}, u32[]{:S(2)}, u32[]{:S(2)}) async-start(f32[16,72,256]{2,1,0:T(8,128)} %shard_map.71), calls=%async_computation.2 | async-start | bytes 2359296 | tf_op jit(solution)/shard_map/all_to_all | solution.py:491
  82.7 0.1 collective-permute-start.6
  82.8 1.1 collective-permute-start.7
  83.9 1.8 %collective-permute-start.8 = (f32[32,512]{1,0:T(8,128)S(1)}, f32[32,512]{1,0:T(8,128)S(1)}, u32[]{:S(2)}, u32[]{:S(2)}) collective-permute-start(f32[32,512]{1,0:T(8,128)S(1)} %get-tuple-element.49), channel_id=1, source_target_pairs={{0,3},{1,4},{2,5},{3,6},{4,7},{5,0},{6,1},{7,2},{8,11},{9,12},{10,... | collective-permute-start | bytes 196616 | tf_op jit(solution)/shard_map/ppermute | solution.py:493
  85.7 3.7 %collective-permute-start.9 = (f32[32,512]{1,0:T(8,128)S(1)}, f32[32,512]{1,0:T(8,128)S(1)}, u32[]{:S(2)}, u32[]{:S(2)}) collective-permute-start(f32[32,512]{1,0:T(8,128)S(1)} %get-tuple-element.50), channel_id=1, source_target_pairs={{0,4},{1,5},{2,6},{3,7},{4,0},{5,1},{6,2},{7,3},{8,12},{9,13},{10,... | collective-permute-start | bytes 196616 | tf_op jit(solution)/shard_map/ppermute | solution.py:493
  89.4 4.9 %collective-permute-start.10 = (f32[32,512]{1,0:T(8,128)S(1)}, f32[32,512]{1,0:T(8,128)S(1)}, u32[]{:S(2)}, u32[]{:S(2)}) collective-permute-start(f32[32,512]{1,0:T(8,128)S(1)} %get-tuple-element.51), channel_id=1, source_target_pairs={{0,5},{1,6},{2,7},{3,0},{4,1},{5,2},{6,3},{7,4},{8,13},{9,14},{10,... | collective-permute-start | bytes 196616 | tf_op jit(solution)/shard_map/ppermute | solution.py:493
  94.3 0.0 collective-permute-done.6.refs_1_
  94.3 0.0 collective-permute-start.11
  94.3 0.0 collective-permute-done.7.refs_2_
  94.3 1.3 %collective-permute-start.12 = (f32[32,512]{1,0:T(8,128)S(1)}, f32[32,512]{1,0:T(8,128)S(1)}, u32[]{:S(2)}, u32[]{:S(2)}) collective-permute-start(f32[32,512]{1,0:T(8,128)S(1)} %get-tuple-element.53), channel_id=1, source_target_pairs={{0,7},{1,0},{2,1},{3,2},{4,3},{5,4},{6,5},{7,6},{8,15},{9,8},{10,9... | collective-permute-start | bytes 196616 | tf_op jit(solution)/shard_map/ppermute | solution.py:493
  95.6 4.9 %all-to-all-done.2.recv_ref = f32[16,72,256]{2,1,0:T(8,128)S(1)} async-done(((f32[16,72,256]{2,1,0:T(8,128)}), f32[16,72,256]{2,1,0:T(8,128)S(1)}, u32[]{:S(2)}, u32[]{:S(2)}) %all-to-all-start.2) | async-done | bytes 1179680 | tf_op jit(solution)/shard_map/all_to_all | solution.py:491
  100.6 0.6 shard_map.73
  101.2 4.5 %all-to-all-start.3 = ((f32[8,8,128]{2,1,0:T(8,128)}), f32[8,8,128]{2,1,0:T(8,128)S(1)}, u32[]{:S(2)}, u32[]{:S(2)}) async-start(f32[8,8,128]{2,1,0:T(8,128)} %shard_map.73), calls=%async_computation.3 | async-start | bytes 65536 | tf_op jit(solution)/shard_map/all_to_all | solution.py:497
  105.7 0.3 shard_map.72
  106.1 0.0 collective-permute-done.8.refs_3_
  106.1 0.0 collective-permute-done.9.refs_4_
  106.1 0.0 collective-permute-done.10.refs_5_
  106.1 0.0 collective-permute-done.11.refs_6_
  106.1 0.0 collective-permute-done.12.refs_7_
  106.1 0.9 shard_map.75
  107.0 5.4 %all-to-all-done.3.sums_ref = f32[8,8,128]{2,1,0:T(8,128)S(1)} async-done(((f32[8,8,128]{2,1,0:T(8,128)}), f32[8,8,128]{2,1,0:T(8,128)S(1)}, u32[]{:S(2)}, u32[]{:S(2)}) %all-to-all-start.3) | async-done | bytes 32800 | tf_op jit(solution)/shard_map/all_to_all | solution.py:497
  112.3 1.0 shard_map.74
  (14 shorter events, 0.2 us)
Async XLA Ops:
  0.6 8.7 %copy-start = (f32[256,512]{1,0:T(8,128)S(1)}, f32[256,512]{1,0:T(8,128)}, u32[]{:S(2)}) copy-start(f32[256,512]{1,0:T(8,128)} %u_ref.3) | copy-start | bytes 1572868
  0.6 24.8 %all-to-all-start = ((f32[8,32,512]{2,1,0:T(8,128)}), f32[8,32,512]{2,1,0:T(8,128)S(1)}, u32[]{:S(2)}, u32[]{:S(2)}) async-start(f32[8,32,512]{2,1,0:T(8,128)} %bitcast.26), calls=%async_computation | async-start | bytes 1048576 | tf_op jit(solution)/shard_map/all_to_all | solution.py:461
  9.4 16.0 %copy-start.1 = (bf16[3,256,256]{2,1,0:T(8,128)(2,1)S(1)}, bf16[3,256,256]{2,1,0:T(8,128)(2,1)}, u32[]{:S(2)}) copy-start(bf16[3,256,256]{2,1,0:T(8,128)(2,1)} %constant.144.clone.dft_ref) | copy-start | bytes 1179652
  9.4 16.0 %copy-start.2 = (f32[4,32,128]{2,1,0:T(8,128)S(1)}, f32[4,32,128]{2,1,0:T(8,128)}, u32[]{:S(2)}) copy-start(f32[4,32,128]{2,1,0:T(8,128)} %constant.145.clone.small_ref) | copy-start | bytes 196612
  10.3 22.2 %collective-permute-start.2 = (f32[4,32,256]{2,1,0:T(8,128)}, f32[4,32,256]{2,1,0:T(8,128)S(1)}, u32[]{:S(2)}, u32[]{:S(2)}) collective-permute-start(f32[4,32,256]{2,1,0:T(8,128)} %get-tuple-element.54), channel_id=1, source_target_pairs={{0,24},{8,0},{16,8},{24,16},{32,56},{40,32},{48,40},{56,48},{64,88... | collective-permute-start | bytes 393224 | tf_op jit(solution)/shard_map/ppermute | solution.py:433
  13.0 19.4 %collective-permute-start.1 = (f32[4,32,256]{2,1,0:T(8,128)S(1)}, f32[4,32,256]{2,1,0:T(8,128)S(1)}, u32[]{:S(2)}, u32[]{:S(2)}) collective-permute-start(f32[4,32,256]{2,1,0:T(8,128)S(1)} %get-tuple-element.55), channel_id=1, source_target_pairs={{0,16},{8,24},{16,0},{24,8},{32,48},{40,56},{48,32},{56,40},{64,80... | collective-permute-start | bytes 393224 | tf_op jit(solution)/shard_map/ppermute | solution.py:433
  13.8 18.7 %collective-permute-start = (f32[4,32,256]{2,1,0:T(8,128)S(1)}, f32[4,32,256]{2,1,0:T(8,128)S(1)}, u32[]{:S(2)}, u32[]{:S(2)}) collective-permute-start(f32[4,32,256]{2,1,0:T(8,128)S(1)} %get-tuple-element.56), channel_id=1, source_target_pairs={{0,8},{8,16},{16,24},{24,0},{32,40},{40,48},{48,56},{56,32},{64,72... | collective-permute-start | bytes 393224 | tf_op jit(solution)/shard_map/ppermute | solution.py:433
  32.5 41.3 %all-to-all-start.1 = ((f32[128,16,128]{2,1,0:T(8,128)}), f32[128,16,128]{2,1,0:T(8,128)S(1)}, u32[]{:S(2)}, u32[]{:S(2)}) async-start(f32[128,16,128]{2,1,0:T(8,128)} %get-tuple-element.33), calls=%async_computation.1 | async-start | bytes 2097152 | tf_op jit(solution)/shard_map/all_to_all | solution.py:473
  42.5 9.6 %collective-permute-start.3 = (f32[4,32,256]{2,1,0:T(8,128)S(1)}, f32[4,32,256]{2,1,0:T(8,128)S(1)}, u32[]{:S(2)}, u32[]{:S(2)}) collective-permute-start(f32[4,32,256]{2,1,0:T(8,128)S(1)} %pad_maximum_fusion.1), channel_id=1, source_target_pairs={{0,32},{8,40},{16,48},{24,56},{32,64},{40,72},{48,80},{56,88},{64,... | collective-permute-start | bytes 393224 | tf_op jit(solution)/shard_map/ppermute | solution.py:443
  44.1 13.8 %collective-permute-start.4 = (f32[4,32,256]{2,1,0:T(8,128)S(1)}, f32[4,32,256]{2,1,0:T(8,128)S(1)}, u32[]{:S(2)}, u32[]{:S(2)}) collective-permute-start(f32[4,32,256]{2,1,0:T(8,128)S(1)} %pad_maximum_fusion.2), channel_id=1, source_target_pairs={{0,64},{8,72},{16,80},{24,88},{32,96},{40,104},{48,112},{56,120},{... | collective-permute-start | bytes 393224 | tf_op jit(solution)/shard_map/ppermute | solution.py:443
  47.3 10.6 %collective-permute-start.5 = (f32[4,32,256]{2,1,0:T(8,128)S(1)}, f32[4,32,256]{2,1,0:T(8,128)S(1)}, u32[]{:S(2)}, u32[]{:S(2)}) collective-permute-start(f32[4,32,256]{2,1,0:T(8,128)S(1)} %pad_maximum_fusion.3), channel_id=1, source_target_pairs={{0,96},{8,104},{16,112},{24,120},{32,0},{40,8},{48,16},{56,24},{64... | collective-permute-start | bytes 393224 | tf_op jit(solution)/shard_map/ppermute | solution.py:443
  60.0 1.0 copy-start.3
  73.8 1.2 %copy-start.4 = (f32[2,16,32,256]{3,2,1,0:T(8,128)S(1)}, f32[2,16,32,256]{3,2,1,0:T(8,128)}, u32[]{:S(2)}) copy-start(f32[2,16,32,256]{3,2,1,0:T(8,128)} %copy-done.3) | copy-start | bytes 3145732
  79.0 21.5 %all-to-all-start.2 = ((f32[16,72,256]{2,1,0:T(8,128)}), f32[16,72,256]{2,1,0:T(8,128)S(1)}, u32[]{:S(2)}, u32[]{:S(2)}) async-start(f32[16,72,256]{2,1,0:T(8,128)} %shard_map.71), calls=%async_computation.2 | async-start | bytes 2359296 | tf_op jit(solution)/shard_map/all_to_all | solution.py:491
  82.7 11.6 %collective-permute-start.6 = (f32[32,512]{1,0:T(8,128)S(1)}, f32[32,512]{1,0:T(8,128)S(1)}, u32[]{:S(2)}, u32[]{:S(2)}) collective-permute-start(f32[32,512]{1,0:T(8,128)S(1)} %get-tuple-element.47), channel_id=1, source_target_pairs={{0,1},{1,2},{2,3},{3,4},{4,5},{5,6},{6,7},{7,0},{8,9},{9,10},{10,1... | collective-permute-start | bytes 196616 | tf_op jit(solution)/shard_map/ppermute | solution.py:493
  82.8 11.5 %collective-permute-start.7 = (f32[32,512]{1,0:T(8,128)S(1)}, f32[32,512]{1,0:T(8,128)S(1)}, u32[]{:S(2)}, u32[]{:S(2)}) collective-permute-start(f32[32,512]{1,0:T(8,128)S(1)} %get-tuple-element.48), channel_id=1, source_target_pairs={{0,2},{1,3},{2,4},{3,5},{4,6},{5,7},{6,0},{7,1},{8,10},{9,11},{10,... | collective-permute-start | bytes 196616 | tf_op jit(solution)/shard_map/ppermute | solution.py:493
  83.9 22.2 %collective-permute-start.8 = (f32[32,512]{1,0:T(8,128)S(1)}, f32[32,512]{1,0:T(8,128)S(1)}, u32[]{:S(2)}, u32[]{:S(2)}) collective-permute-start(f32[32,512]{1,0:T(8,128)S(1)} %get-tuple-element.49), channel_id=1, source_target_pairs={{0,3},{1,4},{2,5},{3,6},{4,7},{5,0},{6,1},{7,2},{8,11},{9,12},{10,... | collective-permute-start | bytes 196616 | tf_op jit(solution)/shard_map/ppermute | solution.py:493
  85.7 20.4 %collective-permute-start.9 = (f32[32,512]{1,0:T(8,128)S(1)}, f32[32,512]{1,0:T(8,128)S(1)}, u32[]{:S(2)}, u32[]{:S(2)}) collective-permute-start(f32[32,512]{1,0:T(8,128)S(1)} %get-tuple-element.50), channel_id=1, source_target_pairs={{0,4},{1,5},{2,6},{3,7},{4,0},{5,1},{6,2},{7,3},{8,12},{9,13},{10,... | collective-permute-start | bytes 196616 | tf_op jit(solution)/shard_map/ppermute | solution.py:493
  89.4 16.7 %collective-permute-start.10 = (f32[32,512]{1,0:T(8,128)S(1)}, f32[32,512]{1,0:T(8,128)S(1)}, u32[]{:S(2)}, u32[]{:S(2)}) collective-permute-start(f32[32,512]{1,0:T(8,128)S(1)} %get-tuple-element.51), channel_id=1, source_target_pairs={{0,5},{1,6},{2,7},{3,0},{4,1},{5,2},{6,3},{7,4},{8,13},{9,14},{10,... | collective-permute-start | bytes 196616 | tf_op jit(solution)/shard_map/ppermute | solution.py:493
  94.3 11.8 %collective-permute-start.11 = (f32[32,512]{1,0:T(8,128)S(1)}, f32[32,512]{1,0:T(8,128)S(1)}, u32[]{:S(2)}, u32[]{:S(2)}) collective-permute-start(f32[32,512]{1,0:T(8,128)S(1)} %get-tuple-element.52), channel_id=1, source_target_pairs={{0,6},{1,7},{2,0},{3,1},{4,2},{5,3},{6,4},{7,5},{8,14},{9,15},{10,... | collective-permute-start | bytes 196616 | tf_op jit(solution)/shard_map/ppermute | solution.py:493
  94.3 11.8 %collective-permute-start.12 = (f32[32,512]{1,0:T(8,128)S(1)}, f32[32,512]{1,0:T(8,128)S(1)}, u32[]{:S(2)}, u32[]{:S(2)}) collective-permute-start(f32[32,512]{1,0:T(8,128)S(1)} %get-tuple-element.53), channel_id=1, source_target_pairs={{0,7},{1,0},{2,1},{3,2},{4,3},{5,4},{6,5},{7,6},{8,15},{9,8},{10,9... | collective-permute-start | bytes 196616 | tf_op jit(solution)/shard_map/ppermute | solution.py:493
  101.2 11.1 %all-to-all-start.3 = ((f32[8,8,128]{2,1,0:T(8,128)}), f32[8,8,128]{2,1,0:T(8,128)S(1)}, u32[]{:S(2)}, u32[]{:S(2)}) async-start(f32[8,8,128]{2,1,0:T(8,128)} %shard_map.73), calls=%async_computation.3 | async-start | bytes 65536 | tf_op jit(solution)/shard_map/all_to_all | solution.py:497

commit v6 on v5

--- a/solution.py
+++ b/solution.py
@@ -15,7 +15,8 @@
 RADIX = 32
 SUB = 128
 PARTS = 3
-GROUP = 8
+SPACE_GROUP = 32
+TIME_GROUP = 8
 VMEM_LIMIT = 24 * 1024 * 1024
 
 
@@ -111,7 +112,7 @@
     return jnp.dot(left, right, preferred_element_type=jnp.float32)
 
 
-def transform(get, put, outputs, symbol, dft_ref, small_ref, a_ref, b_ref):
+def transform(get, put, outputs, symbol, dft_ref, small_ref, a_ref, b_ref, group, after=None):
     re_lanes, im_lanes = slice(0, SUB), slice(SUB, 2 * SUB)
     for half in range(2):
         rows = slice(8 * half, 8 * half + 8)
@@ -124,15 +125,15 @@
                 re, im = re * c + im * s, im * c - re * s
             a_ref[k1, rows, re_lanes] = re
             a_ref[k1, rows, im_lanes] = im
-    for group in range(RADIX // GROUP):
-        ks = slice(group * GROUP, (group + 1) * GROUP)
-        got = product(a_ref[ks].reshape(GROUP * 16, 2 * SUB), dft_ref)
-        got = got.reshape(GROUP, 16, 2 * SUB)
+    for first in range(0, RADIX, group):
+        ks = slice(first, first + group)
+        got = product(a_ref[ks].reshape(group * 16, 2 * SUB), dft_ref)
+        got = got.reshape(group, 16, 2 * SUB)
         re, im = got[:, :, re_lanes], got[:, :, im_lanes]
         for o in range(outputs):
             swapped = jnp.concatenate(symbol(o, ks, re, im)[::-1], axis=2)
-            got = product(swapped.reshape(GROUP * 16, 2 * SUB), dft_ref)
-            got = got.reshape(GROUP, 16, 2 * SUB)
+            got = product(swapped.reshape(group * 16, 2 * SUB), dft_ref)
+            got = got.reshape(group, 16, 2 * SUB)
             im2, re2 = got[:, :, re_lanes], got[:, :, im_lanes]
             c = small_ref[0, ks][:, None, :]
             s = small_ref[1, ks][:, None, :]
@@ -146,6 +147,8 @@
         ]
         for m in range(RADIX):
             put(m, half, [outs[o][m] for o in range(outputs)])
+        if after is not None:
+            after(half)
 
 
 def space_symbol(scale, small_ref):
@@ -221,14 +224,11 @@
     *rest,
 ):
     p_outs = rest[:8]
-    cost_ref, p_ref, v_ref, v_send, g_send, a_ref, b_ref, sems, p_sems = rest[8:]
-
-    def pack(ref, send_ref):
-        for g in range(8):
-            stack = jnp.concatenate([ref[g, :, a * 128 : a * 128 + 128] for a in range(4)], axis=0)
-            turned = stack.T.reshape(16, 8, 128)
-            for owner in range(16):
-                send_ref[owner * 8 + g] = turned[owner]
+    cost_ref, p_ref, v_ref, send_ref, a_ref, b_ref, sems, p_sems = rest[8:]
+
+    def pack(ref, g, slot):
+        stack = jnp.concatenate([ref[g, :, a * 128 : a * 128 + 128] for a in range(4)], axis=0)
+        send_ref[g, :, 8 * slot : 8 * slot + 8, :] = stack.T.reshape(16, 8, 128)
 
     def get_u(m, half):
         g, cols = space_at(m)
@@ -251,20 +251,20 @@
             v_ref[g, rows, cols] = values[0][part] - u_ref[g, rows, cols] * values[1][part]
 
     symbol = space_symbol(scale_ref[0], small_ref)
-    transform(get_u, put_u, 2, symbol, dft_ref, small_ref, a_ref, b_ref)
+    transform(get_u, put_u, 2, symbol, dft_ref, small_ref, a_ref, b_ref, SPACE_GROUP)
     copies = []
     for d in range(8):
         plane = (place_ref[0] + d) % 8
         copies.append(pltpu.make_async_copy(p_ref.at[plane], p_outs[d], p_sems.at[d]))
         copies[-1].start()
     cost_ref[...] = fold(jnp.sum(p_ref[...] * p_ref[...], axis=0))
-    pack(v_ref, v_send)
-    copies.append(pltpu.make_async_copy(v_send, out_ref.at[:, 0:8, :], sems.at[0]))
-    copies[-1].start()
-    transform(get_p, put_p, 2, symbol, dft_ref, small_ref, a_ref, b_ref)
-    pack(v_ref, g_send)
-    copies.append(pltpu.make_async_copy(g_send, out_ref.at[:, 8:16, :], sems.at[1]))
-    copies[-1].start()
+    for g in range(8):
+        pack(v_ref, g, 0)
+    transform(get_p, put_p, 2, symbol, dft_ref, small_ref, a_ref, b_ref, SPACE_GROUP)
+    for g in range(8):
+        pack(v_ref, g, 1)
+        copies.append(pltpu.make_async_copy(send_ref.at[g], out_ref.at[g], sems.at[g]))
+        copies[-1].start()
     for copy in copies:
         copy.wait()
 
@@ -282,7 +282,8 @@
         for part, rows in enumerate(row_parts(half)):
             uq_ref[1, t, rows, cols] = values[0][part]
 
-    transform(get, put, 1, time_symbol(scale_ref[0], small_ref), dft_ref, small_ref, a_ref, b_ref)
+    symbol = time_symbol(scale_ref[0], small_ref)
+    transform(get, put, 1, symbol, dft_ref, small_ref, a_ref, b_ref, TIME_GROUP)
 
 
 def time_second_kernel(
@@ -308,7 +309,7 @@
         for h in range(2):
             cols = slice(h * 128, h * 128 + 128)
             for o, ref in enumerate((v_ref, g_ref)):
-                tiles = blocks4([recv_ref[m * 8 + 4 * h + k, 8 * o : 8 * o + 8] for k in range(4)])
+                tiles = blocks4([recv_ref[(4 * h + k) * 16 + m, 8 * o : 8 * o + 8] for k in range(4)])
                 for a in range(4):
                     rows = slice(8 * a, 8 * a + 8)
                     ref[m, rows, cols] = tiles[a]
@@ -344,8 +345,8 @@
             norms[slot] = norms[slot] + g * g
 
     symbol = time_symbol(scale_ref[0], small_ref)
-    transform(get_v, put_v, 1, symbol, dft_ref, small_ref, a_ref, b_ref)
-    transform(get_s, put_s, 1, symbol, dft_ref, small_ref, a_ref, b_ref)
+    transform(get_v, put_v, 1, symbol, dft_ref, small_ref, a_ref, b_ref, TIME_GROUP)
+    transform(get_s, put_s, 1, symbol, dft_ref, small_ref, a_ref, b_ref, TIME_GROUP)
     copies.append(pltpu.make_async_copy(g_ref, out_ref.at[:, 32:64, :], sems.at[1]))
     copies[-1].start()
     cost = sum(costs) + 0.5 * p_cost_ref[...]
@@ -463,14 +464,14 @@
     first_move = along_x(turned, x)
     pieces, *p_planes, p_cost = call(
         space_kernel,
-        [((128, 16, 128), HB)] + [((32, 512), HB)] * 8 + [((8, 128), VM)],
+        [((8, 16, 16, 128), HB)] + [((32, 512), HB)] * 8 + [((8, 128), VM)],
         [space_scale, z_place, (rows_u, VM), dft, small],
-        [rows, rows, (128, 8, 128), (128, 8, 128), planes, (2, *planes)],
-        [2, 8],
+        [rows, rows, (8, 16, 16, 128), planes, (2, *planes)],
+        [8, 8],
         flops=8 * 10**9,
     )
     pieces, first_move = lax.optimization_barrier((pieces, first_move))
-    received = lax.all_to_all(pieces, ("ta", "gx"), 0, 0)
+    received = lax.all_to_all(pieces.reshape(128, 16, 128), ("gx", "ta"), 0, 0)
     moved = along_y(first_move, y)
     (cols_uq,) = call(
         time_first_kernel,

time: 114 us -> 112 us (0.982)
  transfers between devices with their start and end apart: 17 -> 17, of which waited for: 6 -> 6; matrix products, arithmetic and copies ran while one was open for 1% -> 1% of each run, Pallas kernels for 10% -> 9%
where the time goes in v6:
time: 112 us
  starting transfers between devices  49.4 us (44%)
  waiting for transfers between devices  41.3 us (37%)
  Pallas kernels  15.4 us (14%)
  local copies, waits for them, and re-layouts  3 us (3%)
  between operations  2.34 us (2%)
    pallas_call x8, Pallas kernels, call(): pl.pallas_call(kernel, out_shape=[f32(*shape) for shape, _ in outs], in_s...  15.4 us
    all_to_all x1, waiting for transfers between devices, local(): received = lax.all_to_all(pieces.reshape(128, 16, 128), ('gx', 'ta'), 0, 0)  12.5 us
    ppermute x7, starting transfers between devices, local(): lax.ppermute(plane, 'gx', [(i, (i + d) % 8) for i in range(8)])  12.2 us
    all_to_all x1, waiting for transfers between devices, local(): rows_u = lax.all_to_all(field.reshape(rows), 'gx', 0, 0)  9.96 us
    all_to_all x1, starting transfers between devices, local(): received = lax.all_to_all(pieces.reshape(128, 16, 128), ('gx', 'ta'), 0, 0)  9.75 us
    ppermute x3, waiting for transfers between devices, along_y(): moved.append(lax.ppermute(piece, 'ta', shift_pairs(0, e)) if e else piece)  8.83 us
    all_to_all x1, starting transfers between devices, local(): rows_u = lax.all_to_all(field.reshape(rows), 'gx', 0, 0)  8.71 us
    ppermute x3, starting transfers between devices, along_y(): moved.append(lax.ppermute(piece, 'ta', shift_pairs(0, e)) if e else piece)  6.06 us
  transfers between devices with their start and end apart: 17, of which 6 were waited for; matrix products, arithmetic and copies ran while one was open for 1% of the time, Pallas kernels for 9%

profile of v6, /device:TPU:32, one launch (start us, length us, event | category | flops | bytes accessed | tf_op | source)
XLA Modules:
  0.0 111.6 jit_solution(11748459867877810998)
XLA Ops:
  0.6 0.0 copy-start
  0.6 8.7 %all-to-all-start = ((f32[8,32,512]{2,1,0:T(8,128)}), f32[8,32,512]{2,1,0:T(8,128)S(1)}, u32[]{:S(2)}, u32[]{:S(2)}) async-start(f32[8,32,512]{2,1,0:T(8,128)} %bitcast.27), calls=%async_computation | async-start | bytes 1048576 | tf_op jit(solution)/shard_map/all_to_all | solution.py:462
  9.4 0.0 copy-done
  9.4 0.2 shard_map.69
  9.6 0.7 dynamic-slice_bitcast_fusion
  10.3 2.8 %collective-permute-start.2 = (f32[4,32,256]{2,1,0:T(8,128)}, f32[4,32,256]{2,1,0:T(8,128)S(1)}, u32[]{:S(2)}, u32[]{:S(2)}) collective-permute-start(f32[4,32,256]{2,1,0:T(8,128)} %get-tuple-element.54), channel_id=1, source_target_pairs={{0,24},{8,0},{16,8},{24,16},{32,56},{40,32},{48,40},{56,48},{64,88... | collective-permute-start | bytes 393224 | tf_op jit(solution)/shard_map/ppermute | solution.py:434
  13.0 0.8 collective-permute-start.1
  13.8 0.9 collective-permute-start
  15.4 10.0 %all-to-all-done.u_ref = f32[8,32,512]{2,1,0:T(8,128)S(1)} async-done(((f32[8,32,512]{2,1,0:T(8,128)}), f32[8,32,512]{2,1,0:T(8,128)S(1)}, u32[]{:S(2)}, u32[]{:S(2)}) %all-to-all-start) | async-done | bytes 524320 | tf_op jit(solution)/shard_map/all_to_all | solution.py:462
  25.4 6.4 %shard_map.68 = (f32[8,16,16,128]{3,2,1,0:T(8,128)}, f32[32,512]{1,0:T(8,128)S(1)}, f32[32,512]{1,0:T(8,128)S(1)}, f32[32,512]{1,0:T(8,128)S(1)}, f32[32,512]{1,...) custom-call(f32[1]{0:T(128)S(6)} %div.18.scale_ref, ...), custom_call_target="tpu_custom_call" | custom-call | flops 8000000000 | bytes 2097152 | tf_op jit(solution)/shard_map/pallas_call | solution.py:408
  31.8 0.0 collective-permute-done.2
  31.8 0.0 collective-permute-done.1
  31.8 0.0 collective-permute-done
  31.8 9.8 %all-to-all-start.1 = ((f32[128,16,128]{2,1,0:T(8,128)}), f32[128,16,128]{2,1,0:T(8,128)S(1)}, u32[]{:S(2)}, u32[]{:S(2)}) async-start(f32[128,16,128]{2,1,0:T(8,128)} %bitcast.13), calls=%async_computation.1 | async-start | bytes 2097152 | tf_op jit(solution)/shard_map/all_to_all | solution.py:474
  41.8 1.6 %collective-permute-start.3 = (f32[4,32,256]{2,1,0:T(8,128)S(1)}, f32[4,32,256]{2,1,0:T(8,128)S(1)}, u32[]{:S(2)}, u32[]{:S(2)}) collective-permute-start(f32[4,32,256]{2,1,0:T(8,128)S(1)} %pad_maximum_fusion.1), channel_id=1, source_target_pairs={{0,32},{8,40},{16,48},{24,56},{32,64},{40,72},{48,80},{56,88},{64,... | collective-permute-start | bytes 393224 | tf_op jit(solution)/shard_map/ppermute | solution.py:444
  43.3 2.8 %collective-permute-start.4 = (f32[4,32,256]{2,1,0:T(8,128)S(1)}, f32[4,32,256]{2,1,0:T(8,128)S(1)}, u32[]{:S(2)}, u32[]{:S(2)}) collective-permute-start(f32[4,32,256]{2,1,0:T(8,128)S(1)} %pad_maximum_fusion.2), channel_id=1, source_target_pairs={{0,64},{8,72},{16,80},{24,88},{32,96},{40,104},{48,112},{56,120},{... | collective-permute-start | bytes 393224 | tf_op jit(solution)/shard_map/ppermute | solution.py:444
  46.2 1.7 %collective-permute-start.5 = (f32[4,32,256]{2,1,0:T(8,128)S(1)}, f32[4,32,256]{2,1,0:T(8,128)S(1)}, u32[]{:S(2)}, u32[]{:S(2)}) collective-permute-start(f32[4,32,256]{2,1,0:T(8,128)S(1)} %pad_maximum_fusion.3), channel_id=1, source_target_pairs={{0,96},{8,104},{16,112},{24,120},{32,0},{40,8},{48,16},{56,24},{64... | collective-permute-start | bytes 393224 | tf_op jit(solution)/shard_map/ppermute | solution.py:444
  47.8 0.1 pad_add_fusion.place_ref
  48.6 2.4 %collective-permute-done.3 = f32[4,32,256]{2,1,0:T(8,128)S(1)} collective-permute-done((f32[4,32,256]{2,1,0:T(8,128)S(1)}, f32[4,32,256]{2,1,0:T(8,128)S(1)}, u32[]{:S(2)}, u32[]{:S(2)}) %collective-permute-start.3) | collective-permute-done | bytes 131104 | tf_op jit(solution)/shard_map/ppermute | solution.py:444
  51.0 6.4 %collective-permute-done.4 = f32[4,32,256]{2,1,0:T(8,128)S(1)} collective-permute-done((f32[4,32,256]{2,1,0:T(8,128)S(1)}, f32[4,32,256]{2,1,0:T(8,128)S(1)}, u32[]{:S(2)}, u32[]{:S(2)}) %collective-permute-start.4) | collective-permute-done | bytes 131104 | tf_op jit(solution)/shard_map/ppermute | solution.py:444
  57.5 0.0 collective-permute-done.5
  57.5 2.1 %shard_map.70.uq_ref = f32[2,16,32,256]{3,2,1,0:T(8,128)S(1)} custom-call(f32[1]{0:T(128)S(6)} %div.14.scale_ref, s32[2]{0:T(128)S(1)} %pad_add_fusion.place_ref, f32[4,4,32,256]{3,2,1,0:T(8,128)S(1)} %pad_maximum_fusion.moved_ref, bf16[3,256,256]{2,1,0:T(8,128)(2,1)S(1)} %copy-done.1, f32[4,32,128]{2,1,0:T(8,128)S(1)} %copy-done.2), custom_call_target="tpu_custom_call" | custom-call | flops 2000000000 | bytes 2097152 | tf_op jit(solution)/shard_map/pallas_call | solution.py:408
  59.6 1.0 copy-done.3
  60.6 12.5 %all-to-all-done.1.recv_ref = f32[128,16,128]{2,1,0:T(8,128)S(1)} async-done(((f32[128,16,128]{2,1,0:T(8,128)}), f32[128,16,128]{2,1,0:T(8,128)S(1)}, u32[]{:S(2)}, u32[]{:S(2)}) %all-to-all-start.1) | async-done | bytes 1048608 | tf_op jit(solution)/shard_map/all_to_all | solution.py:474
  73.1 1.2 %copy-done.4 = f32[2,16,32,256]{3,2,1,0:T(8,128)S(1)} copy-done((f32[2,16,32,256]{3,2,1,0:T(8,128)S(1)}, f32[2,16,32,256]{3,2,1,0:T(8,128)}, u32[]{:S(2)}) %copy-start.4) | copy-done | bytes 1048600
  74.3 4.0 %shard_map.71 = f32[16,72,256]{2,1,0:T(8,128)} custom-call(f32[1]{0:T(128)S(6)} %div.14.scale_ref, f32[2,16,32,256]{3,2,1,0:T(8,128)S(1)} %copy-done.4, f32[128,16,128]{2,1,0:T(8,128)S(1)} %all-to-all-done.1.recv_ref, f32[8,128]{1,0:T(8,128)S(1)} %get-tuple-element.34.p_cost_ref, bf16[3,256,256]{2,1,0:T(8,128)(2,1)S(1)} %copy-done.1, f32[4,32,128]{2,1,0:T(8,128)S(1)} %copy-done.2), custom_call_target="tpu_custom_call" | custom-call | flops 4000000000 | bytes 2097152 | tf_op jit(solution)/shard_map/pallas_call | solution.py:408
  78.3 3.7 %all-to-all-start.2 = ((f32[16,72,256]{2,1,0:T(8,128)}), f32[16,72,256]{2,1,0:T(8,128)S(1)}, u32[]{:S(2)}, u32[]{:S(2)}) async-start(f32[16,72,256]{2,1,0:T(8,128)} %shard_map.71), calls=%async_computation.2 | async-start | bytes 2359296 | tf_op jit(solution)/shard_map/all_to_all | solution.py:492
  82.0 0.1 collective-permute-start.6
  82.1 0.4 collective-permute-start.7
  82.5 2.9 %collective-permute-start.8 = (f32[32,512]{1,0:T(8,128)S(1)}, f32[32,512]{1,0:T(8,128)S(1)}, u32[]{:S(2)}, u32[]{:S(2)}) collective-permute-start(f32[32,512]{1,0:T(8,128)S(1)} %get-tuple-element.49), channel_id=1, source_target_pairs={{0,3},{1,4},{2,5},{3,6},{4,7},{5,0},{6,1},{7,2},{8,11},{9,12},{10,... | collective-permute-start | bytes 196616 | tf_op jit(solution)/shard_map/ppermute | solution.py:494
  85.5 3.2 %collective-permute-start.9 = (f32[32,512]{1,0:T(8,128)S(1)}, f32[32,512]{1,0:T(8,128)S(1)}, u32[]{:S(2)}, u32[]{:S(2)}) collective-permute-start(f32[32,512]{1,0:T(8,128)S(1)} %get-tuple-element.50), channel_id=1, source_target_pairs={{0,4},{1,5},{2,6},{3,7},{4,0},{5,1},{6,2},{7,3},{8,12},{9,13},{10,... | collective-permute-start | bytes 196616 | tf_op jit(solution)/shard_map/ppermute | solution.py:494
  88.7 4.2 %collective-permute-start.10 = (f32[32,512]{1,0:T(8,128)S(1)}, f32[32,512]{1,0:T(8,128)S(1)}, u32[]{:S(2)}, u32[]{:S(2)}) collective-permute-start(f32[32,512]{1,0:T(8,128)S(1)} %get-tuple-element.51), channel_id=1, source_target_pairs={{0,5},{1,6},{2,7},{3,0},{4,1},{5,2},{6,3},{7,4},{8,13},{9,14},{10,... | collective-permute-start | bytes 196616 | tf_op jit(solution)/shard_map/ppermute | solution.py:494
  92.9 0.0 collective-permute-done.6.refs_1_
  92.9 0.0 collective-permute-start.11
  92.9 0.0 collective-permute-done.7.refs_2_
  92.9 1.3 %collective-permute-start.12 = (f32[32,512]{1,0:T(8,128)S(1)}, f32[32,512]{1,0:T(8,128)S(1)}, u32[]{:S(2)}, u32[]{:S(2)}) collective-permute-start(f32[32,512]{1,0:T(8,128)S(1)} %get-tuple-element.53), channel_id=1, source_target_pairs={{0,7},{1,0},{2,1},{3,2},{4,3},{5,4},{6,5},{7,6},{8,15},{9,8},{10,9... | collective-permute-start | bytes 196616 | tf_op jit(solution)/shard_map/ppermute | solution.py:494
  94.2 4.6 %all-to-all-done.2.recv_ref = f32[16,72,256]{2,1,0:T(8,128)S(1)} async-done(((f32[16,72,256]{2,1,0:T(8,128)}), f32[16,72,256]{2,1,0:T(8,128)S(1)}, u32[]{:S(2)}, u32[]{:S(2)}) %all-to-all-start.2) | async-done | bytes 1179680 | tf_op jit(solution)/shard_map/all_to_all | solution.py:492
  98.8 0.6 shard_map.73
  99.4 4.6 %all-to-all-start.3 = ((f32[8,8,128]{2,1,0:T(8,128)}), f32[8,8,128]{2,1,0:T(8,128)S(1)}, u32[]{:S(2)}, u32[]{:S(2)}) async-start(f32[8,8,128]{2,1,0:T(8,128)} %shard_map.73), calls=%async_computation.3 | async-start | bytes 65536 | tf_op jit(solution)/shard_map/all_to_all | solution.py:498
  104.0 0.3 shard_map.72
  104.4 0.0 collective-permute-done.8.refs_3_
  104.4 0.0 collective-permute-done.9.refs_4_
  104.4 0.0 collective-permute-done.10.refs_5_
  104.4 0.0 collective-permute-done.11.refs_6_
  104.4 0.0 collective-permute-done.12.refs_7_
  104.4 0.9 shard_map.75
  105.3 5.3 %all-to-all-done.3.sums_ref = f32[8,8,128]{2,1,0:T(8,128)S(1)} async-done(((f32[8,8,128]{2,1,0:T(8,128)}), f32[8,8,128]{2,1,0:T(8,128)S(1)}, u32[]{:S(2)}, u32[]{:S(2)}) %all-to-all-start.3) | async-done | bytes 32800 | tf_op jit(solution)/shard_map/all_to_all | solution.py:498
  110.6 1.0 shard_map.74
  (14 shorter events, 0.2 us)
Async XLA Ops:
  0.6 8.7 %copy-start = (f32[256,512]{1,0:T(8,128)S(1)}, f32[256,512]{1,0:T(8,128)}, u32[]{:S(2)}) copy-start(f32[256,512]{1,0:T(8,128)} %u_ref.3) | copy-start | bytes 1572868
  0.6 24.8 %all-to-all-start = ((f32[8,32,512]{2,1,0:T(8,128)}), f32[8,32,512]{2,1,0:T(8,128)S(1)}, u32[]{:S(2)}, u32[]{:S(2)}) async-start(f32[8,32,512]{2,1,0:T(8,128)} %bitcast.27), calls=%async_computation | async-start | bytes 1048576 | tf_op jit(solution)/shard_map/all_to_all | solution.py:462
  9.4 16.0 %copy-start.1 = (bf16[3,256,256]{2,1,0:T(8,128)(2,1)S(1)}, bf16[3,256,256]{2,1,0:T(8,128)(2,1)}, u32[]{:S(2)}) copy-start(bf16[3,256,256]{2,1,0:T(8,128)(2,1)} %constant.144.clone.dft_ref) | copy-start | bytes 1179652
  9.4 16.0 %copy-start.2 = (f32[4,32,128]{2,1,0:T(8,128)S(1)}, f32[4,32,128]{2,1,0:T(8,128)}, u32[]{:S(2)}) copy-start(f32[4,32,128]{2,1,0:T(8,128)} %constant.145.clone.small_ref) | copy-start | bytes 196612
  10.3 21.5 %collective-permute-start.2 = (f32[4,32,256]{2,1,0:T(8,128)}, f32[4,32,256]{2,1,0:T(8,128)S(1)}, u32[]{:S(2)}, u32[]{:S(2)}) collective-permute-start(f32[4,32,256]{2,1,0:T(8,128)} %get-tuple-element.54), channel_id=1, source_target_pairs={{0,24},{8,0},{16,8},{24,16},{32,56},{40,32},{48,40},{56,48},{64,88... | collective-permute-start | bytes 393224 | tf_op jit(solution)/shard_map/ppermute | solution.py:434
  13.0 18.7 %collective-permute-start.1 = (f32[4,32,256]{2,1,0:T(8,128)S(1)}, f32[4,32,256]{2,1,0:T(8,128)S(1)}, u32[]{:S(2)}, u32[]{:S(2)}) collective-permute-start(f32[4,32,256]{2,1,0:T(8,128)S(1)} %get-tuple-element.55), channel_id=1, source_target_pairs={{0,16},{8,24},{16,0},{24,8},{32,48},{40,56},{48,32},{56,40},{64,80... | collective-permute-start | bytes 393224 | tf_op jit(solution)/shard_map/ppermute | solution.py:434
  13.8 18.0 %collective-permute-start = (f32[4,32,256]{2,1,0:T(8,128)S(1)}, f32[4,32,256]{2,1,0:T(8,128)S(1)}, u32[]{:S(2)}, u32[]{:S(2)}) collective-permute-start(f32[4,32,256]{2,1,0:T(8,128)S(1)} %get-tuple-element.56), channel_id=1, source_target_pairs={{0,8},{8,16},{16,24},{24,0},{32,40},{40,48},{48,56},{56,32},{64,72... | collective-permute-start | bytes 393224 | tf_op jit(solution)/shard_map/ppermute | solution.py:434
  31.8 41.3 %all-to-all-start.1 = ((f32[128,16,128]{2,1,0:T(8,128)}), f32[128,16,128]{2,1,0:T(8,128)S(1)}, u32[]{:S(2)}, u32[]{:S(2)}) async-start(f32[128,16,128]{2,1,0:T(8,128)} %bitcast.13), calls=%async_computation.1 | async-start | bytes 2097152 | tf_op jit(solution)/shard_map/all_to_all | solution.py:474
  41.8 9.3 %collective-permute-start.3 = (f32[4,32,256]{2,1,0:T(8,128)S(1)}, f32[4,32,256]{2,1,0:T(8,128)S(1)}, u32[]{:S(2)}, u32[]{:S(2)}) collective-permute-start(f32[4,32,256]{2,1,0:T(8,128)S(1)} %pad_maximum_fusion.1), channel_id=1, source_target_pairs={{0,32},{8,40},{16,48},{24,56},{32,64},{40,72},{48,80},{56,88},{64,... | collective-permute-start | bytes 393224 | tf_op jit(solution)/shard_map/ppermute | solution.py:444
  43.3 14.1 %collective-permute-start.4 = (f32[4,32,256]{2,1,0:T(8,128)S(1)}, f32[4,32,256]{2,1,0:T(8,128)S(1)}, u32[]{:S(2)}, u32[]{:S(2)}) collective-permute-start(f32[4,32,256]{2,1,0:T(8,128)S(1)} %pad_maximum_fusion.2), channel_id=1, source_target_pairs={{0,64},{8,72},{16,80},{24,88},{32,96},{40,104},{48,112},{56,120},{... | collective-permute-start | bytes 393224 | tf_op jit(solution)/shard_map/ppermute | solution.py:444
  46.2 11.3 %collective-permute-start.5 = (f32[4,32,256]{2,1,0:T(8,128)S(1)}, f32[4,32,256]{2,1,0:T(8,128)S(1)}, u32[]{:S(2)}, u32[]{:S(2)}) collective-permute-start(f32[4,32,256]{2,1,0:T(8,128)S(1)} %pad_maximum_fusion.3), channel_id=1, source_target_pairs={{0,96},{8,104},{16,112},{24,120},{32,0},{40,8},{48,16},{56,24},{64... | collective-permute-start | bytes 393224 | tf_op jit(solution)/shard_map/ppermute | solution.py:444
  59.6 1.0 copy-start.3
  73.1 1.2 %copy-start.4 = (f32[2,16,32,256]{3,2,1,0:T(8,128)S(1)}, f32[2,16,32,256]{3,2,1,0:T(8,128)}, u32[]{:S(2)}) copy-start(f32[2,16,32,256]{3,2,1,0:T(8,128)} %copy-done.3) | copy-start | bytes 3145732
  78.3 20.5 %all-to-all-start.2 = ((f32[16,72,256]{2,1,0:T(8,128)}), f32[16,72,256]{2,1,0:T(8,128)S(1)}, u32[]{:S(2)}, u32[]{:S(2)}) async-start(f32[16,72,256]{2,1,0:T(8,128)} %shard_map.71), calls=%async_computation.2 | async-start | bytes 2359296 | tf_op jit(solution)/shard_map/all_to_all | solution.py:492
  82.0 10.9 %collective-permute-start.6 = (f32[32,512]{1,0:T(8,128)S(1)}, f32[32,512]{1,0:T(8,128)S(1)}, u32[]{:S(2)}, u32[]{:S(2)}) collective-permute-start(f32[32,512]{1,0:T(8,128)S(1)} %get-tuple-element.47), channel_id=1, source_target_pairs={{0,1},{1,2},{2,3},{3,4},{4,5},{5,6},{6,7},{7,0},{8,9},{9,10},{10,1... | collective-permute-start | bytes 196616 | tf_op jit(solution)/shard_map/ppermute | solution.py:494
  82.1 10.8 %collective-permute-start.7 = (f32[32,512]{1,0:T(8,128)S(1)}, f32[32,512]{1,0:T(8,128)S(1)}, u32[]{:S(2)}, u32[]{:S(2)}) collective-permute-start(f32[32,512]{1,0:T(8,128)S(1)} %get-tuple-element.48), channel_id=1, source_target_pairs={{0,2},{1,3},{2,4},{3,5},{4,6},{5,7},{6,0},{7,1},{8,10},{9,11},{10,... | collective-permute-start | bytes 196616 | tf_op jit(solution)/shard_map/ppermute | solution.py:494
  82.5 21.8 %collective-permute-start.8 = (f32[32,512]{1,0:T(8,128)S(1)}, f32[32,512]{1,0:T(8,128)S(1)}, u32[]{:S(2)}, u32[]{:S(2)}) collective-permute-start(f32[32,512]{1,0:T(8,128)S(1)} %get-tuple-element.49), channel_id=1, source_target_pairs={{0,3},{1,4},{2,5},{3,6},{4,7},{5,0},{6,1},{7,2},{8,11},{9,12},{10,... | collective-permute-start | bytes 196616 | tf_op jit(solution)/shard_map/ppermute | solution.py:494
  85.5 18.9 %collective-permute-start.9 = (f32[32,512]{1,0:T(8,128)S(1)}, f32[32,512]{1,0:T(8,128)S(1)}, u32[]{:S(2)}, u32[]{:S(2)}) collective-permute-start(f32[32,512]{1,0:T(8,128)S(1)} %get-tuple-element.50), channel_id=1, source_target_pairs={{0,4},{1,5},{2,6},{3,7},{4,0},{5,1},{6,2},{7,3},{8,12},{9,13},{10,... | collective-permute-start | bytes 196616 | tf_op jit(solution)/shard_map/ppermute | solution.py:494
  88.7 15.7 %collective-permute-start.10 = (f32[32,512]{1,0:T(8,128)S(1)}, f32[32,512]{1,0:T(8,128)S(1)}, u32[]{:S(2)}, u32[]{:S(2)}) collective-permute-start(f32[32,512]{1,0:T(8,128)S(1)} %get-tuple-element.51), channel_id=1, source_target_pairs={{0,5},{1,6},{2,7},{3,0},{4,1},{5,2},{6,3},{7,4},{8,13},{9,14},{10,... | collective-permute-start | bytes 196616 | tf_op jit(solution)/shard_map/ppermute | solution.py:494
  92.9 11.5 %collective-permute-start.11 = (f32[32,512]{1,0:T(8,128)S(1)}, f32[32,512]{1,0:T(8,128)S(1)}, u32[]{:S(2)}, u32[]{:S(2)}) collective-permute-start(f32[32,512]{1,0:T(8,128)S(1)} %get-tuple-element.52), channel_id=1, source_target_pairs={{0,6},{1,7},{2,0},{3,1},{4,2},{5,3},{6,4},{7,5},{8,14},{9,15},{10,... | collective-permute-start | bytes 196616 | tf_op jit(solution)/shard_map/ppermute | solution.py:494
  92.9 11.5 %collective-permute-start.12 = (f32[32,512]{1,0:T(8,128)S(1)}, f32[32,512]{1,0:T(8,128)S(1)}, u32[]{:S(2)}, u32[]{:S(2)}) collective-permute-start(f32[32,512]{1,0:T(8,128)S(1)} %get-tuple-element.53), channel_id=1, source_target_pairs={{0,7},{1,0},{2,1},{3,2},{4,3},{5,4},{6,5},{7,6},{8,15},{9,8},{10,9... | collective-permute-start | bytes 196616 | tf_op jit(solution)/shard_map/ppermute | solution.py:494
  99.4 11.2 %all-to-all-start.3 = ((f32[8,8,128]{2,1,0:T(8,128)}), f32[8,8,128]{2,1,0:T(8,128)S(1)}, u32[]{:S(2)}, u32[]{:S(2)}) async-start(f32[8,8,128]{2,1,0:T(8,128)} %shard_map.73), calls=%async_computation.3 | async-start | bytes 65536 | tf_op jit(solution)/shard_map/all_to_all | solution.py:498

commit v7 on v6

--- a/solution.py
+++ b/solution.py
@@ -15,7 +15,7 @@
 RADIX = 32
 SUB = 128
 PARTS = 3
-SPACE_GROUP = 32
+SPACE_GROUP = 16
 TIME_GROUP = 8
 VMEM_LIMIT = 24 * 1024 * 1024
 
@@ -130,13 +130,16 @@
         got = product(a_ref[ks].reshape(group * 16, 2 * SUB), dft_ref)
         got = got.reshape(group, 16, 2 * SUB)
         re, im = got[:, :, re_lanes], got[:, :, im_lanes]
+        swapped = [
+            jnp.concatenate(symbol(o, ks, re, im)[::-1], axis=2).reshape(group * 16, 2 * SUB)
+            for o in range(outputs)
+        ]
+        got = product(jnp.concatenate(swapped, axis=0), dft_ref)
+        got = got.reshape(outputs, group, 16, 2 * SUB)
+        c = small_ref[0, ks][:, None, :]
+        s = small_ref[1, ks][:, None, :]
         for o in range(outputs):
-            swapped = jnp.concatenate(symbol(o, ks, re, im)[::-1], axis=2)
-            got = product(swapped.reshape(group * 16, 2 * SUB), dft_ref)
-            got = got.reshape(group, 16, 2 * SUB)
-            im2, re2 = got[:, :, re_lanes], got[:, :, im_lanes]
-            c = small_ref[0, ks][:, None, :]
-            s = small_ref[1, ks][:, None, :]
+            im2, re2 = got[o, :, :, re_lanes], got[o, :, :, im_lanes]
             b_ref[o, ks, :, re_lanes] = re2 * c - im2 * s
             b_ref[o, ks, :, im_lanes] = im2 * c + re2 * s
     for half in range(2):
@@ -302,8 +305,18 @@
     b_ref,
     sems,
 ):
-    copies = [pltpu.make_async_copy(uq_ref.at[1], out_ref.at[:, 0:32, :], sems.at[0])]
-    copies[-1].start()
+    copies = []
+
+    def send(ref, first, sem):
+        for h in range(2):
+            lanes = slice(h * 128, h * 128 + 128)
+            rows = slice(first + 32 * h, first + 32 * h + 32)
+            copies.append(
+                pltpu.make_async_copy(ref.at[:, :, lanes], out_ref.at[:, rows, :], sems.at[sem + h])
+            )
+            copies[-1].start()
+
+    send(uq_ref.at[1], 0, 0)
     costs = [jnp.zeros((8, 128), jnp.float32)] * 8
     for m in range(16):
         for h in range(2):
@@ -347,14 +360,12 @@
     symbol = time_symbol(scale_ref[0], small_ref)
     transform(get_v, put_v, 1, symbol, dft_ref, small_ref, a_ref, b_ref, TIME_GROUP)
     transform(get_s, put_s, 1, symbol, dft_ref, small_ref, a_ref, b_ref, TIME_GROUP)
-    copies.append(pltpu.make_async_copy(g_ref, out_ref.at[:, 32:64, :], sems.at[1]))
-    copies[-1].start()
+    send(g_ref, 64, 2)
     cost = sum(costs) + 0.5 * p_cost_ref[...]
     norm = sum(norms)
-    for m in range(16):
-        sums_ref[m, :, 0:128] = cost
-        sums_ref[m, :, 128:256] = norm
-    copies.append(pltpu.make_async_copy(sums_ref, out_ref.at[:, 64:72, :], sems.at[2]))
+    both = jnp.concatenate([cost[0:4] + cost[4:8], norm[0:4] + norm[4:8]], axis=0)
+    sums_ref[...] = jnp.broadcast_to(both[None], (16, 8, 128))
+    copies.append(pltpu.make_async_copy(sums_ref, out_ref.at[:, 128:136, :], sems.at[4]))
     copies[-1].start()
     for copy in copies:
         copy.wait()
@@ -362,8 +373,8 @@
 
 def sums_kernel(recv_ref, out_ref):
     total = jnp.sum(recv_ref[...], axis=0)
-    cost = jnp.sum(total[:, 0:128], axis=0, keepdims=True)
-    norm = jnp.sum(total[:, 128:256], axis=0, keepdims=True)
+    cost = jnp.sum(total[0:4], axis=0, keepdims=True)
+    norm = jnp.sum(total[4:8], axis=0, keepdims=True)
     row = lax.broadcasted_iota(jnp.int32, (8, 128), 0)
     out_ref[...] = jnp.broadcast_to(jnp.where(row == 0, cost, norm)[None], (8, 8, 128))
 
@@ -371,14 +382,14 @@
 def unturn(recv_ref, first, ref):
     for h in range(2):
         for a in range(4):
-            rows = slice(first + 8 * a, first + 8 * a + 8)
-            tile = recv_ref[:, rows, h * 128 : h * 128 + 128]
+            rows = slice(first + 32 * h + 8 * a, first + 32 * h + 8 * a + 8)
+            tile = recv_ref[:, rows, :]
             ref[h * 128 : h * 128 + 128, a * 128 : a * 128 + 128] = tile.reshape(128, 128).T
 
 
 def unturn_kernel(recv_ref, q_ref, g_ref):
     unturn(recv_ref, 0, q_ref)
-    unturn(recv_ref, 32, g_ref)
+    unturn(recv_ref, 64, g_ref)
 
 
 def residual_kernel(place_ref, q_ref, *refs):
@@ -482,10 +493,10 @@
     )
     (cols_out,) = call(
         time_second_kernel,
-        [((16, 72, 256), HB)],
+        [((16, 136, 128), HB)],
         [time_scale, (cols_uq, VM), (received, VM), (p_cost, VM), dft, small],
-        [cols, cols, cols, (16, 8, 256), planes, (1, *planes)],
-        [3],
+        [cols, cols, cols, (16, 8, 128), planes, (1, *planes)],
+        [5],
         flops=4 * 10**9,
     )
     cols_out, p_planes = lax.optimization_barrier((cols_out, p_planes))
@@ -494,7 +505,7 @@
         lax.ppermute(plane, "gx", [(i, (i + d) % 8) for i in range(8)]) if d else plane
         for d, plane in enumerate(p_planes)
     ]
-    (sums,) = call(sums_kernel, [((8, 8, 128), VM)], [(back[:, 64:72, :], VM)])
+    (sums,) = call(sums_kernel, [((8, 8, 128), VM)], [(back[:, 128:136, :], VM)])
     sums = lax.all_to_all(sums, "gx", 0, 0)
     block_q, block_g = call(unturn_kernel, [((256, 512), VM), ((256, 512), VM)], [(back, VM)])
     (residual,) = call(

time: 112 us -> 111 us (level)
  no operation moved by 1% of the time
where the time goes in v7:
time: 111 us
  starting transfers between devices  49.4 us (45%)
  waiting for transfers between devices  40.5 us (36%)
  Pallas kernels  15.2 us (14%)
  local copies, waits for them, and re-layouts  3 us (3%)
  between operations  2.33 us (2%)
    pallas_call x8, Pallas kernels, call(): pl.pallas_call(kernel, out_shape=[f32(*shape) for shape, _ in outs], in_s...  15.2 us
    all_to_all x1, waiting for transfers between devices, local(): received = lax.all_to_all(pieces.reshape(128, 16, 128), ('gx', 'ta'), 0, 0)  12.5 us
    ppermute x7, starting transfers between devices, local(): lax.ppermute(plane, 'gx', [(i, (i + d) % 8) for i in range(8)])  12.2 us
    all_to_all x1, waiting for transfers between devices, local(): rows_u = lax.all_to_all(field.reshape(rows), 'gx', 0, 0)  9.96 us
    all_to_all x1, starting transfers between devices, local(): received = lax.all_to_all(pieces.reshape(128, 16, 128), ('gx', 'ta'), 0, 0)  9.75 us
    ppermute x3, waiting for transfers between devices, along_y(): moved.append(lax.ppermute(piece, 'ta', shift_pairs(0, e)) if e else piece)  8.83 us
    all_to_all x1, starting transfers between devices, local(): rows_u = lax.all_to_all(field.reshape(rows), 'gx', 0, 0)  8.71 us
    ppermute x3, starting transfers between devices, along_y(): moved.append(lax.ppermute(piece, 'ta', shift_pairs(0, e)) if e else piece)  6.06 us
  transfers between devices with their start and end apart: 17, of which 6 were waited for; matrix products, arithmetic and copies ran while one was open for 1% of the time, Pallas kernels for 9%

profile of v7, /device:TPU:32, one launch (start us, length us, event | category | flops | bytes accessed | tf_op | source)
XLA Modules:
  0.0 110.6 jit_solution(871632968492579143)
XLA Ops:
  0.6 0.0 copy-start
  0.6 8.7 %all-to-all-start = ((f32[8,32,512]{2,1,0:T(8,128)}), f32[8,32,512]{2,1,0:T(8,128)S(1)}, u32[]{:S(2)}, u32[]{:S(2)}) async-start(f32[8,32,512]{2,1,0:T(8,128)} %bitcast.27), calls=%async_computation | async-start | bytes 1048576 | tf_op jit(solution)/shard_map/all_to_all | solution.py:473
  9.4 0.0 copy-done
  9.4 0.2 shard_map.69
  9.6 0.7 dynamic-slice_bitcast_fusion
  10.3 2.8 %collective-permute-start.2 = (f32[4,32,256]{2,1,0:T(8,128)}, f32[4,32,256]{2,1,0:T(8,128)S(1)}, u32[]{:S(2)}, u32[]{:S(2)}) collective-permute-start(f32[4,32,256]{2,1,0:T(8,128)} %get-tuple-element.54), channel_id=1, source_target_pairs={{0,24},{8,0},{16,8},{24,16},{32,56},{40,32},{48,40},{56,48},{64,88... | collective-permute-start | bytes 393224 | tf_op jit(solution)/shard_map/ppermute | solution.py:445
  13.1 0.8 collective-permute-start.1
  13.9 0.9 collective-permute-start
  15.4 10.0 %all-to-all-done.u_ref = f32[8,32,512]{2,1,0:T(8,128)S(1)} async-done(((f32[8,32,512]{2,1,0:T(8,128)}), f32[8,32,512]{2,1,0:T(8,128)S(1)}, u32[]{:S(2)}, u32[]{:S(2)}) %all-to-all-start) | async-done | bytes 524320 | tf_op jit(solution)/shard_map/all_to_all | solution.py:473
  25.4 6.1 %shard_map.68 = (f32[8,16,16,128]{3,2,1,0:T(8,128)}, f32[32,512]{1,0:T(8,128)S(1)}, f32[32,512]{1,0:T(8,128)S(1)}, f32[32,512]{1,0:T(8,128)S(1)}, f32[32,512]{1,...) custom-call(f32[1]{0:T(128)S(6)} %div.18.scale_ref, ...), custom_call_target="tpu_custom_call" | custom-call | flops 8000000000 | bytes 2097152 | tf_op jit(solution)/shard_map/pallas_call | solution.py:419
  31.5 0.0 collective-permute-done.2
  31.6 0.0 collective-permute-done.1
  31.6 0.0 collective-permute-done
  31.6 9.8 %all-to-all-start.1 = ((f32[128,16,128]{2,1,0:T(8,128)}), f32[128,16,128]{2,1,0:T(8,128)S(1)}, u32[]{:S(2)}, u32[]{:S(2)}) async-start(f32[128,16,128]{2,1,0:T(8,128)} %bitcast.13), calls=%async_computation.1 | async-start | bytes 2097152 | tf_op jit(solution)/shard_map/all_to_all | solution.py:485
  41.5 1.6 %collective-permute-start.3 = (f32[4,32,256]{2,1,0:T(8,128)S(1)}, f32[4,32,256]{2,1,0:T(8,128)S(1)}, u32[]{:S(2)}, u32[]{:S(2)}) collective-permute-start(f32[4,32,256]{2,1,0:T(8,128)S(1)} %pad_maximum_fusion.1), channel_id=1, source_target_pairs={{0,32},{8,40},{16,48},{24,56},{32,64},{40,72},{48,80},{56,88},{64,... | collective-permute-start | bytes 393224 | tf_op jit(solution)/shard_map/ppermute | solution.py:455
  43.1 2.8 %collective-permute-start.4 = (f32[4,32,256]{2,1,0:T(8,128)S(1)}, f32[4,32,256]{2,1,0:T(8,128)S(1)}, u32[]{:S(2)}, u32[]{:S(2)}) collective-permute-start(f32[4,32,256]{2,1,0:T(8,128)S(1)} %pad_maximum_fusion.2), channel_id=1, source_target_pairs={{0,64},{8,72},{16,80},{24,88},{32,96},{40,104},{48,112},{56,120},{... | collective-permute-start | bytes 393224 | tf_op jit(solution)/shard_map/ppermute | solution.py:455
  45.9 1.7 %collective-permute-start.5 = (f32[4,32,256]{2,1,0:T(8,128)S(1)}, f32[4,32,256]{2,1,0:T(8,128)S(1)}, u32[]{:S(2)}, u32[]{:S(2)}) collective-permute-start(f32[4,32,256]{2,1,0:T(8,128)S(1)} %pad_maximum_fusion.3), channel_id=1, source_target_pairs={{0,96},{8,104},{16,112},{24,120},{32,0},{40,8},{48,16},{56,24},{64... | collective-permute-start | bytes 393224 | tf_op jit(solution)/shard_map/ppermute | solution.py:455
  47.6 0.1 pad_add_fusion.place_ref
  48.4 2.4 %collective-permute-done.3 = f32[4,32,256]{2,1,0:T(8,128)S(1)} collective-permute-done((f32[4,32,256]{2,1,0:T(8,128)S(1)}, f32[4,32,256]{2,1,0:T(8,128)S(1)}, u32[]{:S(2)}, u32[]{:S(2)}) %collective-permute-start.3) | collective-permute-done | bytes 131104 | tf_op jit(solution)/shard_map/ppermute | solution.py:455
  50.8 6.4 %collective-permute-done.4 = f32[4,32,256]{2,1,0:T(8,128)S(1)} collective-permute-done((f32[4,32,256]{2,1,0:T(8,128)S(1)}, f32[4,32,256]{2,1,0:T(8,128)S(1)}, u32[]{:S(2)}, u32[]{:S(2)}) %collective-permute-start.4) | collective-permute-done | bytes 131104 | tf_op jit(solution)/shard_map/ppermute | solution.py:455
  57.2 0.0 collective-permute-done.5
  57.3 2.1 %shard_map.70.uq_ref = f32[2,16,32,256]{3,2,1,0:T(8,128)S(1)} custom-call(f32[1]{0:T(128)S(6)} %div.14.scale_ref, s32[2]{0:T(128)S(1)} %pad_add_fusion.place_ref, f32[4,4,32,256]{3,2,1,0:T(8,128)S(1)} %pad_maximum_fusion.moved_ref, bf16[3,256,256]{2,1,0:T(8,128)(2,1)S(1)} %copy-done.1, f32[4,32,128]{2,1,0:T(8,128)S(1)} %copy-done.2), custom_call_target="tpu_custom_call" | custom-call | flops 2000000000 | bytes 2097152 | tf_op jit(solution)/shard_map/pallas_call | solution.py:419
  59.3 1.0 copy-done.3
  60.3 12.5 %all-to-all-done.1.recv_ref = f32[128,16,128]{2,1,0:T(8,128)S(1)} async-done(((f32[128,16,128]{2,1,0:T(8,128)}), f32[128,16,128]{2,1,0:T(8,128)S(1)}, u32[]{:S(2)}, u32[]{:S(2)}) %all-to-all-start.1) | async-done | bytes 1048608 | tf_op jit(solution)/shard_map/all_to_all | solution.py:485
  72.9 1.2 %copy-done.4 = f32[2,16,32,256]{3,2,1,0:T(8,128)S(1)} copy-done((f32[2,16,32,256]{3,2,1,0:T(8,128)S(1)}, f32[2,16,32,256]{3,2,1,0:T(8,128)}, u32[]{:S(2)}) %copy-start.4) | copy-done | bytes 1048600
  74.1 4.0 %shard_map.71 = f32[16,136,128]{2,1,0:T(8,128)} custom-call(f32[1]{0:T(128)S(6)} %div.14.scale_ref, f32[2,16,32,256]{3,2,1,0:T(8,128)S(1)} %copy-done.4, f32[128,16,128]{2,1,0:T(8,128)S(1)} %all-to-all-done.1.recv_ref, f32[8,128]{1,0:T(8,128)S(1)} %get-tuple-element.34.p_cost_ref, bf16[3,256,256]{2,1,0:T(8,128)(2,1)S(1)} %copy-done.1, ...), custom_call_target="tpu_custom_call" | custom-call | flops 4000000000 | bytes 2097152 | tf_op jit(solution)/shard_map/pallas_call | solution.py:419
  78.1 3.7 %all-to-all-start.2 = ((f32[16,136,128]{2,1,0:T(8,128)}), f32[16,136,128]{2,1,0:T(8,128)S(1)}, u32[]{:S(2)}, u32[]{:S(2)}) async-start(f32[16,136,128]{2,1,0:T(8,128)} %shard_map.71), calls=%async_computation.2 | async-start | bytes 2228224 | tf_op jit(solution)/shard_map/all_to_all | solution.py:503
  81.8 0.1 collective-permute-start.6
  81.9 0.4 collective-permute-start.7
  82.3 2.9 %collective-permute-start.8 = (f32[32,512]{1,0:T(8,128)S(1)}, f32[32,512]{1,0:T(8,128)S(1)}, u32[]{:S(2)}, u32[]{:S(2)}) collective-permute-start(f32[32,512]{1,0:T(8,128)S(1)} %get-tuple-element.49), channel_id=1, source_target_pairs={{0,3},{1,4},{2,5},{3,6},{4,7},{5,0},{6,1},{7,2},{8,11},{9,12},{10,... | collective-permute-start | bytes 196616 | tf_op jit(solution)/shard_map/ppermute | solution.py:505
  85.2 3.2 %collective-permute-start.9 = (f32[32,512]{1,0:T(8,128)S(1)}, f32[32,512]{1,0:T(8,128)S(1)}, u32[]{:S(2)}, u32[]{:S(2)}) collective-permute-start(f32[32,512]{1,0:T(8,128)S(1)} %get-tuple-element.50), channel_id=1, source_target_pairs={{0,4},{1,5},{2,6},{3,7},{4,0},{5,1},{6,2},{7,3},{8,12},{9,13},{10,... | collective-permute-start | bytes 196616 | tf_op jit(solution)/shard_map/ppermute | solution.py:505
  88.4 4.2 %collective-permute-start.10 = (f32[32,512]{1,0:T(8,128)S(1)}, f32[32,512]{1,0:T(8,128)S(1)}, u32[]{:S(2)}, u32[]{:S(2)}) collective-permute-start(f32[32,512]{1,0:T(8,128)S(1)} %get-tuple-element.51), channel_id=1, source_target_pairs={{0,5},{1,6},{2,7},{3,0},{4,1},{5,2},{6,3},{7,4},{8,13},{9,14},{10,... | collective-permute-start | bytes 196616 | tf_op jit(solution)/shard_map/ppermute | solution.py:505
  92.6 0.0 collective-permute-done.6.refs_1_
  92.7 0.0 collective-permute-start.11
  92.7 0.0 collective-permute-done.7.refs_2_
  92.7 1.3 %collective-permute-start.12 = (f32[32,512]{1,0:T(8,128)S(1)}, f32[32,512]{1,0:T(8,128)S(1)}, u32[]{:S(2)}, u32[]{:S(2)}) collective-permute-start(f32[32,512]{1,0:T(8,128)S(1)} %get-tuple-element.53), channel_id=1, source_target_pairs={{0,7},{1,0},{2,1},{3,2},{4,3},{5,4},{6,5},{7,6},{8,15},{9,8},{10,9... | collective-permute-start | bytes 196616 | tf_op jit(solution)/shard_map/ppermute | solution.py:505
  94.0 3.9 %all-to-all-done.2.recv_ref = f32[16,136,128]{2,1,0:T(8,128)S(1)} async-done(((f32[16,136,128]{2,1,0:T(8,128)}), f32[16,136,128]{2,1,0:T(8,128)S(1)}, u32[]{:S(2)}, u32[]{:S(2)}) %all-to-all-start.2) | async-done | bytes 1114144 | tf_op jit(solution)/shard_map/all_to_all | solution.py:503
  97.8 0.6 shard_map.73
  98.5 4.5 %all-to-all-start.3 = ((f32[8,8,128]{2,1,0:T(8,128)}), f32[8,8,128]{2,1,0:T(8,128)S(1)}, u32[]{:S(2)}, u32[]{:S(2)}) async-start(f32[8,8,128]{2,1,0:T(8,128)} %shard_map.73), calls=%async_computation.3 | async-start | bytes 65536 | tf_op jit(solution)/shard_map/all_to_all | solution.py:509
  103.0 0.3 shard_map.72
  103.3 0.0 collective-permute-done.8.refs_3_
  103.3 0.0 collective-permute-done.9.refs_4_
  103.4 0.0 collective-permute-done.10.refs_5_
  103.4 0.0 collective-permute-done.11.refs_6_
  103.4 0.0 collective-permute-done.12.refs_7_
  103.4 0.9 shard_map.75
  104.2 5.3 %all-to-all-done.3.sums_ref = f32[8,8,128]{2,1,0:T(8,128)S(1)} async-done(((f32[8,8,128]{2,1,0:T(8,128)}), f32[8,8,128]{2,1,0:T(8,128)S(1)}, u32[]{:S(2)}, u32[]{:S(2)}) %all-to-all-start.3) | async-done | bytes 32800 | tf_op jit(solution)/shard_map/all_to_all | solution.py:509
  109.6 1.0 shard_map.74
  (14 shorter events, 0.2 us)
Async XLA Ops:
  0.6 8.7 %copy-start = (f32[256,512]{1,0:T(8,128)S(1)}, f32[256,512]{1,0:T(8,128)}, u32[]{:S(2)}) copy-start(f32[256,512]{1,0:T(8,128)} %u_ref.3) | copy-start | bytes 1572868
  0.6 24.8 %all-to-all-start = ((f32[8,32,512]{2,1,0:T(8,128)}), f32[8,32,512]{2,1,0:T(8,128)S(1)}, u32[]{:S(2)}, u32[]{:S(2)}) async-start(f32[8,32,512]{2,1,0:T(8,128)} %bitcast.27), calls=%async_computation | async-start | bytes 1048576 | tf_op jit(solution)/shard_map/all_to_all | solution.py:473
  9.4 16.0 %copy-start.1 = (bf16[3,256,256]{2,1,0:T(8,128)(2,1)S(1)}, bf16[3,256,256]{2,1,0:T(8,128)(2,1)}, u32[]{:S(2)}) copy-start(bf16[3,256,256]{2,1,0:T(8,128)(2,1)} %constant.144.clone.dft_ref) | copy-start | bytes 1179652
  9.4 16.0 %copy-start.2 = (f32[4,32,128]{2,1,0:T(8,128)S(1)}, f32[4,32,128]{2,1,0:T(8,128)}, u32[]{:S(2)}) copy-start(f32[4,32,128]{2,1,0:T(8,128)} %constant.145.clone.small_ref) | copy-start | bytes 196612
  10.3 21.3 %collective-permute-start.2 = (f32[4,32,256]{2,1,0:T(8,128)}, f32[4,32,256]{2,1,0:T(8,128)S(1)}, u32[]{:S(2)}, u32[]{:S(2)}) collective-permute-start(f32[4,32,256]{2,1,0:T(8,128)} %get-tuple-element.54), channel_id=1, source_target_pairs={{0,24},{8,0},{16,8},{24,16},{32,56},{40,32},{48,40},{56,48},{64,88... | collective-permute-start | bytes 393224 | tf_op jit(solution)/shard_map/ppermute | solution.py:445
  13.1 18.5 %collective-permute-start.1 = (f32[4,32,256]{2,1,0:T(8,128)S(1)}, f32[4,32,256]{2,1,0:T(8,128)S(1)}, u32[]{:S(2)}, u32[]{:S(2)}) collective-permute-start(f32[4,32,256]{2,1,0:T(8,128)S(1)} %get-tuple-element.55), channel_id=1, source_target_pairs={{0,16},{8,24},{16,0},{24,8},{32,48},{40,56},{48,32},{56,40},{64,80... | collective-permute-start | bytes 393224 | tf_op jit(solution)/shard_map/ppermute | solution.py:445
  13.9 17.7 %collective-permute-start = (f32[4,32,256]{2,1,0:T(8,128)S(1)}, f32[4,32,256]{2,1,0:T(8,128)S(1)}, u32[]{:S(2)}, u32[]{:S(2)}) collective-permute-start(f32[4,32,256]{2,1,0:T(8,128)S(1)} %get-tuple-element.56), channel_id=1, source_target_pairs={{0,8},{8,16},{16,24},{24,0},{32,40},{40,48},{48,56},{56,32},{64,72... | collective-permute-start | bytes 393224 | tf_op jit(solution)/shard_map/ppermute | solution.py:445
  31.6 41.3 %all-to-all-start.1 = ((f32[128,16,128]{2,1,0:T(8,128)}), f32[128,16,128]{2,1,0:T(8,128)S(1)}, u32[]{:S(2)}, u32[]{:S(2)}) async-start(f32[128,16,128]{2,1,0:T(8,128)} %bitcast.13), calls=%async_computation.1 | async-start | bytes 2097152 | tf_op jit(solution)/shard_map/all_to_all | solution.py:485
  41.5 9.3 %collective-permute-start.3 = (f32[4,32,256]{2,1,0:T(8,128)S(1)}, f32[4,32,256]{2,1,0:T(8,128)S(1)}, u32[]{:S(2)}, u32[]{:S(2)}) collective-permute-start(f32[4,32,256]{2,1,0:T(8,128)S(1)} %pad_maximum_fusion.1), channel_id=1, source_target_pairs={{0,32},{8,40},{16,48},{24,56},{32,64},{40,72},{48,80},{56,88},{64,... | collective-permute-start | bytes 393224 | tf_op jit(solution)/shard_map/ppermute | solution.py:455
  43.1 14.1 %collective-permute-start.4 = (f32[4,32,256]{2,1,0:T(8,128)S(1)}, f32[4,32,256]{2,1,0:T(8,128)S(1)}, u32[]{:S(2)}, u32[]{:S(2)}) collective-permute-start(f32[4,32,256]{2,1,0:T(8,128)S(1)} %pad_maximum_fusion.2), channel_id=1, source_target_pairs={{0,64},{8,72},{16,80},{24,88},{32,96},{40,104},{48,112},{56,120},{... | collective-permute-start | bytes 393224 | tf_op jit(solution)/shard_map/ppermute | solution.py:455
  45.9 11.3 %collective-permute-start.5 = (f32[4,32,256]{2,1,0:T(8,128)S(1)}, f32[4,32,256]{2,1,0:T(8,128)S(1)}, u32[]{:S(2)}, u32[]{:S(2)}) collective-permute-start(f32[4,32,256]{2,1,0:T(8,128)S(1)} %pad_maximum_fusion.3), channel_id=1, source_target_pairs={{0,96},{8,104},{16,112},{24,120},{32,0},{40,8},{48,16},{56,24},{64... | collective-permute-start | bytes 393224 | tf_op jit(solution)/shard_map/ppermute | solution.py:455
  59.3 1.0 copy-start.3
  72.9 1.2 %copy-start.4 = (f32[2,16,32,256]{3,2,1,0:T(8,128)S(1)}, f32[2,16,32,256]{3,2,1,0:T(8,128)}, u32[]{:S(2)}) copy-start(f32[2,16,32,256]{3,2,1,0:T(8,128)} %copy-done.3) | copy-start | bytes 3145732
  78.1 19.8 %all-to-all-start.2 = ((f32[16,136,128]{2,1,0:T(8,128)}), f32[16,136,128]{2,1,0:T(8,128)S(1)}, u32[]{:S(2)}, u32[]{:S(2)}) async-start(f32[16,136,128]{2,1,0:T(8,128)} %shard_map.71), calls=%async_computation.2 | async-start | bytes 2228224 | tf_op jit(solution)/shard_map/all_to_all | solution.py:503
  81.8 10.9 %collective-permute-start.6 = (f32[32,512]{1,0:T(8,128)S(1)}, f32[32,512]{1,0:T(8,128)S(1)}, u32[]{:S(2)}, u32[]{:S(2)}) collective-permute-start(f32[32,512]{1,0:T(8,128)S(1)} %get-tuple-element.47), channel_id=1, source_target_pairs={{0,1},{1,2},{2,3},{3,4},{4,5},{5,6},{6,7},{7,0},{8,9},{9,10},{10,1... | collective-permute-start | bytes 196616 | tf_op jit(solution)/shard_map/ppermute | solution.py:505
  81.9 10.8 %collective-permute-start.7 = (f32[32,512]{1,0:T(8,128)S(1)}, f32[32,512]{1,0:T(8,128)S(1)}, u32[]{:S(2)}, u32[]{:S(2)}) collective-permute-start(f32[32,512]{1,0:T(8,128)S(1)} %get-tuple-element.48), channel_id=1, source_target_pairs={{0,2},{1,3},{2,4},{3,5},{4,6},{5,7},{6,0},{7,1},{8,10},{9,11},{10,... | collective-permute-start | bytes 196616 | tf_op jit(solution)/shard_map/ppermute | solution.py:505
  82.3 21.0 %collective-permute-start.8 = (f32[32,512]{1,0:T(8,128)S(1)}, f32[32,512]{1,0:T(8,128)S(1)}, u32[]{:S(2)}, u32[]{:S(2)}) collective-permute-start(f32[32,512]{1,0:T(8,128)S(1)} %get-tuple-element.49), channel_id=1, source_target_pairs={{0,3},{1,4},{2,5},{3,6},{4,7},{5,0},{6,1},{7,2},{8,11},{9,12},{10,... | collective-permute-start | bytes 196616 | tf_op jit(solution)/shard_map/ppermute | solution.py:505
  85.2 18.1 %collective-permute-start.9 = (f32[32,512]{1,0:T(8,128)S(1)}, f32[32,512]{1,0:T(8,128)S(1)}, u32[]{:S(2)}, u32[]{:S(2)}) collective-permute-start(f32[32,512]{1,0:T(8,128)S(1)} %get-tuple-element.50), channel_id=1, source_target_pairs={{0,4},{1,5},{2,6},{3,7},{4,0},{5,1},{6,2},{7,3},{8,12},{9,13},{10,... | collective-permute-start | bytes 196616 | tf_op jit(solution)/shard_map/ppermute | solution.py:505
  88.4 14.9 %collective-permute-start.10 = (f32[32,512]{1,0:T(8,128)S(1)}, f32[32,512]{1,0:T(8,128)S(1)}, u32[]{:S(2)}, u32[]{:S(2)}) collective-permute-start(f32[32,512]{1,0:T(8,128)S(1)} %get-tuple-element.51), channel_id=1, source_target_pairs={{0,5},{1,6},{2,7},{3,0},{4,1},{5,2},{6,3},{7,4},{8,13},{9,14},{10,... | collective-permute-start | bytes 196616 | tf_op jit(solution)/shard_map/ppermute | solution.py:505
  92.7 10.7 %collective-permute-start.11 = (f32[32,512]{1,0:T(8,128)S(1)}, f32[32,512]{1,0:T(8,128)S(1)}, u32[]{:S(2)}, u32[]{:S(2)}) collective-permute-start(f32[32,512]{1,0:T(8,128)S(1)} %get-tuple-element.52), channel_id=1, source_target_pairs={{0,6},{1,7},{2,0},{3,1},{4,2},{5,3},{6,4},{7,5},{8,14},{9,15},{10,... | collective-permute-start | bytes 196616 | tf_op jit(solution)/shard_map/ppermute | solution.py:505
  92.7 10.7 %collective-permute-start.12 = (f32[32,512]{1,0:T(8,128)S(1)}, f32[32,512]{1,0:T(8,128)S(1)}, u32[]{:S(2)}, u32[]{:S(2)}) collective-permute-start(f32[32,512]{1,0:T(8,128)S(1)} %get-tuple-element.53), channel_id=1, source_target_pairs={{0,7},{1,0},{2,1},{3,2},{4,3},{5,4},{6,5},{7,6},{8,15},{9,8},{10,9... | collective-permute-start | bytes 196616 | tf_op jit(solution)/shard_map/ppermute | solution.py:505
  98.5 11.1 %all-to-all-start.3 = ((f32[8,8,128]{2,1,0:T(8,128)}), f32[8,8,128]{2,1,0:T(8,128)S(1)}, u32[]{:S(2)}, u32[]{:S(2)}) async-start(f32[8,8,128]{2,1,0:T(8,128)} %shard_map.73), calls=%async_computation.3 | async-start | bytes 65536 | tf_op jit(solution)/shard_map/all_to_all | solution.py:509

commit v8 on v7

--- a/solution.py
+++ b/solution.py
@@ -15,8 +15,8 @@
 RADIX = 32
 SUB = 128
 PARTS = 3
-SPACE_GROUP = 16
-TIME_GROUP = 8
+SPACE_GROUP = 32
+TIME_GROUP = 16
 VMEM_LIMIT = 24 * 1024 * 1024
 
 
@@ -112,9 +112,10 @@
     return jnp.dot(left, right, preferred_element_type=jnp.float32)
 
 
-def transform(get, put, outputs, symbol, dft_ref, small_ref, a_ref, b_ref, group, after=None):
+def transform(get, put, outputs, symbol, dft_ref, small_ref, a_ref, b_ref, group):
     re_lanes, im_lanes = slice(0, SUB), slice(SUB, 2 * SUB)
-    for half in range(2):
+
+    def forward(half):
         rows = slice(8 * half, 8 * half + 8)
         planes = dft32(lambda m: get(m, half), -1)
         for k1 in range(RADIX):
@@ -125,24 +126,28 @@
                 re, im = re * c + im * s, im * c - re * s
             a_ref[k1, rows, re_lanes] = re
             a_ref[k1, rows, im_lanes] = im
-    for first in range(0, RADIX, group):
-        ks = slice(first, first + group)
-        got = product(a_ref[ks].reshape(group * 16, 2 * SUB), dft_ref)
-        got = got.reshape(group, 16, 2 * SUB)
-        re, im = got[:, :, re_lanes], got[:, :, im_lanes]
-        swapped = [
-            jnp.concatenate(symbol(o, ks, re, im)[::-1], axis=2).reshape(group * 16, 2 * SUB)
-            for o in range(outputs)
-        ]
-        got = product(jnp.concatenate(swapped, axis=0), dft_ref)
-        got = got.reshape(outputs, group, 16, 2 * SUB)
-        c = small_ref[0, ks][:, None, :]
-        s = small_ref[1, ks][:, None, :]
-        for o in range(outputs):
-            im2, re2 = got[o, :, :, re_lanes], got[o, :, :, im_lanes]
-            b_ref[o, ks, :, re_lanes] = re2 * c - im2 * s
-            b_ref[o, ks, :, im_lanes] = im2 * c + re2 * s
-    for half in range(2):
+
+    def middle(half):
+        rows = slice(8 * half, 8 * half + 8)
+        for first in range(0, RADIX, group):
+            ks = slice(first, first + group)
+            got = product(a_ref[ks, rows].reshape(group * 8, 2 * SUB), dft_ref)
+            got = got.reshape(group, 8, 2 * SUB)
+            re, im = got[:, :, re_lanes], got[:, :, im_lanes]
+            swapped = [
+                jnp.concatenate(symbol(o, ks, re, im)[::-1], axis=2).reshape(group * 8, 2 * SUB)
+                for o in range(outputs)
+            ]
+            got = product(jnp.concatenate(swapped, axis=0), dft_ref)
+            got = got.reshape(outputs, group, 8, 2 * SUB)
+            c = small_ref[0, ks][:, None, :]
+            s = small_ref[1, ks][:, None, :]
+            for o in range(outputs):
+                im2, re2 = got[o, :, :, re_lanes], got[o, :, :, im_lanes]
+                b_ref[o, ks, rows, re_lanes] = re2 * c - im2 * s
+                b_ref[o, ks, rows, im_lanes] = im2 * c + re2 * s
+
+    def inverse(half):
         rows = slice(8 * half, 8 * half + 8)
         outs = [
             dft32(lambda k: (b_ref[o, k, rows, re_lanes], b_ref[o, k, rows, im_lanes]), 1)
@@ -150,8 +155,13 @@
         ]
         for m in range(RADIX):
             put(m, half, [outs[o][m] for o in range(outputs)])
-        if after is not None:
-            after(half)
+
+    forward(0)
+    forward(1)
+    middle(0)
+    middle(1)
+    inverse(0)
+    inverse(1)
 
 
 def space_symbol(scale, small_ref):

time: 111 us -> 111 us (level)
  no operation moved by 1% of the time
where the time goes in v8:
time: 111 us; the launch traced here: 110 us
  starting transfers between devices  49.4 us (45%)
  waiting for transfers between devices  40.6 us (37%)
  Pallas kernels  14.8 us (13%)
  local copies, waits for them, and re-layouts  3 us (3%)
  between operations  2.33 us (2%)
    pallas_call x8, Pallas kernels, call(): pl.pallas_call(kernel, out_shape=[f32(*shape) for shape, _ in outs], in_s...  14.8 us
    all_to_all x1, waiting for transfers between devices, local(): received = lax.all_to_all(pieces.reshape(128, 16, 128), ('gx', 'ta'), 0, 0)  12.6 us
    ppermute x7, starting transfers between devices, local(): lax.ppermute(plane, 'gx', [(i, (i + d) % 8) for i in range(8)])  12.2 us
    all_to_all x1, waiting for transfers between devices, local(): rows_u = lax.all_to_all(field.reshape(rows), 'gx', 0, 0)  9.96 us
    all_to_all x1, starting transfers between devices, local(): received = lax.all_to_all(pieces.reshape(128, 16, 128), ('gx', 'ta'), 0, 0)  9.75 us
    ppermute x3, waiting for transfers between devices, along_y(): moved.append(lax.ppermute(piece, 'ta', shift_pairs(0, e)) if e else piece)  8.83 us
    all_to_all x1, starting transfers between devices, local(): rows_u = lax.all_to_all(field.reshape(rows), 'gx', 0, 0)  8.71 us
    ppermute x3, starting transfers between devices, along_y(): moved.append(lax.ppermute(piece, 'ta', shift_pairs(0, e)) if e else piece)  6.06 us
  transfers between devices with their start and end apart: 17, of which 6 were waited for; matrix products, arithmetic and copies ran while one was open for 1% of the time, Pallas kernels for 9%

profile of v8, /device:TPU:32, one launch (start us, length us, event | category | flops | bytes accessed | tf_op | source)
XLA Modules:
  0.0 110.3 jit_solution(3488455662683631714)
XLA Ops:
  0.6 8.7 %all-to-all-start = ((f32[8,32,512]{2,1,0:T(8,128)}), f32[8,32,512]{2,1,0:T(8,128)S(1)}, u32[]{:S(2)}, u32[]{:S(2)}) async-start(f32[8,32,512]{2,1,0:T(8,128)} %bitcast.27), calls=%async_computation | async-start | bytes 1048576 | tf_op jit(solution)/shard_map/all_to_all | solution.py:483
  9.4 0.0 copy-done
  9.4 0.2 shard_map.69
  9.6 0.7 dynamic-slice_bitcast_fusion
  10.3 2.8 %collective-permute-start.2 = (f32[4,32,256]{2,1,0:T(8,128)}, f32[4,32,256]{2,1,0:T(8,128)S(1)}, u32[]{:S(2)}, u32[]{:S(2)}) collective-permute-start(f32[4,32,256]{2,1,0:T(8,128)} %get-tuple-element.54), channel_id=1, source_target_pairs={{0,24},{8,0},{16,8},{24,16},{32,56},{40,32},{48,40},{56,48},{64,88... | collective-permute-start | bytes 393224 | tf_op jit(solution)/shard_map/ppermute | solution.py:455
  13.1 0.8 collective-permute-start.1
  13.9 0.9 collective-permute-start
  15.4 10.0 %all-to-all-done.u_ref = f32[8,32,512]{2,1,0:T(8,128)S(1)} async-done(((f32[8,32,512]{2,1,0:T(8,128)}), f32[8,32,512]{2,1,0:T(8,128)S(1)}, u32[]{:S(2)}, u32[]{:S(2)}) %all-to-all-start) | async-done | bytes 524320 | tf_op jit(solution)/shard_map/all_to_all | solution.py:483
  25.4 0.0 copy-done.2
  25.4 6.0 %shard_map.68 = (f32[8,16,16,128]{3,2,1,0:T(8,128)}, f32[32,512]{1,0:T(8,128)S(1)}, f32[32,512]{1,0:T(8,128)S(1)}, f32[32,512]{1,0:T(8,128)S(1)}, f32[32,512]{1,...) custom-call(f32[1]{0:T(128)S(6)} %div.18.scale_ref, ...), custom_call_target="tpu_custom_call" | custom-call | flops 8000000000 | bytes 2097152 | tf_op jit(solution)/shard_map/pallas_call | solution.py:429
  31.4 0.0 collective-permute-done.2
  31.4 0.0 collective-permute-done.1
  31.4 0.0 collective-permute-done
  31.4 9.7 %all-to-all-start.1 = ((f32[128,16,128]{2,1,0:T(8,128)}), f32[128,16,128]{2,1,0:T(8,128)S(1)}, u32[]{:S(2)}, u32[]{:S(2)}) async-start(f32[128,16,128]{2,1,0:T(8,128)} %bitcast.13), calls=%async_computation.1 | async-start | bytes 2097152 | tf_op jit(solution)/shard_map/all_to_all | solution.py:495
  41.4 1.6 %collective-permute-start.3 = (f32[4,32,256]{2,1,0:T(8,128)S(1)}, f32[4,32,256]{2,1,0:T(8,128)S(1)}, u32[]{:S(2)}, u32[]{:S(2)}) collective-permute-start(f32[4,32,256]{2,1,0:T(8,128)S(1)} %pad_maximum_fusion.1), channel_id=1, source_target_pairs={{0,32},{8,40},{16,48},{24,56},{32,64},{40,72},{48,80},{56,88},{64,... | collective-permute-start | bytes 393224 | tf_op jit(solution)/shard_map/ppermute | solution.py:465
  42.9 2.8 %collective-permute-start.4 = (f32[4,32,256]{2,1,0:T(8,128)S(1)}, f32[4,32,256]{2,1,0:T(8,128)S(1)}, u32[]{:S(2)}, u32[]{:S(2)}) collective-permute-start(f32[4,32,256]{2,1,0:T(8,128)S(1)} %pad_maximum_fusion.2), channel_id=1, source_target_pairs={{0,64},{8,72},{16,80},{24,88},{32,96},{40,104},{48,112},{56,120},{... | collective-permute-start | bytes 393224 | tf_op jit(solution)/shard_map/ppermute | solution.py:465
  45.8 1.7 %collective-permute-start.5 = (f32[4,32,256]{2,1,0:T(8,128)S(1)}, f32[4,32,256]{2,1,0:T(8,128)S(1)}, u32[]{:S(2)}, u32[]{:S(2)}) collective-permute-start(f32[4,32,256]{2,1,0:T(8,128)S(1)} %pad_maximum_fusion.3), channel_id=1, source_target_pairs={{0,96},{8,104},{16,112},{24,120},{32,0},{40,8},{48,16},{56,24},{64... | collective-permute-start | bytes 393224 | tf_op jit(solution)/shard_map/ppermute | solution.py:465
  47.5 0.1 pad_add_fusion.place_ref
  48.2 2.4 %collective-permute-done.3 = f32[4,32,256]{2,1,0:T(8,128)S(1)} collective-permute-done((f32[4,32,256]{2,1,0:T(8,128)S(1)}, f32[4,32,256]{2,1,0:T(8,128)S(1)}, u32[]{:S(2)}, u32[]{:S(2)}) %collective-permute-start.3) | collective-permute-done | bytes 131104 | tf_op jit(solution)/shard_map/ppermute | solution.py:465
  50.6 6.4 %collective-permute-done.4 = f32[4,32,256]{2,1,0:T(8,128)S(1)} collective-permute-done((f32[4,32,256]{2,1,0:T(8,128)S(1)}, f32[4,32,256]{2,1,0:T(8,128)S(1)}, u32[]{:S(2)}, u32[]{:S(2)}) %collective-permute-start.4) | collective-permute-done | bytes 131104 | tf_op jit(solution)/shard_map/ppermute | solution.py:465
  57.1 0.0 collective-permute-done.5
  57.1 2.0 %shard_map.70.uq_ref = f32[2,16,32,256]{3,2,1,0:T(8,128)S(1)} custom-call(f32[1]{0:T(128)S(6)} %div.14.scale_ref, s32[2]{0:T(128)S(1)} %pad_add_fusion.place_ref, f32[4,4,32,256]{3,2,1,0:T(8,128)S(1)} %pad_maximum_fusion.moved_ref, bf16[3,256,256]{2,1,0:T(8,128)(2,1)S(1)} %copy-done.1, f32[4,32,128]{2,1,0:T(8,128)S(1)} %copy-done.2), custom_call_target="tpu_custom_call" | custom-call | flops 2000000000 | bytes 2097152 | tf_op jit(solution)/shard_map/pallas_call | solution.py:429
  59.1 1.0 copy-done.3
  60.1 12.6 %all-to-all-done.1.recv_ref = f32[128,16,128]{2,1,0:T(8,128)S(1)} async-done(((f32[128,16,128]{2,1,0:T(8,128)}), f32[128,16,128]{2,1,0:T(8,128)S(1)}, u32[]{:S(2)}, u32[]{:S(2)}) %all-to-all-start.1) | async-done | bytes 1048608 | tf_op jit(solution)/shard_map/all_to_all | solution.py:495
  72.7 1.2 %copy-done.4 = f32[2,16,32,256]{3,2,1,0:T(8,128)S(1)} copy-done((f32[2,16,32,256]{3,2,1,0:T(8,128)S(1)}, f32[2,16,32,256]{3,2,1,0:T(8,128)}, u32[]{:S(2)}) %copy-start.4) | copy-done | bytes 1048600
  73.9 3.8 %shard_map.71 = f32[16,136,128]{2,1,0:T(8,128)} custom-call(f32[1]{0:T(128)S(6)} %div.14.scale_ref, f32[2,16,32,256]{3,2,1,0:T(8,128)S(1)} %copy-done.4, f32[128,16,128]{2,1,0:T(8,128)S(1)} %all-to-all-done.1.recv_ref, f32[8,128]{1,0:T(8,128)S(1)} %get-tuple-element.34.p_cost_ref, bf16[3,256,256]{2,1,0:T(8,128)(2,1)S(1)} %copy-done.1, ...), custom_call_target="tpu_custom_call" | custom-call | flops 4000000000 | bytes 2097152 | tf_op jit(solution)/shard_map/pallas_call | solution.py:429
  77.8 3.7 %all-to-all-start.2 = ((f32[16,136,128]{2,1,0:T(8,128)}), f32[16,136,128]{2,1,0:T(8,128)S(1)}, u32[]{:S(2)}, u32[]{:S(2)}) async-start(f32[16,136,128]{2,1,0:T(8,128)} %shard_map.71), calls=%async_computation.2 | async-start | bytes 2228224 | tf_op jit(solution)/shard_map/all_to_all | solution.py:513
  81.5 0.1 collective-permute-start.6
  81.6 0.4 collective-permute-start.7
  82.0 2.9 %collective-permute-start.8 = (f32[32,512]{1,0:T(8,128)S(1)}, f32[32,512]{1,0:T(8,128)S(1)}, u32[]{:S(2)}, u32[]{:S(2)}) collective-permute-start(f32[32,512]{1,0:T(8,128)S(1)} %get-tuple-element.49), channel_id=1, source_target_pairs={{0,3},{1,4},{2,5},{3,6},{4,7},{5,0},{6,1},{7,2},{8,11},{9,12},{10,... | collective-permute-start | bytes 196616 | tf_op jit(solution)/shard_map/ppermute | solution.py:515
  84.9 3.2 %collective-permute-start.9 = (f32[32,512]{1,0:T(8,128)S(1)}, f32[32,512]{1,0:T(8,128)S(1)}, u32[]{:S(2)}, u32[]{:S(2)}) collective-permute-start(f32[32,512]{1,0:T(8,128)S(1)} %get-tuple-element.50), channel_id=1, source_target_pairs={{0,4},{1,5},{2,6},{3,7},{4,0},{5,1},{6,2},{7,3},{8,12},{9,13},{10,... | collective-permute-start | bytes 196616 | tf_op jit(solution)/shard_map/ppermute | solution.py:515
  88.1 4.2 %collective-permute-start.10 = (f32[32,512]{1,0:T(8,128)S(1)}, f32[32,512]{1,0:T(8,128)S(1)}, u32[]{:S(2)}, u32[]{:S(2)}) collective-permute-start(f32[32,512]{1,0:T(8,128)S(1)} %get-tuple-element.51), channel_id=1, source_target_pairs={{0,5},{1,6},{2,7},{3,0},{4,1},{5,2},{6,3},{7,4},{8,13},{9,14},{10,... | collective-permute-start | bytes 196616 | tf_op jit(solution)/shard_map/ppermute | solution.py:515
  92.3 0.0 collective-permute-done.6.refs_1_
  92.4 0.0 collective-permute-start.11
  92.4 0.0 collective-permute-done.7.refs_2_
  92.4 1.3 %collective-permute-start.12 = (f32[32,512]{1,0:T(8,128)S(1)}, f32[32,512]{1,0:T(8,128)S(1)}, u32[]{:S(2)}, u32[]{:S(2)}) collective-permute-start(f32[32,512]{1,0:T(8,128)S(1)} %get-tuple-element.53), channel_id=1, source_target_pairs={{0,7},{1,0},{2,1},{3,2},{4,3},{5,4},{6,5},{7,6},{8,15},{9,8},{10,9... | collective-permute-start | bytes 196616 | tf_op jit(solution)/shard_map/ppermute | solution.py:515
  93.7 3.9 %all-to-all-done.2.recv_ref = f32[16,136,128]{2,1,0:T(8,128)S(1)} async-done(((f32[16,136,128]{2,1,0:T(8,128)}), f32[16,136,128]{2,1,0:T(8,128)S(1)}, u32[]{:S(2)}, u32[]{:S(2)}) %all-to-all-start.2) | async-done | bytes 1114144 | tf_op jit(solution)/shard_map/all_to_all | solution.py:513
  97.5 0.6 shard_map.73
  98.2 4.5 %all-to-all-start.3 = ((f32[8,8,128]{2,1,0:T(8,128)}), f32[8,8,128]{2,1,0:T(8,128)S(1)}, u32[]{:S(2)}, u32[]{:S(2)}) async-start(f32[8,8,128]{2,1,0:T(8,128)} %shard_map.73), calls=%async_computation.3 | async-start | bytes 65536 | tf_op jit(solution)/shard_map/all_to_all | solution.py:519
  102.7 0.3 shard_map.72
  103.0 0.0 collective-permute-done.8.refs_3_
  103.1 0.0 collective-permute-done.9.refs_4_
  103.1 0.0 collective-permute-done.10.refs_5_
  103.1 0.0 collective-permute-done.11.refs_6_
  103.1 0.0 collective-permute-done.12.refs_7_
  103.1 0.9 shard_map.75
  104.0 5.3 %all-to-all-done.3.sums_ref = f32[8,8,128]{2,1,0:T(8,128)S(1)} async-done(((f32[8,8,128]{2,1,0:T(8,128)}), f32[8,8,128]{2,1,0:T(8,128)S(1)}, u32[]{:S(2)}, u32[]{:S(2)}) %all-to-all-start.3) | async-done | bytes 32800 | tf_op jit(solution)/shard_map/all_to_all | solution.py:519
  109.3 1.0 shard_map.74
  (14 shorter events, 0.2 us)
Async XLA Ops:
  0.6 8.7 %copy-start = (f32[256,512]{1,0:T(8,128)S(1)}, f32[256,512]{1,0:T(8,128)}, u32[]{:S(2)}) copy-start(f32[256,512]{1,0:T(8,128)} %u_ref.3) | copy-start | bytes 1572868
  0.6 24.8 %all-to-all-start = ((f32[8,32,512]{2,1,0:T(8,128)}), f32[8,32,512]{2,1,0:T(8,128)S(1)}, u32[]{:S(2)}, u32[]{:S(2)}) async-start(f32[8,32,512]{2,1,0:T(8,128)} %bitcast.27), calls=%async_computation | async-start | bytes 1048576 | tf_op jit(solution)/shard_map/all_to_all | solution.py:483
  9.4 16.0 %copy-start.1 = (bf16[3,256,256]{2,1,0:T(8,128)(2,1)S(1)}, bf16[3,256,256]{2,1,0:T(8,128)(2,1)}, u32[]{:S(2)}) copy-start(bf16[3,256,256]{2,1,0:T(8,128)(2,1)} %constant.144.clone.dft_ref) | copy-start | bytes 1179652
  9.4 16.0 %copy-start.2 = (f32[4,32,128]{2,1,0:T(8,128)S(1)}, f32[4,32,128]{2,1,0:T(8,128)}, u32[]{:S(2)}) copy-start(f32[4,32,128]{2,1,0:T(8,128)} %constant.145.clone.small_ref) | copy-start | bytes 196612
  10.3 21.1 %collective-permute-start.2 = (f32[4,32,256]{2,1,0:T(8,128)}, f32[4,32,256]{2,1,0:T(8,128)S(1)}, u32[]{:S(2)}, u32[]{:S(2)}) collective-permute-start(f32[4,32,256]{2,1,0:T(8,128)} %get-tuple-element.54), channel_id=1, source_target_pairs={{0,24},{8,0},{16,8},{24,16},{32,56},{40,32},{48,40},{56,48},{64,88... | collective-permute-start | bytes 393224 | tf_op jit(solution)/shard_map/ppermute | solution.py:455
  13.1 18.4 %collective-permute-start.1 = (f32[4,32,256]{2,1,0:T(8,128)S(1)}, f32[4,32,256]{2,1,0:T(8,128)S(1)}, u32[]{:S(2)}, u32[]{:S(2)}) collective-permute-start(f32[4,32,256]{2,1,0:T(8,128)S(1)} %get-tuple-element.55), channel_id=1, source_target_pairs={{0,16},{8,24},{16,0},{24,8},{32,48},{40,56},{48,32},{56,40},{64,80... | collective-permute-start | bytes 393224 | tf_op jit(solution)/shard_map/ppermute | solution.py:455
  13.9 17.6 %collective-permute-start = (f32[4,32,256]{2,1,0:T(8,128)S(1)}, f32[4,32,256]{2,1,0:T(8,128)S(1)}, u32[]{:S(2)}, u32[]{:S(2)}) collective-permute-start(f32[4,32,256]{2,1,0:T(8,128)S(1)} %get-tuple-element.56), channel_id=1, source_target_pairs={{0,8},{8,16},{16,24},{24,0},{32,40},{40,48},{48,56},{56,32},{64,72... | collective-permute-start | bytes 393224 | tf_op jit(solution)/shard_map/ppermute | solution.py:455
  31.4 41.3 %all-to-all-start.1 = ((f32[128,16,128]{2,1,0:T(8,128)}), f32[128,16,128]{2,1,0:T(8,128)S(1)}, u32[]{:S(2)}, u32[]{:S(2)}) async-start(f32[128,16,128]{2,1,0:T(8,128)} %bitcast.13), calls=%async_computation.1 | async-start | bytes 2097152 | tf_op jit(solution)/shard_map/all_to_all | solution.py:495
  41.4 9.3 %collective-permute-start.3 = (f32[4,32,256]{2,1,0:T(8,128)S(1)}, f32[4,32,256]{2,1,0:T(8,128)S(1)}, u32[]{:S(2)}, u32[]{:S(2)}) collective-permute-start(f32[4,32,256]{2,1,0:T(8,128)S(1)} %pad_maximum_fusion.1), channel_id=1, source_target_pairs={{0,32},{8,40},{16,48},{24,56},{32,64},{40,72},{48,80},{56,88},{64,... | collective-permute-start | bytes 393224 | tf_op jit(solution)/shard_map/ppermute | solution.py:465
  42.9 14.1 %collective-permute-start.4 = (f32[4,32,256]{2,1,0:T(8,128)S(1)}, f32[4,32,256]{2,1,0:T(8,128)S(1)}, u32[]{:S(2)}, u32[]{:S(2)}) collective-permute-start(f32[4,32,256]{2,1,0:T(8,128)S(1)} %pad_maximum_fusion.2), channel_id=1, source_target_pairs={{0,64},{8,72},{16,80},{24,88},{32,96},{40,104},{48,112},{56,120},{... | collective-permute-start | bytes 393224 | tf_op jit(solution)/shard_map/ppermute | solution.py:465
  45.8 11.3 %collective-permute-start.5 = (f32[4,32,256]{2,1,0:T(8,128)S(1)}, f32[4,32,256]{2,1,0:T(8,128)S(1)}, u32[]{:S(2)}, u32[]{:S(2)}) collective-permute-start(f32[4,32,256]{2,1,0:T(8,128)S(1)} %pad_maximum_fusion.3), channel_id=1, source_target_pairs={{0,96},{8,104},{16,112},{24,120},{32,0},{40,8},{48,16},{56,24},{64... | collective-permute-start | bytes 393224 | tf_op jit(solution)/shard_map/ppermute | solution.py:465
  59.1 1.0 copy-start.3
  72.7 1.2 %copy-start.4 = (f32[2,16,32,256]{3,2,1,0:T(8,128)S(1)}, f32[2,16,32,256]{3,2,1,0:T(8,128)}, u32[]{:S(2)}) copy-start(f32[2,16,32,256]{3,2,1,0:T(8,128)} %copy-done.3) | copy-start | bytes 3145732
  77.8 19.8 %all-to-all-start.2 = ((f32[16,136,128]{2,1,0:T(8,128)}), f32[16,136,128]{2,1,0:T(8,128)S(1)}, u32[]{:S(2)}, u32[]{:S(2)}) async-start(f32[16,136,128]{2,1,0:T(8,128)} %shard_map.71), calls=%async_computation.2 | async-start | bytes 2228224 | tf_op jit(solution)/shard_map/all_to_all | solution.py:513
  81.5 10.9 %collective-permute-start.6 = (f32[32,512]{1,0:T(8,128)S(1)}, f32[32,512]{1,0:T(8,128)S(1)}, u32[]{:S(2)}, u32[]{:S(2)}) collective-permute-start(f32[32,512]{1,0:T(8,128)S(1)} %get-tuple-element.47), channel_id=1, source_target_pairs={{0,1},{1,2},{2,3},{3,4},{4,5},{5,6},{6,7},{7,0},{8,9},{9,10},{10,1... | collective-permute-start | bytes 196616 | tf_op jit(solution)/shard_map/ppermute | solution.py:515
  81.6 10.8 %collective-permute-start.7 = (f32[32,512]{1,0:T(8,128)S(1)}, f32[32,512]{1,0:T(8,128)S(1)}, u32[]{:S(2)}, u32[]{:S(2)}) collective-permute-start(f32[32,512]{1,0:T(8,128)S(1)} %get-tuple-element.48), channel_id=1, source_target_pairs={{0,2},{1,3},{2,4},{3,5},{4,6},{5,7},{6,0},{7,1},{8,10},{9,11},{10,... | collective-permute-start | bytes 196616 | tf_op jit(solution)/shard_map/ppermute | solution.py:515
  82.0 21.0 %collective-permute-start.8 = (f32[32,512]{1,0:T(8,128)S(1)}, f32[32,512]{1,0:T(8,128)S(1)}, u32[]{:S(2)}, u32[]{:S(2)}) collective-permute-start(f32[32,512]{1,0:T(8,128)S(1)} %get-tuple-element.49), channel_id=1, source_target_pairs={{0,3},{1,4},{2,5},{3,6},{4,7},{5,0},{6,1},{7,2},{8,11},{9,12},{10,... | collective-permute-start | bytes 196616 | tf_op jit(solution)/shard_map/ppermute | solution.py:515
  84.9 18.1 %collective-permute-start.9 = (f32[32,512]{1,0:T(8,128)S(1)}, f32[32,512]{1,0:T(8,128)S(1)}, u32[]{:S(2)}, u32[]{:S(2)}) collective-permute-start(f32[32,512]{1,0:T(8,128)S(1)} %get-tuple-element.50), channel_id=1, source_target_pairs={{0,4},{1,5},{2,6},{3,7},{4,0},{5,1},{6,2},{7,3},{8,12},{9,13},{10,... | collective-permute-start | bytes 196616 | tf_op jit(solution)/shard_map/ppermute | solution.py:515
  88.1 14.9 %collective-permute-start.10 = (f32[32,512]{1,0:T(8,128)S(1)}, f32[32,512]{1,0:T(8,128)S(1)}, u32[]{:S(2)}, u32[]{:S(2)}) collective-permute-start(f32[32,512]{1,0:T(8,128)S(1)} %get-tuple-element.51), channel_id=1, source_target_pairs={{0,5},{1,6},{2,7},{3,0},{4,1},{5,2},{6,3},{7,4},{8,13},{9,14},{10,... | collective-permute-start | bytes 196616 | tf_op jit(solution)/shard_map/ppermute | solution.py:515
  92.4 10.7 %collective-permute-start.11 = (f32[32,512]{1,0:T(8,128)S(1)}, f32[32,512]{1,0:T(8,128)S(1)}, u32[]{:S(2)}, u32[]{:S(2)}) collective-permute-start(f32[32,512]{1,0:T(8,128)S(1)} %get-tuple-element.52), channel_id=1, source_target_pairs={{0,6},{1,7},{2,0},{3,1},{4,2},{5,3},{6,4},{7,5},{8,14},{9,15},{10,... | collective-permute-start | bytes 196616 | tf_op jit(solution)/shard_map/ppermute | solution.py:515
  92.4 10.7 %collective-permute-start.12 = (f32[32,512]{1,0:T(8,128)S(1)}, f32[32,512]{1,0:T(8,128)S(1)}, u32[]{:S(2)}, u32[]{:S(2)}) collective-permute-start(f32[32,512]{1,0:T(8,128)S(1)} %get-tuple-element.53), channel_id=1, source_target_pairs={{0,7},{1,0},{2,1},{3,2},{4,3},{5,4},{6,5},{7,6},{8,15},{9,8},{10,9... | collective-permute-start | bytes 196616 | tf_op jit(solution)/shard_map/ppermute | solution.py:515
  98.2 11.1 %all-to-all-start.3 = ((f32[8,8,128]{2,1,0:T(8,128)}), f32[8,8,128]{2,1,0:T(8,128)S(1)}, u32[]{:S(2)}, u32[]{:S(2)}) async-start(f32[8,8,128]{2,1,0:T(8,128)} %shard_map.73), calls=%async_computation.3 | async-start | bytes 65536 | tf_op jit(solution)/shard_map/all_to_all | solution.py:519

commit v9 on v8

--- a/solution.py
+++ b/solution.py
@@ -409,11 +409,21 @@
         r_ref[rows, :] = q_ref[rows, :] + refs[d][...]
 
 
-def update_kernel(u_ref, g_ref, sums_ref, out_ref):
+def update_kernel(u_ref, g_ref, sums_ref, out_ref, new_ref, sems):
     sums = jnp.sum(sums_ref[...], axis=0)
     cost = jnp.sum(sums[0:1, :], axis=1, keepdims=True)
     norm = jnp.sum(sums[1:2, :], axis=1, keepdims=True)
-    out_ref[...] = u_ref[...] - (cost / (norm + GRAD_EPS)) * g_ref[...]
+    step = cost / (norm + GRAD_EPS)
+    copies = []
+    for part in range(4):
+        rows = slice(64 * part, 64 * part + 64)
+        new_ref[rows, :] = u_ref[rows, :] - step * g_ref[rows, :]
+        copies.append(
+            pltpu.make_async_copy(new_ref.at[rows, :], out_ref.at[rows, :], sems.at[part])
+        )
+        copies[-1].start()
+    for copy in copies:
+        copy.wait()
 
 
 VM = pl.BlockSpec(memory_space=pltpu.VMEM)
@@ -524,7 +534,11 @@
         [z_place, (block_q, VM)] + [(plane, VM) for plane in p_block],
     )
     (updated,) = call(
-        update_kernel, [((256, 512), VM)], [(field, VM), (block_g, VM), (sums, VM)]
+        update_kernel,
+        [((256, 512), HB)],
+        [(field, VM), (block_g, VM), (sums, VM)],
+        [(256, 512)],
+        [4],
     )
     return updated, residual
 

time: 111 us -> 111 us (level)
  no operation moved by 1% of the time
where the time goes in v9:
time: 111 us; the launch traced here: 110 us
  starting transfers between devices  49.4 us (45%)
  waiting for transfers between devices  40.6 us (37%)
  Pallas kernels  14.8 us (13%)
  local copies, waits for them, and re-layouts  3 us (3%)
  between operations  2.49 us (2%)
    pallas_call x8, Pallas kernels, call(): pl.pallas_call(kernel, out_shape=[f32(*shape) for shape, _ in outs], in_s...  14.8 us
    all_to_all x1, waiting for transfers between devices, local(): received = lax.all_to_all(pieces.reshape(128, 16, 128), ('gx', 'ta'), 0, 0)  12.6 us
    ppermute x7, starting transfers between devices, local(): lax.ppermute(plane, 'gx', [(i, (i + d) % 8) for i in range(8)])  12.2 us
    all_to_all x1, waiting for transfers between devices, local(): rows_u = lax.all_to_all(field.reshape(rows), 'gx', 0, 0)  9.96 us
    all_to_all x1, starting transfers between devices, local(): received = lax.all_to_all(pieces.reshape(128, 16, 128), ('gx', 'ta'), 0, 0)  9.75 us
    ppermute x3, waiting for transfers between devices, along_y(): moved.append(lax.ppermute(piece, 'ta', shift_pairs(0, e)) if e else piece)  8.83 us
    all_to_all x1, starting transfers between devices, local(): rows_u = lax.all_to_all(field.reshape(rows), 'gx', 0, 0)  8.71 us
    ppermute x3, starting transfers between devices, along_y(): moved.append(lax.ppermute(piece, 'ta', shift_pairs(0, e)) if e else piece)  6.06 us
  transfers between devices with their start and end apart: 17, of which 6 were waited for; matrix products, arithmetic and copies ran while one was open for 1% of the time, Pallas kernels for 9%

profile of v9, /device:TPU:32, one launch (start us, length us, event | category | flops | bytes accessed | tf_op | source)
XLA Modules:
  0.0 110.4 jit_solution(3546070450844072903)
XLA Ops:
  0.6 0.0 copy-start
  0.6 8.7 %all-to-all-start = ((f32[8,32,512]{2,1,0:T(8,128)}), f32[8,32,512]{2,1,0:T(8,128)S(1)}, u32[]{:S(2)}, u32[]{:S(2)}) async-start(f32[8,32,512]{2,1,0:T(8,128)} %bitcast.27), calls=%async_computation | async-start | bytes 1048576 | tf_op jit(solution)/shard_map/all_to_all | solution.py:493
  9.4 0.2 shard_map.69
  9.6 0.7 dynamic-slice_bitcast_fusion
  10.3 2.8 %collective-permute-start.2 = (f32[4,32,256]{2,1,0:T(8,128)}, f32[4,32,256]{2,1,0:T(8,128)S(1)}, u32[]{:S(2)}, u32[]{:S(2)}) collective-permute-start(f32[4,32,256]{2,1,0:T(8,128)} %get-tuple-element.54), channel_id=1, source_target_pairs={{0,24},{8,0},{16,8},{24,16},{32,56},{40,32},{48,40},{56,48},{64,88... | collective-permute-start | bytes 393224 | tf_op jit(solution)/shard_map/ppermute | solution.py:465
  13.1 0.8 collective-permute-start.1
  13.9 0.9 collective-permute-start
  15.4 10.0 %all-to-all-done.u_ref = f32[8,32,512]{2,1,0:T(8,128)S(1)} async-done(((f32[8,32,512]{2,1,0:T(8,128)}), f32[8,32,512]{2,1,0:T(8,128)S(1)}, u32[]{:S(2)}, u32[]{:S(2)}) %all-to-all-start) | async-done | bytes 524320 | tf_op jit(solution)/shard_map/all_to_all | solution.py:493
  25.4 0.0 copy-done.1
  25.4 6.0 %shard_map.68 = (f32[8,16,16,128]{3,2,1,0:T(8,128)}, f32[32,512]{1,0:T(8,128)S(1)}, f32[32,512]{1,0:T(8,128)S(1)}, f32[32,512]{1,0:T(8,128)S(1)}, f32[32,512]{1,...) custom-call(f32[1]{0:T(128)S(6)} %div.18.scale_ref, ...), custom_call_target="tpu_custom_call" | custom-call | flops 8000000000 | bytes 2097152 | tf_op jit(solution)/shard_map/pallas_call | solution.py:439
  31.4 0.0 collective-permute-done.2
  31.4 0.0 collective-permute-done.1
  31.4 0.0 collective-permute-done
  31.4 9.7 %all-to-all-start.1 = ((f32[128,16,128]{2,1,0:T(8,128)}), f32[128,16,128]{2,1,0:T(8,128)S(1)}, u32[]{:S(2)}, u32[]{:S(2)}) async-start(f32[128,16,128]{2,1,0:T(8,128)} %bitcast.13), calls=%async_computation.1 | async-start | bytes 2097152 | tf_op jit(solution)/shard_map/all_to_all | solution.py:505
  41.4 1.6 %collective-permute-start.3 = (f32[4,32,256]{2,1,0:T(8,128)S(1)}, f32[4,32,256]{2,1,0:T(8,128)S(1)}, u32[]{:S(2)}, u32[]{:S(2)}) collective-permute-start(f32[4,32,256]{2,1,0:T(8,128)S(1)} %pad_maximum_fusion.1), channel_id=1, source_target_pairs={{0,32},{8,40},{16,48},{24,56},{32,64},{40,72},{48,80},{56,88},{64,... | collective-permute-start | bytes 393224 | tf_op jit(solution)/shard_map/ppermute | solution.py:475
  42.9 2.8 %collective-permute-start.4 = (f32[4,32,256]{2,1,0:T(8,128)S(1)}, f32[4,32,256]{2,1,0:T(8,128)S(1)}, u32[]{:S(2)}, u32[]{:S(2)}) collective-permute-start(f32[4,32,256]{2,1,0:T(8,128)S(1)} %pad_maximum_fusion.2), channel_id=1, source_target_pairs={{0,64},{8,72},{16,80},{24,88},{32,96},{40,104},{48,112},{56,120},{... | collective-permute-start | bytes 393224 | tf_op jit(solution)/shard_map/ppermute | solution.py:475
  45.8 1.7 %collective-permute-start.5 = (f32[4,32,256]{2,1,0:T(8,128)S(1)}, f32[4,32,256]{2,1,0:T(8,128)S(1)}, u32[]{:S(2)}, u32[]{:S(2)}) collective-permute-start(f32[4,32,256]{2,1,0:T(8,128)S(1)} %pad_maximum_fusion.3), channel_id=1, source_target_pairs={{0,96},{8,104},{16,112},{24,120},{32,0},{40,8},{48,16},{56,24},{64... | collective-permute-start | bytes 393224 | tf_op jit(solution)/shard_map/ppermute | solution.py:475
  47.5 0.1 pad_add_fusion.place_ref
  48.2 2.4 %collective-permute-done.3 = f32[4,32,256]{2,1,0:T(8,128)S(1)} collective-permute-done((f32[4,32,256]{2,1,0:T(8,128)S(1)}, f32[4,32,256]{2,1,0:T(8,128)S(1)}, u32[]{:S(2)}, u32[]{:S(2)}) %collective-permute-start.3) | collective-permute-done | bytes 131104 | tf_op jit(solution)/shard_map/ppermute | solution.py:475
  50.6 6.4 %collective-permute-done.4 = f32[4,32,256]{2,1,0:T(8,128)S(1)} collective-permute-done((f32[4,32,256]{2,1,0:T(8,128)S(1)}, f32[4,32,256]{2,1,0:T(8,128)S(1)}, u32[]{:S(2)}, u32[]{:S(2)}) %collective-permute-start.4) | collective-permute-done | bytes 131104 | tf_op jit(solution)/shard_map/ppermute | solution.py:475
  57.1 0.0 collective-permute-done.5
  57.1 2.0 %shard_map.70.uq_ref = f32[2,16,32,256]{3,2,1,0:T(8,128)S(1)} custom-call(f32[1]{0:T(128)S(6)} %div.14.scale_ref, s32[2]{0:T(128)S(1)} %pad_add_fusion.place_ref, f32[4,4,32,256]{3,2,1,0:T(8,128)S(1)} %pad_maximum_fusion.moved_ref, bf16[3,256,256]{2,1,0:T(8,128)(2,1)S(1)} %copy-done.1, f32[4,32,128]{2,1,0:T(8,128)S(1)} %copy-done.2), custom_call_target="tpu_custom_call" | custom-call | flops 2000000000 | bytes 2097152 | tf_op jit(solution)/shard_map/pallas_call | solution.py:439
  59.1 1.0 copy-done.3
  60.1 12.6 %all-to-all-done.1.recv_ref = f32[128,16,128]{2,1,0:T(8,128)S(1)} async-done(((f32[128,16,128]{2,1,0:T(8,128)}), f32[128,16,128]{2,1,0:T(8,128)S(1)}, u32[]{:S(2)}, u32[]{:S(2)}) %all-to-all-start.1) | async-done | bytes 1048608 | tf_op jit(solution)/shard_map/all_to_all | solution.py:505
  72.7 1.2 %copy-done.4 = f32[2,16,32,256]{3,2,1,0:T(8,128)S(1)} copy-done((f32[2,16,32,256]{3,2,1,0:T(8,128)S(1)}, f32[2,16,32,256]{3,2,1,0:T(8,128)}, u32[]{:S(2)}) %copy-start.4) | copy-done | bytes 1048600
  73.9 3.8 %shard_map.71 = f32[16,136,128]{2,1,0:T(8,128)} custom-call(f32[1]{0:T(128)S(6)} %div.14.scale_ref, f32[2,16,32,256]{3,2,1,0:T(8,128)S(1)} %copy-done.4, f32[128,16,128]{2,1,0:T(8,128)S(1)} %all-to-all-done.1.recv_ref, f32[8,128]{1,0:T(8,128)S(1)} %get-tuple-element.34.p_cost_ref, bf16[3,256,256]{2,1,0:T(8,128)(2,1)S(1)} %copy-done.1, ...), custom_call_target="tpu_custom_call" | custom-call | flops 4000000000 | bytes 2097152 | tf_op jit(solution)/shard_map/pallas_call | solution.py:439
  77.8 3.7 %all-to-all-start.2 = ((f32[16,136,128]{2,1,0:T(8,128)}), f32[16,136,128]{2,1,0:T(8,128)S(1)}, u32[]{:S(2)}, u32[]{:S(2)}) async-start(f32[16,136,128]{2,1,0:T(8,128)} %shard_map.71), calls=%async_computation.2 | async-start | bytes 2228224 | tf_op jit(solution)/shard_map/all_to_all | solution.py:523
  81.5 0.1 collective-permute-start.6
  81.6 0.4 collective-permute-start.7
  82.0 2.9 %collective-permute-start.8 = (f32[32,512]{1,0:T(8,128)S(1)}, f32[32,512]{1,0:T(8,128)S(1)}, u32[]{:S(2)}, u32[]{:S(2)}) collective-permute-start(f32[32,512]{1,0:T(8,128)S(1)} %get-tuple-element.49), channel_id=1, source_target_pairs={{0,3},{1,4},{2,5},{3,6},{4,7},{5,0},{6,1},{7,2},{8,11},{9,12},{10,... | collective-permute-start | bytes 196616 | tf_op jit(solution)/shard_map/ppermute | solution.py:525
  84.9 3.2 %collective-permute-start.9 = (f32[32,512]{1,0:T(8,128)S(1)}, f32[32,512]{1,0:T(8,128)S(1)}, u32[]{:S(2)}, u32[]{:S(2)}) collective-permute-start(f32[32,512]{1,0:T(8,128)S(1)} %get-tuple-element.50), channel_id=1, source_target_pairs={{0,4},{1,5},{2,6},{3,7},{4,0},{5,1},{6,2},{7,3},{8,12},{9,13},{10,... | collective-permute-start | bytes 196616 | tf_op jit(solution)/shard_map/ppermute | solution.py:525
  88.1 4.2 %collective-permute-start.10 = (f32[32,512]{1,0:T(8,128)S(1)}, f32[32,512]{1,0:T(8,128)S(1)}, u32[]{:S(2)}, u32[]{:S(2)}) collective-permute-start(f32[32,512]{1,0:T(8,128)S(1)} %get-tuple-element.51), channel_id=1, source_target_pairs={{0,5},{1,6},{2,7},{3,0},{4,1},{5,2},{6,3},{7,4},{8,13},{9,14},{10,... | collective-permute-start | bytes 196616 | tf_op jit(solution)/shard_map/ppermute | solution.py:525
  92.3 0.0 collective-permute-done.6.refs_1_
  92.4 0.0 collective-permute-start.11
  92.4 0.0 collective-permute-done.7.refs_2_
  92.4 1.3 %collective-permute-start.12 = (f32[32,512]{1,0:T(8,128)S(1)}, f32[32,512]{1,0:T(8,128)S(1)}, u32[]{:S(2)}, u32[]{:S(2)}) collective-permute-start(f32[32,512]{1,0:T(8,128)S(1)} %get-tuple-element.53), channel_id=1, source_target_pairs={{0,7},{1,0},{2,1},{3,2},{4,3},{5,4},{6,5},{7,6},{8,15},{9,8},{10,9... | collective-permute-start | bytes 196616 | tf_op jit(solution)/shard_map/ppermute | solution.py:525
  93.7 3.9 %all-to-all-done.2.recv_ref = f32[16,136,128]{2,1,0:T(8,128)S(1)} async-done(((f32[16,136,128]{2,1,0:T(8,128)}), f32[16,136,128]{2,1,0:T(8,128)S(1)}, u32[]{:S(2)}, u32[]{:S(2)}) %all-to-all-start.2) | async-done | bytes 1114144 | tf_op jit(solution)/shard_map/all_to_all | solution.py:523
  97.5 0.6 shard_map.73
  98.2 4.5 %all-to-all-start.3 = ((f32[8,8,128]{2,1,0:T(8,128)}), f32[8,8,128]{2,1,0:T(8,128)S(1)}, u32[]{:S(2)}, u32[]{:S(2)}) async-start(f32[8,8,128]{2,1,0:T(8,128)} %shard_map.73), calls=%async_computation.3 | async-start | bytes 65536 | tf_op jit(solution)/shard_map/all_to_all | solution.py:529
  102.7 0.3 shard_map.72
  103.0 0.0 collective-permute-done.8.refs_3_
  103.1 0.0 collective-permute-done.9.refs_4_
  103.1 0.0 collective-permute-done.10.refs_5_
  103.1 0.0 collective-permute-done.11.refs_6_
  103.1 0.0 collective-permute-done.12.refs_7_
  103.1 0.9 shard_map.75
  104.0 5.3 %all-to-all-done.3.sums_ref = f32[8,8,128]{2,1,0:T(8,128)S(1)} async-done(((f32[8,8,128]{2,1,0:T(8,128)}), f32[8,8,128]{2,1,0:T(8,128)S(1)}, u32[]{:S(2)}, u32[]{:S(2)}) %all-to-all-start.3) | async-done | bytes 32800 | tf_op jit(solution)/shard_map/all_to_all | solution.py:529
  109.3 1.0 shard_map.74
  (14 shorter events, 0.2 us)
Async XLA Ops:
  0.6 8.7 %copy-start = (f32[256,512]{1,0:T(8,128)S(1)}, f32[256,512]{1,0:T(8,128)}, u32[]{:S(2)}) copy-start(f32[256,512]{1,0:T(8,128)} %u_ref.3) | copy-start | bytes 1572868
  0.6 24.8 %all-to-all-start = ((f32[8,32,512]{2,1,0:T(8,128)}), f32[8,32,512]{2,1,0:T(8,128)S(1)}, u32[]{:S(2)}, u32[]{:S(2)}) async-start(f32[8,32,512]{2,1,0:T(8,128)} %bitcast.27), calls=%async_computation | async-start | bytes 1048576 | tf_op jit(solution)/shard_map/all_to_all | solution.py:493
  9.4 16.0 %copy-start.1 = (bf16[3,256,256]{2,1,0:T(8,128)(2,1)S(1)}, bf16[3,256,256]{2,1,0:T(8,128)(2,1)}, u32[]{:S(2)}) copy-start(bf16[3,256,256]{2,1,0:T(8,128)(2,1)} %constant.144.clone.dft_ref) | copy-start | bytes 1179652
  9.4 16.0 %copy-start.2 = (f32[4,32,128]{2,1,0:T(8,128)S(1)}, f32[4,32,128]{2,1,0:T(8,128)}, u32[]{:S(2)}) copy-start(f32[4,32,128]{2,1,0:T(8,128)} %constant.145.clone.small_ref) | copy-start | bytes 196612
  10.3 21.1 %collective-permute-start.2 = (f32[4,32,256]{2,1,0:T(8,128)}, f32[4,32,256]{2,1,0:T(8,128)S(1)}, u32[]{:S(2)}, u32[]{:S(2)}) collective-permute-start(f32[4,32,256]{2,1,0:T(8,128)} %get-tuple-element.54), channel_id=1, source_target_pairs={{0,24},{8,0},{16,8},{24,16},{32,56},{40,32},{48,40},{56,48},{64,88... | collective-permute-start | bytes 393224 | tf_op jit(solution)/shard_map/ppermute | solution.py:465
  13.1 18.4 %collective-permute-start.1 = (f32[4,32,256]{2,1,0:T(8,128)S(1)}, f32[4,32,256]{2,1,0:T(8,128)S(1)}, u32[]{:S(2)}, u32[]{:S(2)}) collective-permute-start(f32[4,32,256]{2,1,0:T(8,128)S(1)} %get-tuple-element.55), channel_id=1, source_target_pairs={{0,16},{8,24},{16,0},{24,8},{32,48},{40,56},{48,32},{56,40},{64,80... | collective-permute-start | bytes 393224 | tf_op jit(solution)/shard_map/ppermute | solution.py:465
  13.9 17.6 %collective-permute-start = (f32[4,32,256]{2,1,0:T(8,128)S(1)}, f32[4,32,256]{2,1,0:T(8,128)S(1)}, u32[]{:S(2)}, u32[]{:S(2)}) collective-permute-start(f32[4,32,256]{2,1,0:T(8,128)S(1)} %get-tuple-element.56), channel_id=1, source_target_pairs={{0,8},{8,16},{16,24},{24,0},{32,40},{40,48},{48,56},{56,32},{64,72... | collective-permute-start | bytes 393224 | tf_op jit(solution)/shard_map/ppermute | solution.py:465
  31.4 41.3 %all-to-all-start.1 = ((f32[128,16,128]{2,1,0:T(8,128)}), f32[128,16,128]{2,1,0:T(8,128)S(1)}, u32[]{:S(2)}, u32[]{:S(2)}) async-start(f32[128,16,128]{2,1,0:T(8,128)} %bitcast.13), calls=%async_computation.1 | async-start | bytes 2097152 | tf_op jit(solution)/shard_map/all_to_all | solution.py:505
  41.4 9.3 %collective-permute-start.3 = (f32[4,32,256]{2,1,0:T(8,128)S(1)}, f32[4,32,256]{2,1,0:T(8,128)S(1)}, u32[]{:S(2)}, u32[]{:S(2)}) collective-permute-start(f32[4,32,256]{2,1,0:T(8,128)S(1)} %pad_maximum_fusion.1), channel_id=1, source_target_pairs={{0,32},{8,40},{16,48},{24,56},{32,64},{40,72},{48,80},{56,88},{64,... | collective-permute-start | bytes 393224 | tf_op jit(solution)/shard_map/ppermute | solution.py:475
  42.9 14.1 %collective-permute-start.4 = (f32[4,32,256]{2,1,0:T(8,128)S(1)}, f32[4,32,256]{2,1,0:T(8,128)S(1)}, u32[]{:S(2)}, u32[]{:S(2)}) collective-permute-start(f32[4,32,256]{2,1,0:T(8,128)S(1)} %pad_maximum_fusion.2), channel_id=1, source_target_pairs={{0,64},{8,72},{16,80},{24,88},{32,96},{40,104},{48,112},{56,120},{... | collective-permute-start | bytes 393224 | tf_op jit(solution)/shard_map/ppermute | solution.py:475
  45.8 11.3 %collective-permute-start.5 = (f32[4,32,256]{2,1,0:T(8,128)S(1)}, f32[4,32,256]{2,1,0:T(8,128)S(1)}, u32[]{:S(2)}, u32[]{:S(2)}) collective-permute-start(f32[4,32,256]{2,1,0:T(8,128)S(1)} %pad_maximum_fusion.3), channel_id=1, source_target_pairs={{0,96},{8,104},{16,112},{24,120},{32,0},{40,8},{48,16},{56,24},{64... | collective-permute-start | bytes 393224 | tf_op jit(solution)/shard_map/ppermute | solution.py:475
  59.1 1.0 copy-start.3
  72.7 1.2 %copy-start.4 = (f32[2,16,32,256]{3,2,1,0:T(8,128)S(1)}, f32[2,16,32,256]{3,2,1,0:T(8,128)}, u32[]{:S(2)}) copy-start(f32[2,16,32,256]{3,2,1,0:T(8,128)} %copy-done.3) | copy-start | bytes 3145732
  77.8 19.8 %all-to-all-start.2 = ((f32[16,136,128]{2,1,0:T(8,128)}), f32[16,136,128]{2,1,0:T(8,128)S(1)}, u32[]{:S(2)}, u32[]{:S(2)}) async-start(f32[16,136,128]{2,1,0:T(8,128)} %shard_map.71), calls=%async_computation.2 | async-start | bytes 2228224 | tf_op jit(solution)/shard_map/all_to_all | solution.py:523
  81.5 10.9 %collective-permute-start.6 = (f32[32,512]{1,0:T(8,128)S(1)}, f32[32,512]{1,0:T(8,128)S(1)}, u32[]{:S(2)}, u32[]{:S(2)}) collective-permute-start(f32[32,512]{1,0:T(8,128)S(1)} %get-tuple-element.47), channel_id=1, source_target_pairs={{0,1},{1,2},{2,3},{3,4},{4,5},{5,6},{6,7},{7,0},{8,9},{9,10},{10,1... | collective-permute-start | bytes 196616 | tf_op jit(solution)/shard_map/ppermute | solution.py:525
  81.6 10.8 %collective-permute-start.7 = (f32[32,512]{1,0:T(8,128)S(1)}, f32[32,512]{1,0:T(8,128)S(1)}, u32[]{:S(2)}, u32[]{:S(2)}) collective-permute-start(f32[32,512]{1,0:T(8,128)S(1)} %get-tuple-element.48), channel_id=1, source_target_pairs={{0,2},{1,3},{2,4},{3,5},{4,6},{5,7},{6,0},{7,1},{8,10},{9,11},{10,... | collective-permute-start | bytes 196616 | tf_op jit(solution)/shard_map/ppermute | solution.py:525
  82.0 21.0 %collective-permute-start.8 = (f32[32,512]{1,0:T(8,128)S(1)}, f32[32,512]{1,0:T(8,128)S(1)}, u32[]{:S(2)}, u32[]{:S(2)}) collective-permute-start(f32[32,512]{1,0:T(8,128)S(1)} %get-tuple-element.49), channel_id=1, source_target_pairs={{0,3},{1,4},{2,5},{3,6},{4,7},{5,0},{6,1},{7,2},{8,11},{9,12},{10,... | collective-permute-start | bytes 196616 | tf_op jit(solution)/shard_map/ppermute | solution.py:525
  84.9 18.1 %collective-permute-start.9 = (f32[32,512]{1,0:T(8,128)S(1)}, f32[32,512]{1,0:T(8,128)S(1)}, u32[]{:S(2)}, u32[]{:S(2)}) collective-permute-start(f32[32,512]{1,0:T(8,128)S(1)} %get-tuple-element.50), channel_id=1, source_target_pairs={{0,4},{1,5},{2,6},{3,7},{4,0},{5,1},{6,2},{7,3},{8,12},{9,13},{10,... | collective-permute-start | bytes 196616 | tf_op jit(solution)/shard_map/ppermute | solution.py:525
  88.1 14.9 %collective-permute-start.10 = (f32[32,512]{1,0:T(8,128)S(1)}, f32[32,512]{1,0:T(8,128)S(1)}, u32[]{:S(2)}, u32[]{:S(2)}) collective-permute-start(f32[32,512]{1,0:T(8,128)S(1)} %get-tuple-element.51), channel_id=1, source_target_pairs={{0,5},{1,6},{2,7},{3,0},{4,1},{5,2},{6,3},{7,4},{8,13},{9,14},{10,... | collective-permute-start | bytes 196616 | tf_op jit(solution)/shard_map/ppermute | solution.py:525
  92.4 10.7 %collective-permute-start.11 = (f32[32,512]{1,0:T(8,128)S(1)}, f32[32,512]{1,0:T(8,128)S(1)}, u32[]{:S(2)}, u32[]{:S(2)}) collective-permute-start(f32[32,512]{1,0:T(8,128)S(1)} %get-tuple-element.52), channel_id=1, source_target_pairs={{0,6},{1,7},{2,0},{3,1},{4,2},{5,3},{6,4},{7,5},{8,14},{9,15},{10,... | collective-permute-start | bytes 196616 | tf_op jit(solution)/shard_map/ppermute | solution.py:525
  92.4 10.7 %collective-permute-start.12 = (f32[32,512]{1,0:T(8,128)S(1)}, f32[32,512]{1,0:T(8,128)S(1)}, u32[]{:S(2)}, u32[]{:S(2)}) collective-permute-start(f32[32,512]{1,0:T(8,128)S(1)} %get-tuple-element.53), channel_id=1, source_target_pairs={{0,7},{1,0},{2,1},{3,2},{4,3},{5,4},{6,5},{7,6},{8,15},{9,8},{10,9... | collective-permute-start | bytes 196616 | tf_op jit(solution)/shard_map/ppermute | solution.py:525
  98.2 11.1 %all-to-all-start.3 = ((f32[8,8,128]{2,1,0:T(8,128)}), f32[8,8,128]{2,1,0:T(8,128)S(1)}, u32[]{:S(2)}, u32[]{:S(2)}) async-start(f32[8,8,128]{2,1,0:T(8,128)} %shard_map.73), calls=%async_computation.3 | async-start | bytes 65536 | tf_op jit(solution)/shard_map/all_to_all | solution.py:529
